TPU v7x, 32 devices: a whole 2x2x4 slice. The times are simulated.
32 devices in a mesh: groups: 2 (over x), node: 2 (over core), local: 8 (over z, y).
Axes of the slice: x: 2, y: 2, z: 4, core: 2. Of those that a mesh axis runs over, the one named last changes fastest.
Arguments:
- grad_out: bfloat16 [4096, 4096], P(('groups', 'node', 'local')), parts along dimension 0, may hold values from -6 to 6
- layer_in: bfloat16 [4096, 4096], P(('groups', 'node', 'local')), parts along dimension 0, may hold values from -6 to 6
- expert_ids: int32 [4096, 8], P(('groups', 'node', 'local')), parts along dimension 0, may hold values from 0 to 127, all different within a row; in each aligned block of 128 rows (0 to 127, 128 to 255, ...) at most 16 rows name the same one
- gate_probs: float32 [4096, 8], P(('groups', 'node', 'local')), parts along dimension 0, may hold values from 0.1 to 0.6
- sample_ids: int32 [32, 128], P(('groups', 'node', 'local')), parts along dimension 0, may hold values from 0 to 7, never falling along the last dimension, each value on 1 to 64 neighbouring positions
- w_gate: bfloat16 [3072, 4096], P(('node', 'local')), may hold values from -0.09375 to 0.09375
- w_up: bfloat16 [3072, 4096], P(('node', 'local')), may hold values from -0.09375 to 0.09375
- w_down: bfloat16 [3072, 4096], P(('node', 'local')), may hold values from -0.15625 to 0.15625
Outputs:
- grad_in: bfloat16 [4096, 4096], P(('groups', 'node', 'local')), parts along dimension 0
- grad_gate: bfloat16 [6144, 4096], P(('groups', 'node', 'local')), parts along dimension 0
- grad_up: bfloat16 [6144, 4096], P(('groups', 'node', 'local')), parts along dimension 0
- grad_down: bfloat16 [6144, 4096], P(('groups', 'node', 'local')), parts along dimension 0
There are 2 independent parts, one for each index of `groups`. A program takes and returns all parts, laid end to end along the dimension named above; an argument that names none is the same for every part. Nothing has to cross between parts.
Inputs may be any that keep to these rules, and one draw needn't show every extreme that they name: `expert_ids`: in each aligned block of 128 rows (the rows of one device) no expert is named by more than 16 rows, and one expert is named by exactly 16 rows; the numbers in a row differ. `sample_ids`: each packed row holds 8 samples numbered in order, never falling, each of 1 to 64 positions; one sample is exactly that long.
All inputs are finite; a program needn't handle non-finite values.
Results may differ from a plain program's by a relative error of at most 0.0066.
Values may be sent and summed in bfloat16 or wider, within the bound.
No kernel may reach another device: no remote copies, remote signals or barrier semaphores. Data moves between devices by JAX's collectives and lax.ppermute only.
A program may use at most 128 MiB of HBM per device.

v0:
```python
import jax
import jax.numpy as jnp
from jax import lax
from jax.sharding import PartitionSpec as P

FF = 1536
SAMPLES = 8
TOK_DEV = 128
CAP = 16


def silu_parts(pre):
    sigma = jax.nn.sigmoid(pre)
    return (pre * sigma, sigma * (1.0 + pre * (1.0 - sigma)))


def per_device(grad_out, layer_in, expert_ids, gate_probs, sample_ids, w_gate, w_up, w_down):
    tok_count = grad_out.shape[0]
    width = grad_out.shape[1]
    shard_width = w_gate.shape[0]
    node_count = lax.axis_size("node")
    local_count = lax.axis_size("local")
    devices = node_count * local_count
    shards = FF // shard_width
    wave = devices // shards
    contract = (((1,), (1,)), ((), ()))
    over_rows = (((0,), (0,)), ((), ()))
    packed = sample_ids[0]
    same_sample = packed[:, None] == packed[None, :]
    length = jnp.sum(same_sample.astype(jnp.int32), axis=1)
    loss_scale = TOK_DEV / (SAMPLES * length.astype(jnp.float32))
    expert_range = jnp.arange(wave, dtype=jnp.int32)
    hit = expert_ids[:, :, None] == expert_range[None, None, :]
    coef = jnp.sum(jnp.where(hit, gate_probs[:, :, None], 0.0), axis=1)
    member = jnp.any(hit, axis=1).astype(jnp.int32)
    rank = jnp.cumsum(member, axis=0) - 1
    slot_range = jnp.arange(CAP, dtype=jnp.int32)
    picked = (member[:, :, None] == 1) & (rank[:, :, None] == slot_range[None, None, :])
    factor = coef * loss_scale[:, None]
    slot_factor = jnp.sum(jnp.where(picked, factor[:, :, None], 0.0), axis=0).reshape(wave * CAP, 1)
    select = picked.astype(jnp.bfloat16).reshape(tok_count, wave * CAP)
    chosen_grad = lax.dot_general(select, grad_out, over_rows, preferred_element_type=jnp.float32)
    send_grad = (slot_factor * chosen_grad).astype(jnp.bfloat16)
    send_in = lax.dot_general(
        select, layer_in, over_rows, preferred_element_type=jnp.float32
    ).astype(jnp.bfloat16)
    flat_grad = jnp.broadcast_to(
        send_grad.reshape(wave, 1, CAP, width), (wave, shards, CAP, width)
    ).reshape(devices, CAP, width)
    flat_in = jnp.broadcast_to(
        send_in.reshape(wave, 1, CAP, width), (wave, shards, CAP, width)
    ).reshape(devices, CAP, width)
    recv_grad, recv_in = (
        lax.all_to_all(flat_grad, ("node", "local"), split_axis=0, concat_axis=0, tiled=True),
        lax.all_to_all(flat_in, ("node", "local"), split_axis=0, concat_axis=0, tiled=True),
    )
    rows_grad = recv_grad.reshape(devices * CAP, width)
    rows_in = recv_in.reshape(devices * CAP, width)
    gate_pre = lax.dot_general(rows_in, w_gate, contract, preferred_element_type=jnp.float32)
    up_pre = lax.dot_general(rows_in, w_up, contract, preferred_element_type=jnp.float32)
    d_act = lax.dot_general(rows_grad, w_down, contract, preferred_element_type=jnp.float32)
    act, slope = silu_parts(gate_pre)
    hidden = (act * up_pre).astype(jnp.bfloat16)
    d_up = (d_act * act).astype(jnp.bfloat16)
    d_gate = (d_act * up_pre * slope).astype(jnp.bfloat16)
    grad_down = lax.dot_general(
        hidden, rows_grad, over_rows, preferred_element_type=jnp.float32
    ).astype(jnp.bfloat16)
    grad_gate = lax.dot_general(
        d_gate, rows_in, over_rows, preferred_element_type=jnp.float32
    ).astype(jnp.bfloat16)
    grad_up = lax.dot_general(d_up, rows_in, over_rows, preferred_element_type=jnp.float32).astype(
        jnp.bfloat16
    )
    pieces = jnp.dot(d_gate, w_gate, preferred_element_type=jnp.float32)
    pieces = (pieces + jnp.dot(d_up, w_up, preferred_element_type=jnp.float32)).astype(jnp.bfloat16)
    returned = lax.all_to_all(
        pieces.reshape(devices, CAP, width),
        ("node", "local"),
        split_axis=0,
        concat_axis=0,
        tiled=True,
    )
    returned = returned.reshape(devices * CAP, width)
    select_all = jnp.broadcast_to(
        select.reshape(tok_count, wave, 1, CAP), (tok_count, wave, shards, CAP)
    )
    select_all = select_all.reshape(tok_count, devices * CAP)
    grad_in = jnp.dot(select_all, returned, preferred_element_type=jnp.float32).astype(jnp.bfloat16)
    return (grad_in, grad_gate, grad_up, grad_down)


def solution(mesh):
    return jax.shard_map(
        per_device,
        mesh=mesh,
        in_specs=(
            P(("groups", "node", "local"), None),
            P(("groups", "node", "local"), None),
            P(("groups", "node", "local"), None),
            P(("groups", "node", "local"), None),
            P(("groups", "node", "local"), None),
            P(("node", "local"), None),
            P(("node", "local"), None),
            P(("node", "local"), None),
        ),
        out_specs=(
            P(("groups", "node", "local"), None),
            P(("groups", "node", "local"), None),
            P(("groups", "node", "local"), None),
            P(("groups", "node", "local"), None),
        ),
        check_vma=False,
    )
```

profile of v0, /device:TPU:0, one launch (start us, length us, event | category | flops | bytes accessed | tf_op | source)
XLA Modules:
  0.0 176.4 jit_solution(3015049333411255453)
XLA Ops:
  0.6 0.0 copy-start
  0.6 0.8 fusion.7
  1.5 0.1 copy.18
  1.6 0.2 reduce_window_sum.11
  1.8 0.1 copy.19
  1.8 0.1 eq.81
  1.9 0.1 fusion.6
  2.0 1.5 convolution_convert_fusion.4
  3.5 1.6 broadcast_in_dim.59
  5.1 0.0 copy-start.7
  5.1 0.0 copy-start.8
  5.1 0.0 copy-start.9
  5.1 0.0 copy-start.2
  5.1 7.6 %all-to-all-start.1 = ((bf16[16,16,4096]{2,1,0:T(8,128)(2,1)}), bf16[16,16,4096]{2,1,0:T(8,128)(2,1)}, u32[]{:S(2)}, u32[]{:S(2)}) async-start(bf16[16,16,4096]{2,1,0:T(8,128)(2,1)} %bitcast.37), calls=%async_computation.1 | async-start | bytes 4194304 | tf_op jit(solution)/shard_map/all_to_all | solution.py:55
  12.7 0.0 copy-done.7
  12.7 0.0 copy-done.8
  12.7 0.0 copy-done.9
  12.7 0.2 convert_reduce_fusion
  12.9 0.1 select_reduce_fusion
  13.0 0.1 mul.57
  13.1 0.0 copy-done.2
  13.1 0.3 fusion.1
  13.4 46.9 %all-to-all-done.1 = bf16[16,16,4096]{2,1,0:T(8,128)(2,1)} async-done(((bf16[16,16,4096]{2,1,0:T(8,128)(2,1)}), bf16[16,16,4096]{2,1,0:T(8,128)(2,1)}, u32[]{:S(2)}, u32[]{:S(2)}) %all-to-all-start.1) | async-done | bytes 2097184 | tf_op jit(solution)/shard_map/all_to_all | solution.py:55
  60.3 1.6 broadcast_in_dim.57
  61.8 5.2 %all-to-all-start = ((bf16[16,16,4096]{2,1,0:T(8,128)(2,1)}), bf16[16,16,4096]{2,1,0:T(8,128)(2,1)}, u32[]{:S(2)}, u32[]{:S(2)}) async-start(bf16[16,16,4096]{2,1,0:T(8,128)(2,1)} %bitcast.38), calls=%async_computation | async-start | bytes 4194304 | tf_op jit(solution)/shard_map/all_to_all | solution.py:54
  67.0 0.0 copy-start.1
  67.0 0.0 copy-done
  67.0 2.5 %fusion.10 = f32[256,192]{0,1:T(8,128)S(1)} fusion(bf16[256,4096]{1,0:T(8,128)(2,1)} %bitcast.9, bf16[192,4096]{1,0:T(8,128)(2,1)S(1)} %copy-done), kind=kOutput, calls=%fused_computation.30 | convolution fusion | flops 402653184 | bytes 3866624 | tf_op jit(solution)/shard_map/dot_general | solution.py:59
  69.6 0.0 copy-done.1
  69.6 2.4 %fusion.9 = f32[256,192]{0,1:T(8,128)S(1)} fusion(bf16[256,4096]{1,0:T(8,128)(2,1)} %bitcast.9, bf16[192,4096]{1,0:T(8,128)(2,1)S(1)} %copy-done.1), kind=kOutput, calls=%fused_computation.29 | convolution fusion | flops 402653184 | bytes 3866624 | tf_op jit(solution)/shard_map/dot_general | solution.py:60
  72.0 42.6 %all-to-all-done = bf16[16,16,4096]{2,1,0:T(8,128)(2,1)} async-done(((bf16[16,16,4096]{2,1,0:T(8,128)(2,1)}), bf16[16,16,4096]{2,1,0:T(8,128)(2,1)}, u32[]{:S(2)}, u32[]{:S(2)}) %all-to-all-start) | async-done | bytes 2097184 | tf_op jit(solution)/shard_map/all_to_all | solution.py:54
  114.6 2.9 %multiply_convert_fusion.1 = (bf16[256,192]{0,1:T(8,128)(2,1)S(1)}, bf16[256,192]{0,1:T(8,128)(2,1)S(1)}) fusion(f32[256,192]{0,1:T(8,128)S(1)} %fusion.10, f32[256,192]{0,1:T(8,128)S(1)} %fusion.9, bf16[256,4096]{1,0:T(8,128)(2,1)} %bitcast.6, bf16[192,4096]{1,0:T(8,128)(2,1)} %param.15), kind=kOutput, calls=%fused_computation.10 | convolution fusion | flops 403292160 | bytes 4259840 | tf_op jit(solution)/shard_map/dot_general | solution.py:61
  117.5 0.0 copy-start.5
  117.5 0.0 copy-start.3
  117.6 0.7 fusion.11
  118.3 0.0 copy-done.5
  118.3 0.0 copy-done.3
  118.3 2.1 %fusion = bf16[256,4096]{1,0:T(8,128)(2,1)} fusion(f32[256,4096]{1,0:T(8,128)S(1)} %fusion.11, bf16[256,192]{0,1:T(8,128)(2,1)S(1)} %get-tuple-element.4, bf16[192,4096]{1,0:T(8,128)(2,1)S(1)} %copy-done.1), kind=kOutput, calls=%fused_computation.1 | convolution fusion | flops 404750336 | bytes 7962624 | tf_op jit(solution)/shard_map/dot_general | solution.py:76
  120.4 0.0 copy-start.4
  120.4 5.3 %all-to-all-start.2 = ((bf16[16,16,4096]{2,1,0:T(8,128)(2,1)}), bf16[16,16,4096]{2,1,0:T(8,128)(2,1)}, u32[]{:S(2)}, u32[]{:S(2)}) async-start(bf16[16,16,4096]{2,1,0:T(8,128)(2,1)} %bitcast.39), calls=%async_computation.2 | async-start | bytes 4194304 | tf_op jit(solution)/shard_map/all_to_all | solution.py:77
  125.7 0.0 copy-start.6
  125.8 0.0 copy-done.4
  125.8 3.4 %convolution_convert_fusion.1 = bf16[192,4096]{1,0:T(8,128)(2,1)} fusion(bf16[256,192]{0,1:T(8,128)(2,1)S(1)} %copy-done.4, bf16[256,4096]{1,0:T(8,128)(2,1)} %bitcast.9), kind=kOutput, calls=%fused_computation.3 | convolution fusion | flops 403439616 | bytes 3768320 | tf_op jit(solution)/shard_map/dot_general | solution.py:72
  129.1 0.0 copy-done.6
  129.1 3.3 %convolution_convert_fusion.2 = bf16[192,4096]{1,0:T(8,128)(2,1)} fusion(bf16[256,192]{0,1:T(8,128)(2,1)S(1)} %copy-done.6, bf16[256,4096]{1,0:T(8,128)(2,1)} %bitcast.9), kind=kOutput, calls=%fused_computation.4 | convolution fusion | flops 403439616 | bytes 3768320 | tf_op jit(solution)/shard_map/dot_general | solution.py:69
  132.5 3.3 %convolution_convert_fusion = bf16[192,4096]{1,0:T(8,128)(2,1)} fusion(bf16[256,4096]{1,0:T(8,128)(2,1)} %bitcast.6, f32[256,192]{0,1:T(8,128)S(1)} %fusion.9, f32[256,192]{0,1:T(8,128)S(1)} %fusion.10), kind=kOutput, calls=%fused_computation.2 | convolution fusion | flops 403734528 | bytes 4063232 | tf_op jit(solution)/shard_map/dot_general | solution.py:66
  135.8 37.6 %all-to-all-done.2 = bf16[16,16,4096]{2,1,0:T(8,128)(2,1)} async-done(((bf16[16,16,4096]{2,1,0:T(8,128)(2,1)}), bf16[16,16,4096]{2,1,0:T(8,128)(2,1)}, u32[]{:S(2)}, u32[]{:S(2)}) %all-to-all-start.2) | async-done | bytes 2097184 | tf_op jit(solution)/shard_map/all_to_all | solution.py:77
  173.4 3.0 %convolution_convert_fusion.3 = bf16[128,4096]{1,0:T(8,128)(2,1)} fusion(bf16[128,256]{0,1:T(8,128)(2,1)S(1)} %bitcast.42, bf16[256,4096]{1,0:T(8,128)(2,1)} %bitcast.11), kind=kOutput, calls=%fused_computation.5 | convolution fusion | flops 268959744 | bytes 3211264 | tf_op jit(solution)/shard_map/dot_general | solution.py:89
  (8 shorter events, 0.1 us)
Async XLA Ops:
  0.6 66.4 %copy-start = (bf16[192,4096]{1,0:T(8,128)(2,1)S(1)}, bf16[192,4096]{1,0:T(8,128)(2,1)}, u32[]{:S(2)}) copy-start(bf16[192,4096]{1,0:T(8,128)(2,1)} %param.13) | copy-start | bytes 4718596
  5.1 7.6 %copy-start.7 = (s32[128,8]{0,1:T(8,128)S(1)}, s32[128,8]{0,1:T(8,128)}, u32[]{:S(2)}) copy-start(s32[128,8]{0,1:T(8,128)} %param.10) | copy-start | bytes 12292
  5.1 7.6 %copy-start.8 = (f32[128,8]{0,1:T(8,128)S(1)}, f32[128,8]{0,1:T(8,128)}, u32[]{:S(2)}) copy-start(f32[128,8]{0,1:T(8,128)} %param.11) | copy-start | bytes 12292
  5.1 7.6 %copy-start.9 = (s32[1,128]{1,0:T(1,128)S(1)}, s32[1,128]{1,0:T(1,128)}, u32[]{:S(2)}) copy-start(s32[1,128]{1,0:T(1,128)} %param.12) | copy-start | bytes 1540
  5.1 8.0 %copy-start.2 = (bf16[128,4096]{1,0:T(8,128)(2,1)S(1)}, bf16[128,4096]{1,0:T(8,128)(2,1)}, u32[]{:S(2)}) copy-start(bf16[128,4096]{1,0:T(8,128)(2,1)} %param.8) | copy-start | bytes 3145732
  5.1 55.2 %all-to-all-start.1 = ((bf16[16,16,4096]{2,1,0:T(8,128)(2,1)}), bf16[16,16,4096]{2,1,0:T(8,128)(2,1)}, u32[]{:S(2)}, u32[]{:S(2)}) async-start(bf16[16,16,4096]{2,1,0:T(8,128)(2,1)} %bitcast.37), calls=%async_computation.1 | async-start | bytes 4194304 | tf_op jit(solution)/shard_map/all_to_all | solution.py:55
  61.8 52.8 %all-to-all-start = ((bf16[16,16,4096]{2,1,0:T(8,128)(2,1)}), bf16[16,16,4096]{2,1,0:T(8,128)(2,1)}, u32[]{:S(2)}, u32[]{:S(2)}) async-start(bf16[16,16,4096]{2,1,0:T(8,128)(2,1)} %bitcast.38), calls=%async_computation | async-start | bytes 4194304 | tf_op jit(solution)/shard_map/all_to_all | solution.py:54
  67.0 2.6 %copy-start.1 = (bf16[192,4096]{1,0:T(8,128)(2,1)S(1)}, bf16[192,4096]{1,0:T(8,128)(2,1)}, u32[]{:S(2)}) copy-start(bf16[192,4096]{1,0:T(8,128)(2,1)} %param.14) | copy-start | bytes 4718596
  117.5 0.8 copy-start.5
  117.5 0.8 copy-start.3
  120.4 5.3 %copy-start.4 = (bf16[256,192]{0,1:T(8,128)(2,1)S(1)}, bf16[256,192]{0,1:T(8,128)(2,1)}, u32[]{:S(2)}) copy-start(bf16[256,192]{0,1:T(8,128)(2,1)} %copy-done.3) | copy-start | bytes 294916
  120.4 52.9 %all-to-all-start.2 = ((bf16[16,16,4096]{2,1,0:T(8,128)(2,1)}), bf16[16,16,4096]{2,1,0:T(8,128)(2,1)}, u32[]{:S(2)}, u32[]{:S(2)}) async-start(bf16[16,16,4096]{2,1,0:T(8,128)(2,1)} %bitcast.39), calls=%async_computation.2 | async-start | bytes 4194304 | tf_op jit(solution)/shard_map/all_to_all | solution.py:77
  125.7 3.4 %copy-start.6 = (bf16[256,192]{0,1:T(8,128)(2,1)S(1)}, bf16[256,192]{0,1:T(8,128)(2,1)}, u32[]{:S(2)}) copy-start(bf16[256,192]{0,1:T(8,128)(2,1)} %copy-done.5) | copy-start | bytes 294916
where the time goes:
time: 177 us; the launch traced here: 176 us
  waiting for transfers between devices  127 us (72%)
  matrix products  25.6 us (14%)
  starting transfers between devices  18 us (10%)
  local copies, waits for them, and re-layouts  3.51 us (2%)
    all_to_all x1, waiting for transfers between devices, per_device(): lax.all_to_all(flat_in, ('node', 'local'), split_axis=0, concat_axis=0, t...  46.9 us
    all_to_all x1, waiting for transfers between devices, per_device(): lax.all_to_all(flat_grad, ('node', 'local'), split_axis=0, concat_axis=0,...  42.6 us
    all_to_all x1, waiting for transfers between devices, per_device(): lax.all_to_all(pieces.reshape(devices, CAP, width), ('node', 'local'), sp...  37.6 us
    all_to_all x1, starting transfers between devices, per_device(): lax.all_to_all(flat_in, ('node', 'local'), split_axis=0, concat_axis=0, t...  7.58 us
    all_to_all x1, starting transfers between devices, per_device(): lax.all_to_all(pieces.reshape(devices, CAP, width), ('node', 'local'), sp...  5.29 us
    all_to_all x1, starting transfers between devices, per_device(): lax.all_to_all(flat_grad, ('node', 'local'), split_axis=0, concat_axis=0,...  5.15 us
  transfers between devices with their start and end apart: 3, of which 3 were waited for; matrix products, arithmetic and copies ran while one was open for 9% of the time, Pallas kernels for 0%

commit v1 on v0

--- a/solution.py
+++ b/solution.py
@@ -14,7 +14,7 @@
     return (pre * sigma, sigma * (1.0 + pre * (1.0 - sigma)))
 
 
-def per_device(grad_out, layer_in, expert_ids, gate_probs, sample_ids, w_gate, w_up, w_down):
+def per_device_exchange(grad_out, layer_in, expert_ids, gate_probs, sample_ids, w_gate, w_up, w_down):
     tok_count = grad_out.shape[0]
     width = grad_out.shape[1]
     shard_width = w_gate.shape[0]
@@ -90,7 +90,120 @@
     return (grad_in, grad_gate, grad_up, grad_down)
 
 
+def ring_orders(count):
+    order = list(range(0, count, 2)) + list(range(count - 1, 0, -2))
+    ahead = [(order[i], order[(i + 1) % count]) for i in range(count)]
+    behind = [(order[i], order[(i - 1) % count]) for i in range(count)]
+    return ahead, behind
+
+
+def per_device_ring(grad_out, layer_in, expert_ids, gate_probs, sample_ids, w_gate, w_up, w_down):
+    width = grad_out.shape[1]
+    local_count = lax.axis_size("local")
+    wave = lax.axis_size("node")
+    me = lax.axis_index("node")
+    contract = (((1,), (1,)), ((), ()))
+    over_rows = (((0,), (0,)), ((), ()))
+    packed = sample_ids[0]
+    same_sample = packed[:, None] == packed[None, :]
+    length = jnp.sum(same_sample.astype(jnp.int32), axis=1)
+    loss_scale = TOK_DEV / (SAMPLES * length.astype(jnp.float32))
+    expert_range = (jnp.arange(wave, dtype=jnp.int32) + me) % wave
+    hit = expert_ids[:, :, None] == expert_range[None, None, :]
+    coef = jnp.sum(jnp.where(hit, gate_probs[:, :, None], 0.0), axis=1)
+    member = jnp.any(hit, axis=1).astype(jnp.int32)
+    rank = jnp.cumsum(member, axis=0) - 1
+    slot_range = jnp.arange(CAP, dtype=jnp.int32)
+    picked = (member[:, :, None] == 1) & (rank[:, :, None] == slot_range[None, None, :])
+    factor = coef * loss_scale[:, None]
+    slot_factor = jnp.sum(jnp.where(picked, factor[:, :, None], 0.0), axis=0).reshape(wave * CAP, 1)
+    select = picked.astype(jnp.bfloat16).reshape(-1, wave * CAP)
+    chosen_grad = lax.dot_general(select, grad_out, over_rows, preferred_element_type=jnp.float32)
+    send_grad = (slot_factor * chosen_grad).astype(jnp.bfloat16)
+    send_in = lax.dot_general(
+        select, layer_in, over_rows, preferred_element_type=jnp.float32
+    ).astype(jnp.bfloat16)
+    mine = jnp.concatenate([send_grad[:CAP], send_in[:CAP]])
+    other = jnp.concatenate([send_grad[CAP:], send_in[CAP:]])
+
+    swap = [(0, 1), (1, 0)]
+    ahead, behind = ring_orders(local_count)
+    go = lambda x: lax.ppermute(x, "local", ahead)
+    back = lambda x: lax.ppermute(x, "local", behind)
+    half = local_count // 2
+
+    near = mine
+    far = lax.ppermute(other, "node", swap)
+
+    rows = {0: (near, far)}
+    a_f, a_b, b_f, b_b = near, near, far, far
+    for s in range(1, half + 1):
+        a_f = go(a_f)
+        b_b = back(b_b)
+        if s < half:
+            b_f = go(b_f)
+            a_b = back(a_b)
+            rows[-s] = (a_f, b_f)
+            rows[s] = (a_b, b_b)
+        else:
+            rows[s] = (a_f, b_b)
+
+    hid = {}
+    pieces = {}
+    for s, (a, b) in rows.items():
+        grads = jnp.concatenate([a[:CAP], b[:CAP]])
+        ins = jnp.concatenate([a[CAP:], b[CAP:]])
+        gate_pre = lax.dot_general(ins, w_gate, contract, preferred_element_type=jnp.float32)
+        up_pre = lax.dot_general(ins, w_up, contract, preferred_element_type=jnp.float32)
+        d_act = lax.dot_general(grads, w_down, contract, preferred_element_type=jnp.float32)
+        act, slope = silu_parts(gate_pre)
+        hidden = (act * up_pre).astype(jnp.bfloat16)
+        d_up = (d_act * act).astype(jnp.bfloat16)
+        d_gate = (d_act * up_pre * slope).astype(jnp.bfloat16)
+        hid[s] = (hidden, d_up, d_gate, grads, ins)
+        p = jnp.dot(d_gate, w_gate, preferred_element_type=jnp.float32)
+        pieces[s] = p + jnp.dot(d_up, w_up, preferred_element_type=jnp.float32)
+
+    def piece(s, which):
+        return pieces[s][which * CAP : (which + 1) * CAP]
+
+    def summed(which, step, far_side, hops):
+        carry = None
+        for s in range(hops, 0, -1):
+            p = piece(s if s == half else far_side * s, which)
+            carry = (p if carry is None else p + carry.astype(jnp.float32)).astype(jnp.bfloat16)
+            carry = step(carry)
+        return carry.astype(jnp.float32)
+
+    total_b = piece(0, 1) + summed(1, back, -1, half) + summed(1, go, 1, half - 1)
+    total_a = piece(0, 0) + summed(0, back, -1, half - 1) + summed(0, go, 1, half)
+    returned = lax.ppermute(total_b.astype(jnp.bfloat16), "node", swap)
+    back_rows = jnp.concatenate([total_a.astype(jnp.bfloat16), returned])
+    grad_in = jnp.dot(select, back_rows, preferred_element_type=jnp.float32).astype(jnp.bfloat16)
+
+    hidden, d_up, d_gate, rows_grad, rows_in = (jnp.concatenate(x) for x in zip(*hid.values()))
+    grad_down = lax.dot_general(
+        hidden, rows_grad, over_rows, preferred_element_type=jnp.float32
+    ).astype(jnp.bfloat16)
+    grad_gate = lax.dot_general(
+        d_gate, rows_in, over_rows, preferred_element_type=jnp.float32
+    ).astype(jnp.bfloat16)
+    grad_up = lax.dot_general(d_up, rows_in, over_rows, preferred_element_type=jnp.float32).astype(
+        jnp.bfloat16
+    )
+    return (grad_in, grad_gate, grad_up, grad_down)
+
+
 def solution(mesh):
+    nodes, locals_ = mesh.shape["node"], mesh.shape["local"]
+    ring = nodes == 2 and locals_ % 2 == 0 and locals_ >= 4
+
+    def per_device(*args):
+        shards = FF // args[5].shape[0]
+        if ring and shards == locals_:
+            return per_device_ring(*args)
+        return per_device_exchange(*args)
+
     return jax.shard_map(
         per_device,
         mesh=mesh,

time: 177 us -> 99.9 us (0.56)
  waiting for transfers between devices: 127 us -> 33.4 us
  starting transfers between devices: 18 us -> 31.4 us
  matrix products: 25.6 us -> 29.2 us
  local copies, waits for them, and re-layouts: 3.51 us -> 1.05 us
  other arithmetic: 1.39 us -> 3.42 us
    all_to_all x3 -> x0, waiting for transfers between devices: 127 us -> none  [the longest x1 46.9 us: per_device(): lax.all_to_all(flat_in, ('node', 'local'), split_axis=0, concat_axis=0, t...]
    ppermute x0 -> x30, waiting for transfers between devices: none -> 33.4 us  [the longest x14 21.4 us: per_device_ring(): go = lambda x: lax.ppermute(x, 'local', ahead)]
    ppermute x0 -> x30, starting transfers between devices: none -> 31.4 us  [the longest x14 25.2 us: per_device_ring(): go = lambda x: lax.ppermute(x, 'local', ahead)]
    all_to_all x3 -> x0, starting transfers between devices: 18 us -> none  [the longest x1 7.58 us: per_device(): lax.all_to_all(flat_in, ('node', 'local'), split_axis=0, concat_axis=0, t...]
    dot_general x11 -> x46, matrix products: 25.6 us -> 29.2 us  [the longest x8 5.01 us: per_device_ring(): lax.dot_general(ins, w_gate, contract, preferred_element_type=jnp.float32)]
    broadcast_in_dim x3 -> x0, local copies, waits for them, and re-layouts: 3.11 us -> none  [the longest x1 1.55 us: per_device(): jnp.broadcast_to(send_in.reshape(wave, 1, CAP, width), (wave, shards, CAP...]
  transfers between devices with their start and end apart: 3 -> 30, of which waited for: 3 -> 16; matrix products, arithmetic and copies ran while one was open for 9% -> 27% of each run, Pallas kernels for 0% -> 0%
where the time goes in v1:
time: 99.9 us; the launch traced here: 99.6 us
  waiting for transfers between devices  33.4 us (33%)
  starting transfers between devices  31.4 us (31%)
  matrix products  29.2 us (29%)
  other arithmetic  3.42 us (3%)
  local copies, waits for them, and re-layouts  1.05 us (1%)
  between operations  1.04 us (1%)
    ppermute x14, starting transfers between devices, per_device_ring(): go = lambda x: lax.ppermute(x, 'local', ahead)  25.2 us
    ppermute x14, waiting for transfers between devices, per_device_ring(): go = lambda x: lax.ppermute(x, 'local', ahead)  21.4 us
    ppermute x14, waiting for transfers between devices, per_device_ring(): back = lambda x: lax.ppermute(x, 'local', behind)  12 us
    ppermute x14, starting transfers between devices, per_device_ring(): back = lambda x: lax.ppermute(x, 'local', behind)  5.66 us
    dot_general x8, matrix products, per_device_ring(): lax.dot_general(ins, w_gate, contract, preferred_element_type=jnp.float32)  5.01 us
    dot_general x8, matrix products, per_device_ring(): lax.dot_general(ins, w_up, contract, preferred_element_type=jnp.float32)  4.71 us
    dot_general x8, matrix products, per_device_ring(): lax.dot_general(grads, w_down, contract, preferred_element_type=jnp.float32)  4.63 us
    dot_general x8, matrix products, per_device_ring(): pieces[s] = p + jnp.dot(d_up, w_up, preferred_element_type=jnp.float32)  3.3 us
  transfers between devices with their start and end apart: 30, of which 16 were waited for; matrix products, arithmetic and copies ran while one was open for 27% of the time, Pallas kernels for 0%

profile of v1, /device:TPU:0, one launch (start us, length us, event | category | flops | bytes accessed | tf_op | source)
XLA Modules:
  0.0 99.6 jit_solution(3402647927992639683)
XLA Ops:
  0.8 0.9 compare_reduce_fusion
  2.1 0.8 fusion.75
  2.9 0.9 convert_reduce_fusion
  4.1 1.5 %convolution_convert_fusion.4 = bf16[32,4096]{1,0:T(8,128)(2,1)S(1)} fusion(pred[128,32]{0,1:T(32,128)(4,1)S(1)} %fusion.74, bf16[128,4096]{1,0:T(8,128)(2,1)} %param.9), kind=kOutput, calls=%fused_computation.15 | convolution fusion | flops 33685504 | bytes 1314816 | tf_op jit(solution)/shard_map/dot_general | solution.py:123
  6.5 2.7 %collective-permute-start.1 = (bf16[32,4096]{1,0:T(8,128)(2,1)S(1)}, bf16[32,4096]{1,0:T(8,128)(2,1)S(1)}, u32[]{:S(2)}, u32[]{:S(2)}) collective-permute-start(bf16[32,4096]{1,0:T(8,128)(2,1)S(1)} %pad_maximum_fusion), channel_id=1, source_target_pairs={{0,2},{2,4},{4,6},{6,7},{7,5},{5,3},{3,1},{1,0},{8,10},{10,12},{12... | collective-permute-start | bytes 786440 | tf_op jit(solution)/shard_map/ppermute | solution.py:131
  10.4 2.1 %collective-permute-start.2 = (bf16[32,4096]{1,0:T(8,128)(2,1)S(1)}, bf16[32,4096]{1,0:T(8,128)(2,1)S(1)}, u32[]{:S(2)}, u32[]{:S(2)}) collective-permute-start(bf16[32,4096]{1,0:T(8,128)(2,1)S(1)} %collective-permute-done), channel_id=1, source_target_pairs={{0,2},{2,4},{4,6},{6,7},{7,5},{5,3},{3,1},{1,0},{8,10},{10,12},{12... | collective-permute-start | bytes 786440 | tf_op jit(solution)/shard_map/ppermute | solution.py:131
  12.5 0.6 constant_dynamic-update-slice_fusion.7
  13.1 3.2 %collective-permute-done.1 = bf16[32,4096]{1,0:T(8,128)(2,1)S(1)} collective-permute-done((bf16[32,4096]{1,0:T(8,128)(2,1)S(1)}, bf16[32,4096]{1,0:T(8,128)(2,1)S(1)}, u32[]{:S(2)}, u32[]{:S(2)}) %collective-permute-start.1) | collective-permute-done | bytes 262176 | tf_op jit(solution)/shard_map/ppermute | solution.py:131
  16.3 2.0 %collective-permute-start.3 = (bf16[32,4096]{1,0:T(8,128)(2,1)S(1)}, bf16[32,4096]{1,0:T(8,128)(2,1)S(1)}, u32[]{:S(2)}, u32[]{:S(2)}) collective-permute-start(bf16[32,4096]{1,0:T(8,128)(2,1)S(1)} %collective-permute-done.1), channel_id=1, source_target_pairs={{0,2},{2,4},{4,6},{6,7},{7,5},{5,3},{3,1},{1,0},{8,10},{10,12},{12... | collective-permute-start | bytes 786440 | tf_op jit(solution)/shard_map/ppermute | solution.py:131
  19.2 2.7 %collective-permute-done.2 = bf16[32,4096]{1,0:T(8,128)(2,1)S(1)} collective-permute-done((bf16[32,4096]{1,0:T(8,128)(2,1)S(1)}, bf16[32,4096]{1,0:T(8,128)(2,1)S(1)}, u32[]{:S(2)}, u32[]{:S(2)}) %collective-permute-start.2) | collective-permute-done | bytes 262176 | tf_op jit(solution)/shard_map/ppermute | solution.py:131
  23.1 0.8 collective-permute-done.11
  24.5 0.6 fusion.56
  25.1 0.6 constant_dynamic-update-slice_fusion.6
  25.8 0.6 constant_dynamic-update-slice_fusion.5
  26.8 1.6 %collective-permute-start.4 = (bf16[32,4096]{1,0:T(8,128)(2,1)S(1)}, bf16[32,4096]{1,0:T(8,128)(2,1)S(1)}, u32[]{:S(2)}, u32[]{:S(2)}) collective-permute-start(bf16[32,4096]{1,0:T(8,128)(2,1)S(1)} %collective-permute-done.2), channel_id=1, source_target_pairs={{0,2},{2,4},{4,6},{6,7},{7,5},{5,3},{3,1},{1,0},{8,10},{10,12},{12... | collective-permute-start | bytes 786440 | tf_op jit(solution)/shard_map/ppermute | solution.py:131
  29.3 1.6 %collective-permute-start.5 = (bf16[32,4096]{1,0:T(8,128)(2,1)S(1)}, bf16[32,4096]{1,0:T(8,128)(2,1)S(1)}, u32[]{:S(2)}, u32[]{:S(2)}) collective-permute-start(bf16[32,4096]{1,0:T(8,128)(2,1)S(1)} %collective-permute-done.3), channel_id=1, source_target_pairs={{0,2},{2,4},{4,6},{6,7},{7,5},{5,3},{3,1},{1,0},{8,10},{10,12},{12... | collective-permute-start | bytes 786440 | tf_op jit(solution)/shard_map/ppermute | solution.py:131
  32.3 3.8 %collective-permute-done.4 = bf16[32,4096]{1,0:T(8,128)(2,1)S(1)} collective-permute-done((bf16[32,4096]{1,0:T(8,128)(2,1)S(1)}, bf16[32,4096]{1,0:T(8,128)(2,1)S(1)}, u32[]{:S(2)}, u32[]{:S(2)}) %collective-permute-start.4) | collective-permute-done | bytes 262176 | tf_op jit(solution)/shard_map/ppermute | solution.py:131
  38.3 0.6 fusion.54
  38.9 0.6 constant_dynamic-update-slice_fusion.4
  39.5 0.6 constant_dynamic-update-slice_fusion.3
  41.0 1.6 %collective-permute-start.6 = (bf16[32,4096]{1,0:T(8,128)(2,1)S(1)}, bf16[32,4096]{1,0:T(8,128)(2,1)S(1)}, u32[]{:S(2)}, u32[]{:S(2)}) collective-permute-start(bf16[32,4096]{1,0:T(8,128)(2,1)S(1)} %collective-permute-done.4), channel_id=1, source_target_pairs={{0,2},{2,4},{4,6},{6,7},{7,5},{5,3},{3,1},{1,0},{8,10},{10,12},{12... | collective-permute-start | bytes 786440 | tf_op jit(solution)/shard_map/ppermute | solution.py:131
  43.4 1.8 %collective-permute-start.16 = (bf16[32,4096]{1,0:T(8,128)(2,1)S(1)}, bf16[32,4096]{1,0:T(8,128)(2,1)S(1)}, u32[]{:S(2)}, u32[]{:S(2)}) collective-permute-start(bf16[32,4096]{1,0:T(8,128)(2,1)S(1)} %collective-permute-done.5), channel_id=1, source_target_pairs={{0,2},{2,4},{4,6},{6,7},{7,5},{5,3},{3,1},{1,0},{8,10},{10,12},{12... | collective-permute-start | bytes 786440 | tf_op jit(solution)/shard_map/ppermute | solution.py:131
  45.7 2.4 %collective-permute-done.6 = bf16[32,4096]{1,0:T(8,128)(2,1)S(1)} collective-permute-done((bf16[32,4096]{1,0:T(8,128)(2,1)S(1)}, bf16[32,4096]{1,0:T(8,128)(2,1)S(1)}, u32[]{:S(2)}, u32[]{:S(2)}) %collective-permute-start.6) | collective-permute-done | bytes 262176 | tf_op jit(solution)/shard_map/ppermute | solution.py:131
  49.9 0.6 fusion.52
  50.5 0.6 constant_dynamic-update-slice_fusion.2
  51.2 0.6 constant_dynamic-update-slice_fusion.1
  52.6 1.6 %collective-permute-start.26 = (bf16[16,4096]{1,0:T(8,128)(2,1)S(1)}, bf16[16,4096]{1,0:T(8,128)(2,1)S(1)}, u32[]{:S(2)}, u32[]{:S(2)}) collective-permute-start(bf16[16,4096]{1,0:T(8,128)(2,1)S(1)} %slice.328), channel_id=1, source_target_pairs={{0,2},{2,4},{4,6},{6,7},{7,5},{5,3},{3,1},{1,0},{8,10},{10,12},{12... | collective-permute-start | bytes 393224 | tf_op jit(solution)/shard_map/ppermute | solution.py:131
  55.6 1.5 %collective-permute-start.17 = (bf16[32,4096]{1,0:T(8,128)(2,1)S(1)}, bf16[32,4096]{1,0:T(8,128)(2,1)S(1)}, u32[]{:S(2)}, u32[]{:S(2)}) collective-permute-start(bf16[32,4096]{1,0:T(8,128)(2,1)S(1)} %collective-permute-done.15), channel_id=1, source_target_pairs={{0,1},{2,0},{4,2},{6,4},{7,6},{5,7},{3,5},{1,3},{8,9},{10,8},{12,1... | collective-permute-start | bytes 786440 | tf_op jit(solution)/shard_map/ppermute | solution.py:132
  57.2 6.3 %collective-permute-done.17 = bf16[32,4096]{1,0:T(8,128)(2,1)S(1)} collective-permute-done((bf16[32,4096]{1,0:T(8,128)(2,1)S(1)}, bf16[32,4096]{1,0:T(8,128)(2,1)S(1)}, u32[]{:S(2)}, u32[]{:S(2)}) %collective-permute-start.17) | collective-permute-done | bytes 262176 | tf_op jit(solution)/shard_map/ppermute | solution.py:132
  64.1 0.6 fusion.50
  64.7 0.6 constant_dynamic-update-slice_fusion
  66.2 1.6 %collective-permute-start.18 = (bf16[16,4096]{1,0:T(8,128)(2,1)S(1)}, bf16[16,4096]{1,0:T(8,128)(2,1)S(1)}, u32[]{:S(2)}, u32[]{:S(2)}) collective-permute-start(bf16[16,4096]{1,0:T(8,128)(2,1)S(1)} %get-tuple-element.112), channel_id=1, source_target_pairs={{0,2},{2,4},{4,6},{6,7},{7,5},{5,3},{3,1},{1,0},{8,10},{10,12},{12... | collective-permute-start | bytes 393224 | tf_op jit(solution)/shard_map/ppermute | solution.py:131
  68.3 1.8 %convolution_convert_fusion.2 = bf16[192,4096]{1,0:T(8,128)(2,1)} fusion(bf16[256,192]{1,0:T(8,128)(2,1)S(1)} %get-tuple-element.20, bf16[256,4096]{1,0:T(8,128)(2,1)S(1)} %get-tuple-element.47), kind=kOutput, calls=%fused_computation.2 | convolution fusion | flops 403439616 | bytes 3768320 | tf_op jit(solution)/shard_map/dot_general | solution.py:188
  70.0 2.5 %collective-permute-done.18 = bf16[16,4096]{1,0:T(8,128)(2,1)S(1)} collective-permute-done((bf16[16,4096]{1,0:T(8,128)(2,1)S(1)}, bf16[16,4096]{1,0:T(8,128)(2,1)S(1)}, u32[]{:S(2)}, u32[]{:S(2)}) %collective-permute-start.18) | collective-permute-done | bytes 131104 | tf_op jit(solution)/shard_map/ppermute | solution.py:131
  72.6 1.6 %collective-permute-start.19 = (bf16[16,4096]{1,0:T(8,128)(2,1)S(1)}, bf16[16,4096]{1,0:T(8,128)(2,1)S(1)}, u32[]{:S(2)}, u32[]{:S(2)}) collective-permute-start(bf16[16,4096]{1,0:T(8,128)(2,1)S(1)} %fusion.10), channel_id=1, source_target_pairs={{0,2},{2,4},{4,6},{6,7},{7,5},{5,3},{3,1},{1,0},{8,10},{10,12},{12... | collective-permute-start | bytes 393224 | tf_op jit(solution)/shard_map/ppermute | solution.py:131
  74.7 4.2 %collective-permute-done.19 = bf16[16,4096]{1,0:T(8,128)(2,1)S(1)} collective-permute-done((bf16[16,4096]{1,0:T(8,128)(2,1)S(1)}, bf16[16,4096]{1,0:T(8,128)(2,1)S(1)}, u32[]{:S(2)}, u32[]{:S(2)}) %collective-permute-start.19) | collective-permute-done | bytes 131104 | tf_op jit(solution)/shard_map/ppermute | solution.py:131
  79.0 1.6 %collective-permute-start.20 = (bf16[16,4096]{1,0:T(8,128)(2,1)S(1)}, bf16[16,4096]{1,0:T(8,128)(2,1)S(1)}, u32[]{:S(2)}, u32[]{:S(2)}) collective-permute-start(bf16[16,4096]{1,0:T(8,128)(2,1)S(1)} %get-tuple-element.44), channel_id=1, source_target_pairs={{0,2},{2,4},{4,6},{6,7},{7,5},{5,3},{3,1},{1,0},{8,10},{10,12},{12... | collective-permute-start | bytes 393224 | tf_op jit(solution)/shard_map/ppermute | solution.py:131
  80.7 1.6 %collective-permute-start.27 = (bf16[16,4096]{1,0:T(8,128)(2,1)S(1)}, bf16[16,4096]{1,0:T(8,128)(2,1)S(1)}, u32[]{:S(2)}, u32[]{:S(2)}) collective-permute-start(bf16[16,4096]{1,0:T(8,128)(2,1)S(1)} %get-tuple-element.45), channel_id=1, source_target_pairs={{0,2},{2,4},{4,6},{6,7},{7,5},{5,3},{3,1},{1,0},{8,10},{10,12},{12... | collective-permute-start | bytes 393224 | tf_op jit(solution)/shard_map/ppermute | solution.py:131
  83.2 0.8 collective-permute-done.20
  84.1 1.6 %collective-permute-done.27 = bf16[16,4096]{1,0:T(8,128)(2,1)S(1)} collective-permute-done((bf16[16,4096]{1,0:T(8,128)(2,1)S(1)}, bf16[16,4096]{1,0:T(8,128)(2,1)S(1)}, u32[]{:S(2)}, u32[]{:S(2)}) %collective-permute-start.27) | collective-permute-done | bytes 131104 | tf_op jit(solution)/shard_map/ppermute | solution.py:131
  85.7 1.7 %collective-permute-start.21 = (bf16[16,4096]{1,0:T(8,128)(2,1)S(1)}, bf16[16,4096]{1,0:T(8,128)(2,1)S(1)}, u32[]{:S(2)}, u32[]{:S(2)}) collective-permute-start(bf16[16,4096]{1,0:T(8,128)(2,1)S(1)} %get-tuple-element.42), channel_id=1, source_target_pairs={{0,2},{2,4},{4,6},{6,7},{7,5},{5,3},{3,1},{1,0},{8,10},{10,12},{12... | collective-permute-start | bytes 393224 | tf_op jit(solution)/shard_map/ppermute | solution.py:131
  87.6 1.4 %collective-permute-done.24 = bf16[16,4096]{1,0:T(8,128)(2,1)S(1)} collective-permute-done((bf16[16,4096]{1,0:T(8,128)(2,1)S(1)}, bf16[16,4096]{1,0:T(8,128)(2,1)S(1)}, u32[]{:S(2)}, u32[]{:S(2)}) %collective-permute-start.24) | collective-permute-done | bytes 131104 | tf_op jit(solution)/shard_map/ppermute | solution.py:132
  89.3 1.9 %collective-permute-start.28 = (bf16[16,4096]{1,0:T(8,128)(2,1)S(1)}, bf16[16,4096]{1,0:T(8,128)(2,1)S(1)}, u32[]{:S(2)}, u32[]{:S(2)}) collective-permute-start(bf16[16,4096]{1,0:T(8,128)(2,1)S(1)} %get-tuple-element.43), channel_id=1, source_target_pairs={{0,2},{2,4},{4,6},{6,7},{7,5},{5,3},{3,1},{1,0},{8,10},{10,12},{12... | collective-permute-start | bytes 393224 | tf_op jit(solution)/shard_map/ppermute | solution.py:131
  91.3 1.8 %convolution_convert_fusion.1 = bf16[192,4096]{1,0:T(8,128)(2,1)} fusion(bf16[256,192]{1,0:T(8,128)(2,1)S(1)} %get-tuple-element.115, bf16[256,4096]{1,0:T(8,128)(2,1)S(1)} %get-tuple-element.47), kind=kOutput, calls=%fused_computation.1 | convolution fusion | flops 403439616 | bytes 3768320 | tf_op jit(solution)/shard_map/dot_general | solution.py:191
  93.1 1.0 %collective-permute-done.9 = bf16[16,4096]{1,0:T(8,128)(2,1)S(1)} collective-permute-done((bf16[16,4096]{1,0:T(8,128)(2,1)S(1)}, bf16[16,4096]{1,0:T(8,128)(2,1)S(1)}, u32[]{:S(2)}, u32[]{:S(2)}) %collective-permute-start.9) | collective-permute-done | bytes 131104 | tf_op jit(solution)/shard_map/ppermute | solution.py:132
  94.3 1.9 %collective-permute-done.25 = bf16[16,4096]{1,0:T(8,128)(2,1)S(1)} collective-permute-done((bf16[16,4096]{1,0:T(8,128)(2,1)S(1)}, bf16[16,4096]{1,0:T(8,128)(2,1)S(1)}, u32[]{:S(2)}, u32[]{:S(2)}) %collective-permute-start.25) | collective-permute-done | bytes 131104 | tf_op jit(solution)/shard_map/ppermute | solution.py:132
  96.4 1.8 %convolution_convert_fusion = bf16[192,4096]{1,0:T(8,128)(2,1)} fusion(bf16[256,192]{1,0:T(8,128)(2,1)S(1)} %get-tuple-element.114, bf16[256,4096]{1,0:T(8,128)(2,1)S(1)} %get-tuple-element.46), kind=kOutput, calls=%fused_computation | convolution fusion | flops 403439616 | bytes 3768320 | tf_op jit(solution)/shard_map/dot_general | solution.py:185
  98.1 1.5 %convolution_convert_fusion.3 = bf16[128,4096]{1,0:T(8,128)(2,1)} fusion(pred[128,32]{0,1:T(32,128)(4,1)S(1)} %fusion.74, bf16[16,4096]{1,0:T(8,128)(2,1)S(1)} %collective-permute-done.29, bf16[16,4096]{1,0:T(8,128)(2,1)S(1)} %get-tuple-element.36), kind=kOutput, calls=%fused_computation.3 | convolution fusion | flops 34603008 | bytes 1314816 | tf_op jit(solution)/shard_map/dot_general | solution.py:182
  (110 shorter events, 20.9 us)
Async XLA Ops:
  0.6 11.8 %copy-start = (bf16[192,4096]{1,0:T(8,128)(2,1)S(1)}, bf16[192,4096]{1,0:T(8,128)(2,1)}, u32[]{:S(2)}) copy-start(bf16[192,4096]{1,0:T(8,128)(2,1)} %param.13) | copy-start | bytes 4718596
  0.6 4.9 %copy-start.3 = (bf16[128,4096]{1,0:T(8,128)(2,1)S(1)}, bf16[128,4096]{1,0:T(8,128)(2,1)}, u32[]{:S(2)}) copy-start(bf16[128,4096]{1,0:T(8,128)(2,1)} %param.8) | copy-start | bytes 3145732
  5.9 3.4 %copy-start.2 = (bf16[192,4096]{1,0:T(8,128)(2,1)S(1)}, bf16[192,4096]{1,0:T(8,128)(2,1)}, u32[]{:S(2)}) copy-start(bf16[192,4096]{1,0:T(8,128)(2,1)} %param.15) | copy-start | bytes 4718596
  6.0 3.2 %collective-permute-start = (bf16[32,4096]{1,0:T(8,128)(2,1)S(1)}, bf16[32,4096]{1,0:T(8,128)(2,1)S(1)}, u32[]{:S(2)}, u32[]{:S(2)}) collective-permute-start(bf16[32,4096]{1,0:T(8,128)(2,1)S(1)} %pad_maximum_fusion.3), channel_id=1, source_target_pairs={{0,8},{8,0},{1,9},{9,1},{2,10},{10,2},{3,11},{11,3},{4,12},{12,4},... | collective-permute-start | bytes 786440 | tf_op jit(solution)/shard_map/ppermute | solution.py:136
  6.5 3.3 %copy-start.1 = (bf16[192,4096]{1,0:T(8,128)(2,1)S(1)}, bf16[192,4096]{1,0:T(8,128)(2,1)}, u32[]{:S(2)}) copy-start(bf16[192,4096]{1,0:T(8,128)(2,1)} %param.14) | copy-start | bytes 4718596
  6.5 9.8 %collective-permute-start.1 = (bf16[32,4096]{1,0:T(8,128)(2,1)S(1)}, bf16[32,4096]{1,0:T(8,128)(2,1)S(1)}, u32[]{:S(2)}, u32[]{:S(2)}) collective-permute-start(bf16[32,4096]{1,0:T(8,128)(2,1)S(1)} %pad_maximum_fusion), channel_id=1, source_target_pairs={{0,2},{2,4},{4,6},{6,7},{7,5},{5,3},{3,1},{1,0},{8,10},{10,12},{12... | collective-permute-start | bytes 786440 | tf_op jit(solution)/shard_map/ppermute | solution.py:131
  9.2 9.5 %collective-permute-start.10 = (bf16[32,4096]{1,0:T(8,128)(2,1)S(1)}, bf16[32,4096]{1,0:T(8,128)(2,1)S(1)}, u32[]{:S(2)}, u32[]{:S(2)}) collective-permute-start(bf16[32,4096]{1,0:T(8,128)(2,1)S(1)} %pad_maximum_fusion), channel_id=1, source_target_pairs={{0,1},{2,0},{4,2},{6,4},{7,6},{5,7},{3,5},{1,3},{8,9},{10,8},{12,1... | collective-permute-start | bytes 786440 | tf_op jit(solution)/shard_map/ppermute | solution.py:132
  10.4 11.5 %collective-permute-start.2 = (bf16[32,4096]{1,0:T(8,128)(2,1)S(1)}, bf16[32,4096]{1,0:T(8,128)(2,1)S(1)}, u32[]{:S(2)}, u32[]{:S(2)}) collective-permute-start(bf16[32,4096]{1,0:T(8,128)(2,1)S(1)} %collective-permute-done), channel_id=1, source_target_pairs={{0,2},{2,4},{4,6},{6,7},{7,5},{5,3},{3,1},{1,0},{8,10},{10,12},{12... | collective-permute-start | bytes 786440 | tf_op jit(solution)/shard_map/ppermute | solution.py:131
  12.5 11.5 %collective-permute-start.11 = (bf16[32,4096]{1,0:T(8,128)(2,1)S(1)}, bf16[32,4096]{1,0:T(8,128)(2,1)S(1)}, u32[]{:S(2)}, u32[]{:S(2)}) collective-permute-start(bf16[32,4096]{1,0:T(8,128)(2,1)S(1)} %collective-permute-done), channel_id=1, source_target_pairs={{0,1},{2,0},{4,2},{6,4},{7,6},{5,7},{3,5},{1,3},{8,9},{10,8},{12,1... | collective-permute-start | bytes 786440 | tf_op jit(solution)/shard_map/ppermute | solution.py:132
  16.3 13.0 %collective-permute-start.3 = (bf16[32,4096]{1,0:T(8,128)(2,1)S(1)}, bf16[32,4096]{1,0:T(8,128)(2,1)S(1)}, u32[]{:S(2)}, u32[]{:S(2)}) collective-permute-start(bf16[32,4096]{1,0:T(8,128)(2,1)S(1)} %collective-permute-done.1), channel_id=1, source_target_pairs={{0,2},{2,4},{4,6},{6,7},{7,5},{5,3},{3,1},{1,0},{8,10},{10,12},{12... | collective-permute-start | bytes 786440 | tf_op jit(solution)/shard_map/ppermute | solution.py:131
  18.7 12.6 %collective-permute-start.12 = (bf16[32,4096]{1,0:T(8,128)(2,1)S(1)}, bf16[32,4096]{1,0:T(8,128)(2,1)S(1)}, u32[]{:S(2)}, u32[]{:S(2)}) collective-permute-start(bf16[32,4096]{1,0:T(8,128)(2,1)S(1)} %collective-permute-done.10), channel_id=1, source_target_pairs={{0,1},{2,0},{4,2},{6,4},{7,6},{5,7},{3,5},{1,3},{8,9},{10,8},{12,1... | collective-permute-start | bytes 786440 | tf_op jit(solution)/shard_map/ppermute | solution.py:132
  26.8 9.3 %collective-permute-start.4 = (bf16[32,4096]{1,0:T(8,128)(2,1)S(1)}, bf16[32,4096]{1,0:T(8,128)(2,1)S(1)}, u32[]{:S(2)}, u32[]{:S(2)}) collective-permute-start(bf16[32,4096]{1,0:T(8,128)(2,1)S(1)} %collective-permute-done.2), channel_id=1, source_target_pairs={{0,2},{2,4},{4,6},{6,7},{7,5},{5,3},{3,1},{1,0},{8,10},{10,12},{12... | collective-permute-start | bytes 786440 | tf_op jit(solution)/shard_map/ppermute | solution.py:131
  28.4 9.2 %collective-permute-start.13 = (bf16[32,4096]{1,0:T(8,128)(2,1)S(1)}, bf16[32,4096]{1,0:T(8,128)(2,1)S(1)}, u32[]{:S(2)}, u32[]{:S(2)}) collective-permute-start(bf16[32,4096]{1,0:T(8,128)(2,1)S(1)} %collective-permute-done.11), channel_id=1, source_target_pairs={{0,1},{2,0},{4,2},{6,4},{7,6},{5,7},{3,5},{1,3},{8,9},{10,8},{12,1... | collective-permute-start | bytes 786440 | tf_op jit(solution)/shard_map/ppermute | solution.py:132
  29.3 14.1 %collective-permute-start.5 = (bf16[32,4096]{1,0:T(8,128)(2,1)S(1)}, bf16[32,4096]{1,0:T(8,128)(2,1)S(1)}, u32[]{:S(2)}, u32[]{:S(2)}) collective-permute-start(bf16[32,4096]{1,0:T(8,128)(2,1)S(1)} %collective-permute-done.3), channel_id=1, source_target_pairs={{0,2},{2,4},{4,6},{6,7},{7,5},{5,3},{3,1},{1,0},{8,10},{10,12},{12... | collective-permute-start | bytes 786440 | tf_op jit(solution)/shard_map/ppermute | solution.py:131
  31.3 17.4 %collective-permute-start.14 = (bf16[32,4096]{1,0:T(8,128)(2,1)S(1)}, bf16[32,4096]{1,0:T(8,128)(2,1)S(1)}, u32[]{:S(2)}, u32[]{:S(2)}) collective-permute-start(bf16[32,4096]{1,0:T(8,128)(2,1)S(1)} %collective-permute-done.12), channel_id=1, source_target_pairs={{0,1},{2,0},{4,2},{6,4},{7,6},{5,7},{3,5},{1,3},{8,9},{10,8},{12,1... | collective-permute-start | bytes 786440 | tf_op jit(solution)/shard_map/ppermute | solution.py:132
  41.0 7.1 %collective-permute-start.6 = (bf16[32,4096]{1,0:T(8,128)(2,1)S(1)}, bf16[32,4096]{1,0:T(8,128)(2,1)S(1)}, u32[]{:S(2)}, u32[]{:S(2)}) collective-permute-start(bf16[32,4096]{1,0:T(8,128)(2,1)S(1)} %collective-permute-done.4), channel_id=1, source_target_pairs={{0,2},{2,4},{4,6},{6,7},{7,5},{5,3},{3,1},{1,0},{8,10},{10,12},{12... | collective-permute-start | bytes 786440 | tf_op jit(solution)/shard_map/ppermute | solution.py:131
  42.6 6.7 %collective-permute-start.15 = (bf16[32,4096]{1,0:T(8,128)(2,1)S(1)}, bf16[32,4096]{1,0:T(8,128)(2,1)S(1)}, u32[]{:S(2)}, u32[]{:S(2)}) collective-permute-start(bf16[32,4096]{1,0:T(8,128)(2,1)S(1)} %collective-permute-done.13), channel_id=1, source_target_pairs={{0,1},{2,0},{4,2},{6,4},{7,6},{5,7},{3,5},{1,3},{8,9},{10,8},{12,1... | collective-permute-start | bytes 786440 | tf_op jit(solution)/shard_map/ppermute | solution.py:132
  43.4 13.7 %collective-permute-start.16 = (bf16[32,4096]{1,0:T(8,128)(2,1)S(1)}, bf16[32,4096]{1,0:T(8,128)(2,1)S(1)}, u32[]{:S(2)}, u32[]{:S(2)}) collective-permute-start(bf16[32,4096]{1,0:T(8,128)(2,1)S(1)} %collective-permute-done.5), channel_id=1, source_target_pairs={{0,2},{2,4},{4,6},{6,7},{7,5},{5,3},{3,1},{1,0},{8,10},{10,12},{12... | collective-permute-start | bytes 786440 | tf_op jit(solution)/shard_map/ppermute | solution.py:131
  52.6 22.1 %collective-permute-start.26 = (bf16[16,4096]{1,0:T(8,128)(2,1)S(1)}, bf16[16,4096]{1,0:T(8,128)(2,1)S(1)}, u32[]{:S(2)}, u32[]{:S(2)}) collective-permute-start(bf16[16,4096]{1,0:T(8,128)(2,1)S(1)} %slice.328), channel_id=1, source_target_pairs={{0,2},{2,4},{4,6},{6,7},{7,5},{5,3},{3,1},{1,0},{8,10},{10,12},{12... | collective-permute-start | bytes 393224 | tf_op jit(solution)/shard_map/ppermute | solution.py:131
  55.1 27.2 %collective-permute-start.7 = (bf16[16,4096]{1,0:T(8,128)(2,1)S(1)}, bf16[16,4096]{1,0:T(8,128)(2,1)S(1)}, u32[]{:S(2)}, u32[]{:S(2)}) collective-permute-start(bf16[16,4096]{1,0:T(8,128)(2,1)S(1)} %slice.329), channel_id=1, source_target_pairs={{0,1},{2,0},{4,2},{6,4},{7,6},{5,7},{3,5},{1,3},{8,9},{10,8},{12,1... | collective-permute-start | bytes 393224 | tf_op jit(solution)/shard_map/ppermute | solution.py:132
  55.6 7.9 %collective-permute-start.17 = (bf16[32,4096]{1,0:T(8,128)(2,1)S(1)}, bf16[32,4096]{1,0:T(8,128)(2,1)S(1)}, u32[]{:S(2)}, u32[]{:S(2)}) collective-permute-start(bf16[32,4096]{1,0:T(8,128)(2,1)S(1)} %collective-permute-done.15), channel_id=1, source_target_pairs={{0,1},{2,0},{4,2},{6,4},{7,6},{5,7},{3,5},{1,3},{8,9},{10,8},{12,1... | collective-permute-start | bytes 786440 | tf_op jit(solution)/shard_map/ppermute | solution.py:132
  66.2 6.4 %collective-permute-start.18 = (bf16[16,4096]{1,0:T(8,128)(2,1)S(1)}, bf16[16,4096]{1,0:T(8,128)(2,1)S(1)}, u32[]{:S(2)}, u32[]{:S(2)}) collective-permute-start(bf16[16,4096]{1,0:T(8,128)(2,1)S(1)} %get-tuple-element.112), channel_id=1, source_target_pairs={{0,2},{2,4},{4,6},{6,7},{7,5},{5,3},{3,1},{1,0},{8,10},{10,12},{12... | collective-permute-start | bytes 393224 | tf_op jit(solution)/shard_map/ppermute | solution.py:131
  67.8 6.4 %collective-permute-start.22 = (bf16[16,4096]{1,0:T(8,128)(2,1)S(1)}, bf16[16,4096]{1,0:T(8,128)(2,1)S(1)}, u32[]{:S(2)}, u32[]{:S(2)}) collective-permute-start(bf16[16,4096]{1,0:T(8,128)(2,1)S(1)} %get-tuple-element.113), channel_id=1, source_target_pairs={{0,1},{2,0},{4,2},{6,4},{7,6},{5,7},{3,5},{1,3},{8,9},{10,8},{12,1... | collective-permute-start | bytes 393224 | tf_op jit(solution)/shard_map/ppermute | solution.py:132
  72.6 6.4 %collective-permute-start.19 = (bf16[16,4096]{1,0:T(8,128)(2,1)S(1)}, bf16[16,4096]{1,0:T(8,128)(2,1)S(1)}, u32[]{:S(2)}, u32[]{:S(2)}) collective-permute-start(bf16[16,4096]{1,0:T(8,128)(2,1)S(1)} %fusion.10), channel_id=1, source_target_pairs={{0,2},{2,4},{4,6},{6,7},{7,5},{5,3},{3,1},{1,0},{8,10},{10,12},{12... | collective-permute-start | bytes 393224 | tf_op jit(solution)/shard_map/ppermute | solution.py:131
  74.2 8.1 %collective-permute-start.23 = (bf16[16,4096]{1,0:T(8,128)(2,1)S(1)}, bf16[16,4096]{1,0:T(8,128)(2,1)S(1)}, u32[]{:S(2)}, u32[]{:S(2)}) collective-permute-start(bf16[16,4096]{1,0:T(8,128)(2,1)S(1)} %fusion.5), channel_id=1, source_target_pairs={{0,1},{2,0},{4,2},{6,4},{7,6},{5,7},{3,5},{1,3},{8,9},{10,8},{12,1... | collective-permute-start | bytes 393224 | tf_op jit(solution)/shard_map/ppermute | solution.py:132
  79.0 5.0 %collective-permute-start.20 = (bf16[16,4096]{1,0:T(8,128)(2,1)S(1)}, bf16[16,4096]{1,0:T(8,128)(2,1)S(1)}, u32[]{:S(2)}, u32[]{:S(2)}) collective-permute-start(bf16[16,4096]{1,0:T(8,128)(2,1)S(1)} %get-tuple-element.44), channel_id=1, source_target_pairs={{0,2},{2,4},{4,6},{6,7},{7,5},{5,3},{3,1},{1,0},{8,10},{10,12},{12... | collective-permute-start | bytes 393224 | tf_op jit(solution)/shard_map/ppermute | solution.py:131
  80.7 5.0 %collective-permute-start.27 = (bf16[16,4096]{1,0:T(8,128)(2,1)S(1)}, bf16[16,4096]{1,0:T(8,128)(2,1)S(1)}, u32[]{:S(2)}, u32[]{:S(2)}) collective-permute-start(bf16[16,4096]{1,0:T(8,128)(2,1)S(1)} %get-tuple-element.45), channel_id=1, source_target_pairs={{0,2},{2,4},{4,6},{6,7},{7,5},{5,3},{3,1},{1,0},{8,10},{10,12},{12... | collective-permute-start | bytes 393224 | tf_op jit(solution)/shard_map/ppermute | solution.py:131
  82.4 5.2 %collective-permute-start.8 = (bf16[16,4096]{1,0:T(8,128)(2,1)S(1)}, bf16[16,4096]{1,0:T(8,128)(2,1)S(1)}, u32[]{:S(2)}, u32[]{:S(2)}) collective-permute-start(bf16[16,4096]{1,0:T(8,128)(2,1)S(1)} %get-tuple-element.40), channel_id=1, source_target_pairs={{0,1},{2,0},{4,2},{6,4},{7,6},{5,7},{3,5},{1,3},{8,9},{10,8},{12,1... | collective-permute-start | bytes 393224 | tf_op jit(solution)/shard_map/ppermute | solution.py:132
  82.8 6.2 %collective-permute-start.24 = (bf16[16,4096]{1,0:T(8,128)(2,1)S(1)}, bf16[16,4096]{1,0:T(8,128)(2,1)S(1)}, u32[]{:S(2)}, u32[]{:S(2)}) collective-permute-start(bf16[16,4096]{1,0:T(8,128)(2,1)S(1)} %get-tuple-element.41), channel_id=1, source_target_pairs={{0,1},{2,0},{4,2},{6,4},{7,6},{5,7},{3,5},{1,3},{8,9},{10,8},{12,1... | collective-permute-start | bytes 393224 | tf_op jit(solution)/shard_map/ppermute | solution.py:132
  85.7 7.4 %collective-permute-start.21 = (bf16[16,4096]{1,0:T(8,128)(2,1)S(1)}, bf16[16,4096]{1,0:T(8,128)(2,1)S(1)}, u32[]{:S(2)}, u32[]{:S(2)}) collective-permute-start(bf16[16,4096]{1,0:T(8,128)(2,1)S(1)} %get-tuple-element.42), channel_id=1, source_target_pairs={{0,2},{2,4},{4,6},{6,7},{7,5},{5,3},{3,1},{1,0},{8,10},{10,12},{12... | collective-permute-start | bytes 393224 | tf_op jit(solution)/shard_map/ppermute | solution.py:131
  89.1 5.0 %collective-permute-start.9 = (bf16[16,4096]{1,0:T(8,128)(2,1)S(1)}, bf16[16,4096]{1,0:T(8,128)(2,1)S(1)}, u32[]{:S(2)}, u32[]{:S(2)}) collective-permute-start(bf16[16,4096]{1,0:T(8,128)(2,1)S(1)} %get-tuple-element.38), channel_id=1, source_target_pairs={{0,1},{2,0},{4,2},{6,4},{7,6},{5,7},{3,5},{1,3},{8,9},{10,8},{12,1... | collective-permute-start | bytes 393224 | tf_op jit(solution)/shard_map/ppermute | solution.py:132
  89.3 5.0 %collective-permute-start.28 = (bf16[16,4096]{1,0:T(8,128)(2,1)S(1)}, bf16[16,4096]{1,0:T(8,128)(2,1)S(1)}, u32[]{:S(2)}, u32[]{:S(2)}) collective-permute-start(bf16[16,4096]{1,0:T(8,128)(2,1)S(1)} %get-tuple-element.43), channel_id=1, source_target_pairs={{0,2},{2,4},{4,6},{6,7},{7,5},{5,3},{3,1},{1,0},{8,10},{10,12},{12... | collective-permute-start | bytes 393224 | tf_op jit(solution)/shard_map/ppermute | solution.py:131
  91.2 5.0 %collective-permute-start.25 = (bf16[16,4096]{1,0:T(8,128)(2,1)S(1)}, bf16[16,4096]{1,0:T(8,128)(2,1)S(1)}, u32[]{:S(2)}, u32[]{:S(2)}) collective-permute-start(bf16[16,4096]{1,0:T(8,128)(2,1)S(1)} %get-tuple-element.39), channel_id=1, source_target_pairs={{0,1},{2,0},{4,2},{6,4},{7,6},{5,7},{3,5},{1,3},{8,9},{10,8},{12,1... | collective-permute-start | bytes 393224 | tf_op jit(solution)/shard_map/ppermute | solution.py:132
  96.3 1.8 %collective-permute-start.29 = (bf16[16,4096]{1,0:T(8,128)(2,1)S(1)}, bf16[16,4096]{1,0:T(8,128)(2,1)S(1)}, u32[]{:S(2)}, u32[]{:S(2)}) collective-permute-start(bf16[16,4096]{1,0:T(8,128)(2,1)S(1)} %get-tuple-element.37), channel_id=1, source_target_pairs={{0,8},{8,0},{1,9},{9,1},{2,10},{10,2},{3,11},{11,3},{4,12},{12,4},... | collective-permute-start | bytes 393224 | tf_op jit(solution)/shard_map/ppermute | solution.py:180

commit v2 on v0

--- a/solution.py
+++ b/solution.py
@@ -1,12 +1,23 @@
+import functools
+
 import jax
 import jax.numpy as jnp
 from jax import lax
+from jax.experimental import pallas as pl
+from jax.experimental.pallas import tpu as pltpu
 from jax.sharding import PartitionSpec as P
 
 FF = 1536
 SAMPLES = 8
 TOK_DEV = 128
 CAP = 16
+BF = jnp.bfloat16
+F32 = jnp.float32
+NT = (((1,), (1,)), ((), ()))
+TN = (((0,), (0,)), ((), ()))
+NN = (((1,), (0,)), ((), ()))
+IN_VMEM = pl.BlockSpec(memory_space=pltpu.VMEM)
+LIGHT = pl.CostEstimate(flops=0, bytes_accessed=0, transcendentals=0)
 
 
 def silu_parts(pre):
@@ -14,7 +25,7 @@
     return (pre * sigma, sigma * (1.0 + pre * (1.0 - sigma)))
 
 
-def per_device(grad_out, layer_in, expert_ids, gate_probs, sample_ids, w_gate, w_up, w_down):
+def per_device_exchange(grad_out, layer_in, expert_ids, gate_probs, sample_ids, w_gate, w_up, w_down):
     tok_count = grad_out.shape[0]
     width = grad_out.shape[1]
     shard_width = w_gate.shape[0]
@@ -90,7 +101,294 @@
     return (grad_in, grad_gate, grad_up, grad_down)
 
 
+def ring_orders(count):
+    order = list(range(0, count, 2)) + list(range(count - 1, 0, -2))
+    ahead = [(order[i], order[(i + 1) % count]) for i in range(count)]
+    behind = [(order[i], order[(i - 1) % count]) for i in range(count)]
+    return ahead, behind
+
+
+def dot(x, y, dims=NN):
+    return lax.dot_general(x, y, dims, preferred_element_type=F32)
+
+
+def held(x):
+    return pltpu.with_memory_space_constraint(x, pltpu.VMEM)
+
+
+def streamed(x):
+    return pltpu.with_memory_space_constraint(x, pltpu.HBM)
+
+
+def after(x, *earlier):
+    return lax.optimization_barrier((x, *earlier))[0]
+
+
+def together(*arrays):
+    return lax.optimization_barrier(arrays)
+
+
+def in_vmem(*shape, dtype=BF):
+    return pltpu.MemorySpace.VMEM(shape, dtype)
+
+
+def tiles_of(width, tile):
+    return [pl.ds(k, min(tile, width - k)) for k in range(0, width, tile)]
+
+
+def pick_kernel(ids_hbm, probs_hbm, samples_hbm, grad_hbm, in_hbm, mine_ref, other_ref, select_ref, *scratch):
+    ids_ref, probs_ref, samples_ref, grad_ref, in_ref, sem = scratch
+    sources = (ids_hbm, probs_hbm, samples_hbm, grad_hbm, in_hbm)
+    copies = [pltpu.make_async_copy(x, y, sem.at[i]) for i, (x, y) in enumerate(zip(sources, scratch))]
+    for copy in copies:
+        copy.start()
+    count = grad_ref.shape[0]
+    me = lax.axis_index("node")
+    upto = lax.broadcasted_iota(jnp.int32, (count, count), 0) <= lax.broadcasted_iota(
+        jnp.int32, (count, count), 1
+    )
+    upto = upto.astype(F32).astype(BF)
+    slot = lax.broadcasted_iota(jnp.int32, (CAP, count), 0).astype(F32) + 1.0
+    for copy in copies[:3]:
+        copy.wait()
+    ids, probs = ids_ref[...], probs_ref[...]
+    sample = jnp.broadcast_to(samples_ref[...].astype(F32), (count, count))
+    length = jnp.sum((sample == sample.T).astype(F32), axis=0, keepdims=True)
+    loss_scale = TOK_DEV / (SAMPLES * length)
+    selects, factors = [], []
+    for i in range(2):
+        hit = ids == (me + i) % 2
+        coef = jnp.sum(jnp.where(hit, probs, 0.0), axis=0, keepdims=True)
+        member = jnp.max(hit.astype(F32), axis=0, keepdims=True)
+        rank = dot(jnp.broadcast_to(member, (CAP, count)).astype(BF), upto)
+        picked = (rank == slot) & (member > 0.0)
+        selects.append(picked.astype(F32))
+        factors.append(jnp.sum(jnp.where(picked, coef * loss_scale, 0.0), axis=1, keepdims=True))
+    select = jnp.concatenate(selects).astype(BF)
+    factor = jnp.concatenate(factors)
+    select_ref[...] = select
+    tiles = tiles_of(grad_ref.shape[1], 1024)
+    copies[3].wait()
+    for k in tiles:
+        grads = (factor * dot(select, grad_ref[:, k])).astype(BF)
+        mine_ref[:CAP, k] = grads[:CAP]
+        other_ref[:CAP, k] = grads[CAP:]
+    copies[4].wait()
+    for k in tiles:
+        ins = dot(select, in_ref[:, k]).astype(BF)
+        mine_ref[CAP:, k] = ins[:CAP]
+        other_ref[CAP:, k] = ins[CAP:]
+
+
+def pick(*arrays):
+    count, width = arrays[-1].shape
+    return pl.pallas_call(
+        pick_kernel,
+        in_specs=[pl.BlockSpec(memory_space=pltpu.HBM)] * 5,
+        out_specs=[IN_VMEM] * 3,
+        out_shape=[in_vmem(2 * CAP, width), in_vmem(2 * CAP, width), in_vmem(2 * CAP, count)],
+        scratch_shapes=[pltpu.VMEM(x.shape, x.dtype) for x in arrays] + [pltpu.SemaphoreType.DMA((5,))],
+        compiler_params=pltpu.CompilerParams(vmem_limit_bytes=8 << 20),
+        name="pick",
+    )(*[streamed(x) for x in arrays])
+
+
+def load_kernel(n, *refs):
+    copies = [pltpu.make_async_copy(refs[i], refs[n + i], refs[2 * n].at[i]) for i in range(n)]
+    for copy in copies:
+        copy.start()
+    for copy in copies:
+        copy.wait()
+
+
+def load(*arrays):
+    n = len(arrays)
+    return pl.pallas_call(
+        functools.partial(load_kernel, n),
+        in_specs=[pl.BlockSpec(memory_space=pltpu.HBM)] * n,
+        out_specs=[IN_VMEM] * n,
+        out_shape=[in_vmem(*x.shape) for x in arrays],
+        scratch_shapes=[pltpu.SemaphoreType.DMA((n,))],
+        cost_estimate=LIGHT,
+        compiler_params=pltpu.CompilerParams(vmem_limit_bytes=1 << 20),
+        name="load",
+    )(*[streamed(x) for x in arrays])
+
+
+def work_kernel(n, *refs):
+    blocks, (gate_ref, up_ref, down_ref) = refs[:n], refs[n : n + 3]
+    pieces = refs[n + 3 : 2 * n + 3]
+    hidden_ref, d_up_ref, d_gate_ref, grads_ref, ins_ref = refs[2 * n + 3 :]
+    for i, block in enumerate(blocks):
+        rows = pl.ds(i * CAP, CAP)
+        grads_ref[rows, :] = block[:CAP, :]
+        ins_ref[rows, :] = block[CAP:, :]
+    gate_pre = jnp.zeros((n * CAP, gate_ref.shape[0]), F32)
+    up_pre = d_act = gate_pre
+    for k in tiles_of(gate_ref.shape[1], 1024):
+        gate_pre += dot(ins_ref[:, k], gate_ref[:, k], NT)
+        up_pre += dot(ins_ref[:, k], up_ref[:, k], NT)
+        d_act += dot(grads_ref[:, k], down_ref[:, k], NT)
+    act, slope = silu_parts(gate_pre)
+    d_up = (d_act * act).astype(BF)
+    d_gate = (d_act * up_pre * slope).astype(BF)
+    hidden_ref[...] = (act * up_pre).astype(BF)
+    d_up_ref[...] = d_up
+    d_gate_ref[...] = d_gate
+    for k in tiles_of(gate_ref.shape[1], 1024):
+        p = (dot(d_gate, gate_ref[:, k]) + dot(d_up, up_ref[:, k])).astype(BF)
+        for i, piece in enumerate(pieces):
+            piece[:, k] = p[i * CAP : (i + 1) * CAP]
+
+
+def work(blocks, w_gate, w_up, w_down):
+    n = len(blocks)
+    hid, width = w_gate.shape
+    outs = [in_vmem(CAP, width)] * n + [in_vmem(n * CAP, hid)] * 3 + [in_vmem(n * CAP, width)] * 2
+    out = pl.pallas_call(
+        functools.partial(work_kernel, n),
+        in_specs=[IN_VMEM] * (n + 3),
+        out_specs=[IN_VMEM] * len(outs),
+        out_shape=outs,
+        cost_estimate=LIGHT,
+        compiler_params=pltpu.CompilerParams(vmem_limit_bytes=4 << 20),
+        name="work",
+    )(*[held(x) for x in blocks], held(w_gate), held(w_up), held(w_down))
+    return out[:n], out[n:]
+
+
+def weight_grads_kernel(n, *refs):
+    hidden, d_up, d_gate, grads, ins = (refs[i * n : (i + 1) * n] for i in range(5))
+    outs, (buffer, sem) = refs[5 * n : 5 * n + 3], refs[5 * n + 3 :]
+    copies = []
+    for i, (left, right) in enumerate(((d_gate, ins), (d_up, ins), (hidden, grads))):
+        across = jnp.concatenate([x[...] for x in left]).astype(F32).T.astype(BF)
+        for k in tiles_of(buffer.shape[2], 512):
+            buffer[i, :, k] = dot(across, jnp.concatenate([x[:, k] for x in right])).astype(BF)
+        copies.append(pltpu.make_async_copy(buffer.at[i], outs[i], sem.at[i]))
+        copies[i].start()
+    for copy in copies:
+        copy.wait()
+
+
+def weight_grads(saved):
+    n = len(saved)
+    hid, width = saved[0][0].shape[1], saved[0][3].shape[1]
+    return pl.pallas_call(
+        functools.partial(weight_grads_kernel, n),
+        in_specs=[IN_VMEM] * (5 * n),
+        out_specs=[pl.BlockSpec(memory_space=pl.ANY)] * 3,
+        out_shape=[jax.ShapeDtypeStruct((hid, width), BF)] * 3,
+        scratch_shapes=[pltpu.VMEM((3, hid, width), BF), pltpu.SemaphoreType.DMA((3,))],
+        cost_estimate=LIGHT,
+        compiler_params=pltpu.CompilerParams(vmem_limit_bytes=8 << 20),
+        name="weight_grads",
+    )(*[held(x) for part in zip(*saved) for x in part])
+
+
+def place_kernel(select_ref, own_ref, ahead_ref, behind_ref, first_ref, second_ref, out_ref, rows_ref, buffer, sem):
+    spread = select_ref[...].astype(F32).T.astype(BF)
+    for k in tiles_of(out_ref.shape[1], 1024):
+        here = own_ref[:, k].astype(F32) + ahead_ref[:, k].astype(F32) + behind_ref[:, k].astype(F32)
+        there = first_ref[:, k].astype(F32) + second_ref[:, k].astype(F32)
+        rows_ref[:CAP, k] = here.astype(BF)
+        rows_ref[CAP:, k] = there.astype(BF)
+    copies = []
+    for j, r in enumerate(tiles_of(out_ref.shape[0], buffer.shape[0] // 2)):
+        for k in tiles_of(out_ref.shape[1], 1024):
+            buffer[r, k] = dot(spread[r.start : r.start + r.size], rows_ref[:, k]).astype(BF)
+        copies.append(pltpu.make_async_copy(buffer.at[r], out_ref.at[r], sem.at[j]))
+        copies[j].start()
+    for copy in copies:
+        copy.wait()
+
+
+def place(select, own, ahead, behind, first, second):
+    count, width = select.shape[1], own.shape[1]
+    return pl.pallas_call(
+        place_kernel,
+        in_specs=[IN_VMEM] * 6,
+        out_specs=pl.BlockSpec(memory_space=pl.ANY),
+        out_shape=jax.ShapeDtypeStruct((count, width), BF),
+        scratch_shapes=[pltpu.VMEM((2 * CAP, width), BF), pltpu.VMEM((count, width), BF), pltpu.SemaphoreType.DMA((2,))],
+        compiler_params=pltpu.CompilerParams(vmem_limit_bytes=8 << 20),
+        name="place",
+    )(*[held(x) for x in (select, own, ahead, behind, first, second)])
+
+
+def per_device_ring(grad_out, layer_in, expert_ids, gate_probs, sample_ids, w_gate, w_up, w_down):
+    swap = [(0, 1), (1, 0)]
+    ahead, behind = ring_orders(lax.axis_size("local"))
+    half = lax.axis_size("local") // 2
+
+    def go(x):
+        return lax.ppermute(x, "local", ahead)
+
+    def back(x):
+        return lax.ppermute(x, "local", behind)
+
+    near, other, select = pick(expert_ids.T, gate_probs.T, sample_ids, grad_out, layer_in)
+    far = lax.ppermute(other, "node", swap)
+
+    weights = load(w_gate, w_up, w_down)
+    saved = []
+    pieces = {}
+
+    def work_on(members):
+        outs, keep = work([rows[member] for member in members], *weights)
+        pieces.update(zip(members, outs))
+        saved.append(keep)
+        return keep[0]
+
+    rows = {(0, 0): near, (0, 1): far}
+    near_go, near_back, far_go, far_back = near, near, far, far
+    for s in range(1, half):
+        near_go, near_back = go(near_go), back(near_back)
+        if s == 2:
+            far_go, far_back = after(far_go, weights[0]), after(far_back, weights[0])
+        far_go, far_back = go(far_go), back(far_back)
+        rows.update({(-s, 0): near_go, (s, 0): near_back, (-s, 1): far_go, (s, 1): far_back})
+        if s == half - 2:
+            done = work_on(list(rows)[:-2])
+            near_go, near_back = after(near_go, done), after(near_back, done)
+    near_go, near_back = together(near_go, near_back)
+    far_go, far_back = together(far_go, far_back)
+    near_go = go(near_go)
+    far_back = back(far_back)
+    rows.update({(half, 0): near_go, (half, 1): far_back})
+    work_on([member for member in rows if member not in pieces])
+
+    def add(x, y):
+        return (x.astype(F32) + y.astype(F32)).astype(BF)
+
+    far_long, near_long = pieces[half, 1], pieces[half, 0]
+    far_short, near_short = pieces[half - 1, 1], pieces[1 - half, 0]
+    for s in range(half - 1, 0, -1):
+        far_long, near_long = back(far_long), go(near_long)
+        far_short, near_short = go(far_short), back(near_short)
+        far_long, near_long = add(pieces[-s, 1], far_long), add(pieces[s, 0], near_long)
+        if s > 1:
+            far_short, near_short = add(pieces[s - 1, 1], far_short), add(pieces[1 - s, 0], near_short)
+            far_short, near_short = after(far_short, far_long), after(near_short, near_long)
+    saved[0] = [after(saved[0][0], far_long, near_long), *saved[0][1:]]
+    grad_gate, grad_up, grad_down = weight_grads(saved)
+    far_long, near_long = back(far_long), go(near_long)
+    first = lax.ppermute(after(add(pieces[0, 1], far_short), grad_gate), "node", swap)
+    second = lax.ppermute(far_long, "node", swap)
+    grad_in = place(select, pieces[0, 0], near_long, near_short, first, second)
+    return (grad_in, grad_gate, grad_up, grad_down)
+
+
 def solution(mesh):
+    nodes, locals_ = mesh.shape["node"], mesh.shape["local"]
+    ring = nodes == 2 and locals_ % 2 == 0 and locals_ >= 8
+
+    def per_device(*args):
+        shards = FF // args[5].shape[0]
+        if ring and shards == locals_:
+            return per_device_ring(*args)
+        return per_device_exchange(*args)
+
     return jax.shard_map(
         per_device,
         mesh=mesh,

time: 177 us -> 80.9 us (0.46)
  waiting for transfers between devices: 127 us -> 32.3 us
  matrix products: 25.6 us -> 0 us
  starting transfers between devices: 18 us -> 32.9 us
  Pallas kernels: 0 us -> 14.4 us
  local copies, waits for them, and re-layouts: 3.51 us -> 0 us
    all_to_all x3 -> x0, waiting for transfers between devices: 127 us -> none  [the longest x1 46.9 us: per_device(): lax.all_to_all(flat_in, ('node', 'local'), split_axis=0, concat_axis=0, t...]
    ppermute x0 -> x31, starting transfers between devices: none -> 32.9 us  [the longest x14 25.6 us: back(): return lax.ppermute(x, 'local', behind)]
    ppermute x0 -> x31, waiting for transfers between devices: none -> 32.3 us  [the longest x14 16.9 us: go(): return lax.ppermute(x, 'local', ahead)]
    dot_general x11 -> x0, matrix products: 25.6 us -> none  [the longest x1 3.35 us: per_device(): lax.dot_general(d_up, rows_in, over_rows, preferred_element_type=jnp.floa...]
    all_to_all x3 -> x0, starting transfers between devices: 18 us -> none  [the longest x1 7.58 us: per_device(): lax.all_to_all(flat_in, ('node', 'local'), split_axis=0, concat_axis=0, t...]
    pallas_call x0 -> x6, Pallas kernels: none -> 14.4 us  [the longest x2 5.95 us: work(): pl.pallas_call(functools.partial(work_kernel, n), in_specs=[IN_VMEM] * (n...]
    broadcast_in_dim x3 -> x0, local copies, waits for them, and re-layouts: 3.11 us -> none  [the longest x1 1.55 us: per_device(): jnp.broadcast_to(send_in.reshape(wave, 1, CAP, width), (wave, shards, CAP...]
  transfers between devices with their start and end apart: 3 -> 31, of which waited for: 3 -> 20; matrix products, arithmetic and copies ran while one was open for 9% -> 0% of each run, Pallas kernels for 0% -> 10%
where the time goes in v2:
time: 80.9 us; the launch traced here: 80.8 us
  starting transfers between devices  32.9 us (41%)
  waiting for transfers between devices  32.3 us (40%)
  Pallas kernels  14.4 us (18%)
    ppermute x14, starting transfers between devices, back(): return lax.ppermute(x, 'local', behind)  25.6 us
    ppermute x14, waiting for transfers between devices, go(): return lax.ppermute(x, 'local', ahead)  16.9 us
    ppermute x14, waiting for transfers between devices, back(): return lax.ppermute(x, 'local', behind)  14.2 us
    ppermute x14, starting transfers between devices, go(): return lax.ppermute(x, 'local', ahead)  6.49 us
    pallas_call x2, Pallas kernels, work(): pl.pallas_call(functools.partial(work_kernel, n), in_specs=[IN_VMEM] * (n...  5.95 us
    pallas_call x1, Pallas kernels, weight_grads(): pl.pallas_call(functools.partial(weight_grads_kernel, n), in_specs=[IN_VM...  2.84 us
    pallas_call x1, Pallas kernels, load(): pl.pallas_call(functools.partial(load_kernel, n), in_specs=[pl.BlockSpec(...  2.38 us
    pallas_call x1, Pallas kernels, pick(): pl.pallas_call(pick_kernel, in_specs=[pl.BlockSpec(memory_space=pltpu.HBM...  1.91 us
  transfers between devices with their start and end apart: 31, of which 20 were waited for; matrix products, arithmetic and copies ran while one was open for 0% of the time, Pallas kernels for 10%

profile of v2, /device:TPU:0, one launch (start us, length us, event | category | flops | bytes accessed | tf_op | source)
XLA Modules:
  0.0 80.8 jit_solution(8379418888882580107)
XLA Ops:
  0.6 1.9 %pick.1 = (bf16[32,4096]{1,0:T(8,128)(2,1)S(1)}, bf16[32,4096]{1,0:T(8,128)(2,1)S(1)}, bf16[32,128]{1,0:T(8,128)(2,1)S(1)}) custom-call(s32[8,128]{1,0:T(8,128)} %bitcast.2, f32[8,128]{1,0:T(8,128)} %bitcast.3, s32[1,128]{1,0:T(1,128)} %samples_hbm.1, bf16[128,4096]{1,0:T(8,128)(2,1)} %grad_hbm.1, bf16[128,4096]{1,0:T(8,128)(2,1)} %in_hbm.1), custom_call_target="tpu_custom_call" | custom-call | tf_op jit(solution)/shard_map/pick/pallas_call | solution.py:185
  2.6 0.5 collective-permute-start
  3.1 2.6 %collective-permute-start.2 = (bf16[32,4096]{1,0:T(8,128)(2,1)S(1)}, bf16[32,4096]{1,0:T(8,128)(2,1)S(1)}, u32[]{:S(2)}, u32[]{:S(2)}) collective-permute-start(bf16[32,4096]{1,0:T(8,128)(2,1)S(1)} %get-tuple-element.52.refs_0_), channel_id=1, source_target_pairs={{0,1},{2,0},{4,2},{6,4},{7,6},{5,7},{3,5},{1,3},{8,9},{10,8},{12,1... | collective-permute-start | bytes 786440 | tf_op jit(solution)/shard_map/ppermute | solution.py:328
  5.8 1.9 %collective-permute-start.4 = (bf16[32,4096]{1,0:T(8,128)(2,1)S(1)}, bf16[32,4096]{1,0:T(8,128)(2,1)S(1)}, u32[]{:S(2)}, u32[]{:S(2)}) collective-permute-start(bf16[32,4096]{1,0:T(8,128)(2,1)S(1)} %collective-permute-done.refs_1_), channel_id=1, source_target_pairs={{0,1},{2,0},{4,2},{6,4},{7,6},{5,7},{3,5},{1,3},{8,9},{10,8},{12,1... | collective-permute-start | bytes 786440 | tf_op jit(solution)/shard_map/ppermute | solution.py:328
  7.8 5.0 %collective-permute-done.2.refs_3_ = bf16[32,4096]{1,0:T(8,128)(2,1)S(1)} collective-permute-done((bf16[32,4096]{1,0:T(8,128)(2,1)S(1)}, bf16[32,4096]{1,0:T(8,128)(2,1)S(1)}, u32[]{:S(2)}, u32[]{:S(2)}) %collective-permute-start.2) | collective-permute-done | bytes 262176 | tf_op jit(solution)/shard_map/ppermute | solution.py:328
  12.9 1.9 %collective-permute-start.6 = (bf16[32,4096]{1,0:T(8,128)(2,1)S(1)}, bf16[32,4096]{1,0:T(8,128)(2,1)S(1)}, u32[]{:S(2)}, u32[]{:S(2)}) collective-permute-start(bf16[32,4096]{1,0:T(8,128)(2,1)S(1)} %collective-permute-done.2.refs_3_), channel_id=1, source_target_pairs={{0,1},{2,0},{4,2},{6,4},{7,6},{5,7},{3,5},{1,3},{8,9},{10,8},{12,1... | collective-permute-start | bytes 786440 | tf_op jit(solution)/shard_map/ppermute | solution.py:328
  14.9 2.4 %load.1 = (bf16[192,4096]{1,0:T(8,128)(2,1)S(1)}, bf16[192,4096]{1,0:T(8,128)(2,1)S(1)}, bf16[192,4096]{1,0:T(8,128)(2,1)S(1)}) custom-call(bf16[192,4096]{1,0:T(8,128)(2,1)} %refs_0_.1, bf16[192,4096]{1,0:T(8,128)(2,1)} %refs_1_.1, bf16[192,4096]{1,0:T(8,128)(2,1)} %refs_2_.1), custom_call_target="tpu_custom_call" | custom-call | tf_op jit(solution)/shard_map/load/pallas_call | solution.py:206
  17.3 1.2 %collective-permute-done.4.refs_5_ = bf16[32,4096]{1,0:T(8,128)(2,1)S(1)} collective-permute-done((bf16[32,4096]{1,0:T(8,128)(2,1)S(1)}, bf16[32,4096]{1,0:T(8,128)(2,1)S(1)}, u32[]{:S(2)}, u32[]{:S(2)}) %collective-permute-start.4) | collective-permute-done | bytes 262176 | tf_op jit(solution)/shard_map/ppermute | solution.py:328
  18.5 1.9 %collective-permute-done.3.refs_4_ = bf16[32,4096]{1,0:T(8,128)(2,1)S(1)} collective-permute-done((bf16[32,4096]{1,0:T(8,128)(2,1)S(1)}, bf16[32,4096]{1,0:T(8,128)(2,1)S(1)}, u32[]{:S(2)}, u32[]{:S(2)}) %collective-permute-start.3) | collective-permute-done | bytes 262176 | tf_op jit(solution)/shard_map/ppermute | solution.py:325
  20.5 1.9 %collective-permute-start.8 = (bf16[32,4096]{1,0:T(8,128)(2,1)S(1)}, bf16[32,4096]{1,0:T(8,128)(2,1)S(1)}, u32[]{:S(2)}, u32[]{:S(2)}) collective-permute-start(bf16[32,4096]{1,0:T(8,128)(2,1)S(1)} %collective-permute-done.4.refs_5_), channel_id=1, source_target_pairs={{0,1},{2,0},{4,2},{6,4},{7,6},{5,7},{3,5},{1,3},{8,9},{10,8},{12,1... | collective-permute-start | bytes 786440 | tf_op jit(solution)/shard_map/ppermute | solution.py:328
  22.4 1.7 %collective-permute-done.6.refs_7_ = bf16[32,4096]{1,0:T(8,128)(2,1)S(1)} collective-permute-done((bf16[32,4096]{1,0:T(8,128)(2,1)S(1)}, bf16[32,4096]{1,0:T(8,128)(2,1)S(1)}, u32[]{:S(2)}, u32[]{:S(2)}) %collective-permute-start.6) | collective-permute-done | bytes 262176 | tf_op jit(solution)/shard_map/ppermute | solution.py:328
  24.1 1.9 %collective-permute-done.5.refs_6_ = bf16[32,4096]{1,0:T(8,128)(2,1)S(1)} collective-permute-done((bf16[32,4096]{1,0:T(8,128)(2,1)S(1)}, bf16[32,4096]{1,0:T(8,128)(2,1)S(1)}, u32[]{:S(2)}, u32[]{:S(2)}) %collective-permute-start.5) | collective-permute-done | bytes 262176 | tf_op jit(solution)/shard_map/ppermute | solution.py:325
  26.0 3.0 %work.2 = (bf16[16,4096]{1,0:T(8,128)(2,1)S(1)}, bf16[16,4096]{1,0:T(8,128)(2,1)S(1)}, bf16[16,4096]{1,0:T(8,128)(2,1)S(1)}, bf16[16,4096]{1,0:T(8,128)(2,1)S(1)...) custom-call(bf16[32,4096]{1,0:T(8,128)(2,1)S(1)} %get-tuple-element., ...), custom_call_target="tpu_custom_call" | custom-call | tf_op jit(solution)/shard_map/work/pallas_call | solution.py:248
  29.0 0.2 collective-permute-start.9
  29.2 1.9 %collective-permute-start.10 = (bf16[32,4096]{1,0:T(8,128)(2,1)S(1)}, bf16[32,4096]{1,0:T(8,128)(2,1)S(1)}, u32[]{:S(2)}, u32[]{:S(2)}) collective-permute-start(bf16[32,4096]{1,0:T(8,128)(2,1)S(1)} %collective-permute-done.6.refs_7_), channel_id=1, source_target_pairs={{0,1},{2,0},{4,2},{6,4},{7,6},{5,7},{3,5},{1,3},{8,9},{10,8},{12,1... | collective-permute-start | bytes 786440 | tf_op jit(solution)/shard_map/ppermute | solution.py:328
  31.1 0.4 collective-permute-done.7.refs_0_
  31.5 2.0 %collective-permute-start.12 = (bf16[32,4096]{1,0:T(8,128)(2,1)S(1)}, bf16[32,4096]{1,0:T(8,128)(2,1)S(1)}, u32[]{:S(2)}, u32[]{:S(2)}) collective-permute-start(bf16[32,4096]{1,0:T(8,128)(2,1)S(1)} %collective-permute-done.8.refs_1_), channel_id=1, source_target_pairs={{0,1},{2,0},{4,2},{6,4},{7,6},{5,7},{3,5},{1,3},{8,9},{10,8},{12,1... | collective-permute-start | bytes 786440 | tf_op jit(solution)/shard_map/ppermute | solution.py:328
  33.5 4.8 %collective-permute-done.9.refs_2_ = bf16[32,4096]{1,0:T(8,128)(2,1)S(1)} collective-permute-done((bf16[32,4096]{1,0:T(8,128)(2,1)S(1)}, bf16[32,4096]{1,0:T(8,128)(2,1)S(1)}, u32[]{:S(2)}, u32[]{:S(2)}) %collective-permute-start.9) | collective-permute-done | bytes 262176 | tf_op jit(solution)/shard_map/ppermute | solution.py:325
  38.5 1.9 %collective-permute-start.13 = (bf16[32,4096]{1,0:T(8,128)(2,1)S(1)}, bf16[32,4096]{1,0:T(8,128)(2,1)S(1)}, u32[]{:S(2)}, u32[]{:S(2)}) collective-permute-start(bf16[32,4096]{1,0:T(8,128)(2,1)S(1)} %collective-permute-done.9.refs_2_), channel_id=1, source_target_pairs={{0,2},{2,4},{4,6},{6,7},{7,5},{5,3},{3,1},{1,0},{8,10},{10,12},{12... | collective-permute-start | bytes 786440 | tf_op jit(solution)/shard_map/ppermute | solution.py:325
  40.4 3.5 %collective-permute-done.11.refs_4_ = bf16[32,4096]{1,0:T(8,128)(2,1)S(1)} collective-permute-done((bf16[32,4096]{1,0:T(8,128)(2,1)S(1)}, bf16[32,4096]{1,0:T(8,128)(2,1)S(1)}, u32[]{:S(2)}, u32[]{:S(2)}) %collective-permute-start.11) | collective-permute-done | bytes 262176 | tf_op jit(solution)/shard_map/ppermute | solution.py:325
  43.9 1.6 %collective-permute-start.14 = (bf16[32,4096]{1,0:T(8,128)(2,1)S(1)}, bf16[32,4096]{1,0:T(8,128)(2,1)S(1)}, u32[]{:S(2)}, u32[]{:S(2)}) collective-permute-start(bf16[32,4096]{1,0:T(8,128)(2,1)S(1)} %collective-permute-done.12.refs_5_), channel_id=1, source_target_pairs={{0,1},{2,0},{4,2},{6,4},{7,6},{5,7},{3,5},{1,3},{8,9},{10,8},{12,1... | collective-permute-start | bytes 786440 | tf_op jit(solution)/shard_map/ppermute | solution.py:328
  45.5 2.2 %collective-permute-done.13.refs_6_ = bf16[32,4096]{1,0:T(8,128)(2,1)S(1)} collective-permute-done((bf16[32,4096]{1,0:T(8,128)(2,1)S(1)}, bf16[32,4096]{1,0:T(8,128)(2,1)S(1)}, u32[]{:S(2)}, u32[]{:S(2)}) %collective-permute-start.13) | collective-permute-done | bytes 262176 | tf_op jit(solution)/shard_map/ppermute | solution.py:325
  47.7 2.6 %collective-permute-done.14.refs_7_ = bf16[32,4096]{1,0:T(8,128)(2,1)S(1)} collective-permute-done((bf16[32,4096]{1,0:T(8,128)(2,1)S(1)}, bf16[32,4096]{1,0:T(8,128)(2,1)S(1)}, u32[]{:S(2)}, u32[]{:S(2)}) %collective-permute-start.14) | collective-permute-done | bytes 262176 | tf_op jit(solution)/shard_map/ppermute | solution.py:328
  50.3 3.0 %work.3 = (bf16[16,4096]{1,0:T(8,128)(2,1)S(1)}, bf16[16,4096]{1,0:T(8,128)(2,1)S(1)}, bf16[16,4096]{1,0:T(8,128)(2,1)S(1)}, bf16[16,4096]{1,0:T(8,128)(2,1)S(1)...) custom-call(bf16[32,4096]{1,0:T(8,128)(2,1)S(1)} %collective-permute, ...), custom_call_target="tpu_custom_call" | custom-call | tf_op jit(solution)/shard_map/work/pallas_call | solution.py:248
  53.3 0.3 collective-permute-start.15
  53.6 1.8 %collective-permute-start.19 = (bf16[16,4096]{1,0:T(8,128)(2,1)S(1)}, bf16[16,4096]{1,0:T(8,128)(2,1)S(1)}, u32[]{:S(2)}, u32[]{:S(2)}) collective-permute-start(bf16[16,4096]{1,0:T(8,128)(2,1)S(1)} %get-tuple-element.71), channel_id=1, source_target_pairs={{0,1},{2,0},{4,2},{6,4},{7,6},{5,7},{3,5},{1,3},{8,9},{10,8},{12,1... | collective-permute-start | bytes 393224 | tf_op jit(solution)/shard_map/ppermute | solution.py:328
  55.4 0.2 collective-permute-start.22
  55.6 1.8 %collective-permute-start.23 = (bf16[16,4096]{1,0:T(8,128)(2,1)S(1)}, bf16[16,4096]{1,0:T(8,128)(2,1)S(1)}, u32[]{:S(2)}, u32[]{:S(2)}) collective-permute-start(bf16[16,4096]{1,0:T(8,128)(2,1)S(1)} %get-tuple-element.79), channel_id=1, source_target_pairs={{0,1},{2,0},{4,2},{6,4},{7,6},{5,7},{3,5},{1,3},{8,9},{10,8},{12,1... | collective-permute-start | bytes 393224 | tf_op jit(solution)/shard_map/ppermute | solution.py:328
  57.4 1.0 %collective-permute-done.15 = bf16[16,4096]{1,0:T(8,128)(2,1)S(1)} collective-permute-done((bf16[16,4096]{1,0:T(8,128)(2,1)S(1)}, bf16[16,4096]{1,0:T(8,128)(2,1)S(1)}, u32[]{:S(2)}, u32[]{:S(2)}) %collective-permute-start.15) | collective-permute-done | bytes 131104 | tf_op jit(solution)/shard_map/ppermute | solution.py:325
  58.4 0.5 collective-permute-start.16
  59.0 1.0 %collective-permute-done.19 = bf16[16,4096]{1,0:T(8,128)(2,1)S(1)} collective-permute-done((bf16[16,4096]{1,0:T(8,128)(2,1)S(1)}, bf16[16,4096]{1,0:T(8,128)(2,1)S(1)}, u32[]{:S(2)}, u32[]{:S(2)}) %collective-permute-start.19) | collective-permute-done | bytes 131104 | tf_op jit(solution)/shard_map/ppermute | solution.py:328
  60.0 1.7 %collective-permute-start.20 = (bf16[16,4096]{1,0:T(8,128)(2,1)S(1)}, bf16[16,4096]{1,0:T(8,128)(2,1)S(1)}, u32[]{:S(2)}, u32[]{:S(2)}) collective-permute-start(bf16[16,4096]{1,0:T(8,128)(2,1)S(1)} %add_convert_fusion.7), channel_id=1, source_target_pairs={{0,1},{2,0},{4,2},{6,4},{7,6},{5,7},{3,5},{1,3},{8,9},{10,8},{12,1... | collective-permute-start | bytes 393224 | tf_op jit(solution)/shard_map/ppermute | solution.py:328
  61.7 0.8 collective-permute-done.23
  62.5 1.9 %collective-permute-start.25 = (bf16[16,4096]{1,0:T(8,128)(2,1)S(1)}, bf16[16,4096]{1,0:T(8,128)(2,1)S(1)}, u32[]{:S(2)}, u32[]{:S(2)}) collective-permute-start(bf16[16,4096]{1,0:T(8,128)(2,1)S(1)} %add_convert_fusion.4), channel_id=1, source_target_pairs={{0,1},{2,0},{4,2},{6,4},{7,6},{5,7},{3,5},{1,3},{8,9},{10,8},{12,1... | collective-permute-start | bytes 393224 | tf_op jit(solution)/shard_map/ppermute | solution.py:328
  64.5 0.2 collective-permute-start.24
  64.8 1.8 %collective-permute-start.17 = (bf16[16,4096]{1,0:T(8,128)(2,1)S(1)}, bf16[16,4096]{1,0:T(8,128)(2,1)S(1)}, u32[]{:S(2)}, u32[]{:S(2)}) collective-permute-start(bf16[16,4096]{1,0:T(8,128)(2,1)S(1)} %add_convert_fusion.9), channel_id=1, source_target_pairs={{0,2},{2,4},{4,6},{6,7},{7,5},{5,3},{3,1},{1,0},{8,10},{10,12},{12... | collective-permute-start | bytes 393224 | tf_op jit(solution)/shard_map/ppermute | solution.py:325
  66.6 0.8 collective-permute-start.21
  67.4 0.2 collective-permute-done.25
  67.6 2.1 %collective-permute-start.27 = (bf16[16,4096]{1,0:T(8,128)(2,1)S(1)}, bf16[16,4096]{1,0:T(8,128)(2,1)S(1)}, u32[]{:S(2)}, u32[]{:S(2)}) collective-permute-start(bf16[16,4096]{1,0:T(8,128)(2,1)S(1)} %add_convert_fusion.2), channel_id=1, source_target_pairs={{0,1},{2,0},{4,2},{6,4},{7,6},{5,7},{3,5},{1,3},{8,9},{10,8},{12,1... | collective-permute-start | bytes 393224 | tf_op jit(solution)/shard_map/ppermute | solution.py:328
  69.8 1.1 %collective-permute-done.17 = bf16[16,4096]{1,0:T(8,128)(2,1)S(1)} collective-permute-done((bf16[16,4096]{1,0:T(8,128)(2,1)S(1)}, bf16[16,4096]{1,0:T(8,128)(2,1)S(1)}, u32[]{:S(2)}, u32[]{:S(2)}) %collective-permute-start.17) | collective-permute-done | bytes 131104 | tf_op jit(solution)/shard_map/ppermute | solution.py:325
  70.9 0.7 collective-permute-start.18
  71.7 1.3 %collective-permute-done.27 = bf16[16,4096]{1,0:T(8,128)(2,1)S(1)} collective-permute-done((bf16[16,4096]{1,0:T(8,128)(2,1)S(1)}, bf16[16,4096]{1,0:T(8,128)(2,1)S(1)}, u32[]{:S(2)}, u32[]{:S(2)}) %collective-permute-start.27) | collective-permute-done | bytes 131104 | tf_op jit(solution)/shard_map/ppermute | solution.py:328
  73.1 1.7 %collective-permute-start.29 = (bf16[16,4096]{1,0:T(8,128)(2,1)S(1)}, bf16[16,4096]{1,0:T(8,128)(2,1)S(1)}, u32[]{:S(2)}, u32[]{:S(2)}) collective-permute-start(bf16[16,4096]{1,0:T(8,128)(2,1)S(1)} %add_convert_fusion), channel_id=1, source_target_pairs={{0,1},{2,0},{4,2},{6,4},{7,6},{5,7},{3,5},{1,3},{8,9},{10,8},{12,1... | collective-permute-start | bytes 393224 | tf_op jit(solution)/shard_map/ppermute | solution.py:328
  74.8 2.8 %weight_grads.1 = (bf16[192,4096]{1,0:T(8,128)(2,1)}, bf16[192,4096]{1,0:T(8,128)(2,1)}, bf16[192,4096]{1,0:T(8,128)(2,1)}) custom-call(bf16[128,192]{1,0:T(8,128)(2,1)S(1)} %get-tuple-element.84.refs_0_, bf16[128,192]{1,0:T(8,128)(2,1)S(1)} %get-tuple-element.85.refs_1_, bf16[128,192]{1,0:T(8,128)(2,1)S(1)} %get-tuple-element.86.refs_2_, ...), custom_call_target="tpu_custom_call" | custom-call | tf_op jit(solution)/shard_map/weight_grads/pallas_call | solution.py:277
  77.8 0.3 collective-permute-done.29
  78.3 0.8 %collective-permute-done.28.first_ref = bf16[16,4096]{1,0:T(8,128)(2,1)S(1)} collective-permute-done((bf16[16,4096]{1,0:T(8,128)(2,1)S(1)}, bf16[16,4096]{1,0:T(8,128)(2,1)S(1)}, u32[]{:S(2)}, u32[]{:S(2)}) %collective-permute-start.28) | collective-permute-done | bytes 131104 | tf_op jit(solution)/shard_map/ppermute | solution.py:376
  79.1 0.3 collective-permute-done.30.second_ref
  79.4 1.3 %place.1 = bf16[128,4096]{1,0:T(8,128)(2,1)} custom-call(bf16[32,128]{1,0:T(8,128)(2,1)S(1)} %get-tuple-element.51.select_ref, bf16[16,4096]{1,0:T(8,128)(2,1)S(1)} %get-tuple-element.57.own_ref, bf16[16,4096]{1,0:T(8,128)(2,1)S(1)} %collective-permute-done.18.ahead_ref, bf16[16,4096]{1,0:T(8,128)(2,1)S(1)} %collective-permute-done.21.behind_ref, ...), custom_call_target="tpu_custom_call" | custom-call | tf_op jit(solution)/shard_map/place/pallas_call | solution.py:308
  (31 shorter events, 1.4 us)
Async XLA Ops:
  2.6 3.2 %collective-permute-start = (bf16[32,4096]{1,0:T(8,128)(2,1)S(1)}, bf16[32,4096]{1,0:T(8,128)(2,1)S(1)}, u32[]{:S(2)}, u32[]{:S(2)}) collective-permute-start(bf16[32,4096]{1,0:T(8,128)(2,1)S(1)} %get-tuple-element.53), channel_id=1, source_target_pairs={{0,8},{8,0},{1,9},{9,1},{2,10},{10,2},{3,11},{11,3},{4,12},{12,4},... | collective-permute-start | bytes 786440 | tf_op jit(solution)/shard_map/ppermute | solution.py:331
  3.1 9.8 %collective-permute-start.2 = (bf16[32,4096]{1,0:T(8,128)(2,1)S(1)}, bf16[32,4096]{1,0:T(8,128)(2,1)S(1)}, u32[]{:S(2)}, u32[]{:S(2)}) collective-permute-start(bf16[32,4096]{1,0:T(8,128)(2,1)S(1)} %get-tuple-element.52.refs_0_), channel_id=1, source_target_pairs={{0,1},{2,0},{4,2},{6,4},{7,6},{5,7},{3,5},{1,3},{8,9},{10,8},{12,1... | collective-permute-start | bytes 786440 | tf_op jit(solution)/shard_map/ppermute | solution.py:328
  5.6 9.1 %collective-permute-start.1 = (bf16[32,4096]{1,0:T(8,128)(2,1)S(1)}, bf16[32,4096]{1,0:T(8,128)(2,1)S(1)}, u32[]{:S(2)}, u32[]{:S(2)}) collective-permute-start(bf16[32,4096]{1,0:T(8,128)(2,1)S(1)} %get-tuple-element.52.refs_0_), channel_id=1, source_target_pairs={{0,2},{2,4},{4,6},{6,7},{7,5},{5,3},{3,1},{1,0},{8,10},{10,12},{12... | collective-permute-start | bytes 786440 | tf_op jit(solution)/shard_map/ppermute | solution.py:325
  5.8 12.7 %collective-permute-start.4 = (bf16[32,4096]{1,0:T(8,128)(2,1)S(1)}, bf16[32,4096]{1,0:T(8,128)(2,1)S(1)}, u32[]{:S(2)}, u32[]{:S(2)}) collective-permute-start(bf16[32,4096]{1,0:T(8,128)(2,1)S(1)} %collective-permute-done.refs_1_), channel_id=1, source_target_pairs={{0,1},{2,0},{4,2},{6,4},{7,6},{5,7},{3,5},{1,3},{8,9},{10,8},{12,1... | collective-permute-start | bytes 786440 | tf_op jit(solution)/shard_map/ppermute | solution.py:328
  7.7 12.7 %collective-permute-start.3 = (bf16[32,4096]{1,0:T(8,128)(2,1)S(1)}, bf16[32,4096]{1,0:T(8,128)(2,1)S(1)}, u32[]{:S(2)}, u32[]{:S(2)}) collective-permute-start(bf16[32,4096]{1,0:T(8,128)(2,1)S(1)} %collective-permute-done.refs_1_), channel_id=1, source_target_pairs={{0,2},{2,4},{4,6},{6,7},{7,5},{5,3},{3,1},{1,0},{8,10},{10,12},{12... | collective-permute-start | bytes 786440 | tf_op jit(solution)/shard_map/ppermute | solution.py:325
  12.9 11.2 %collective-permute-start.6 = (bf16[32,4096]{1,0:T(8,128)(2,1)S(1)}, bf16[32,4096]{1,0:T(8,128)(2,1)S(1)}, u32[]{:S(2)}, u32[]{:S(2)}) collective-permute-start(bf16[32,4096]{1,0:T(8,128)(2,1)S(1)} %collective-permute-done.2.refs_3_), channel_id=1, source_target_pairs={{0,1},{2,0},{4,2},{6,4},{7,6},{5,7},{3,5},{1,3},{8,9},{10,8},{12,1... | collective-permute-start | bytes 786440 | tf_op jit(solution)/shard_map/ppermute | solution.py:328
  14.8 11.2 %collective-permute-start.5 = (bf16[32,4096]{1,0:T(8,128)(2,1)S(1)}, bf16[32,4096]{1,0:T(8,128)(2,1)S(1)}, u32[]{:S(2)}, u32[]{:S(2)}) collective-permute-start(bf16[32,4096]{1,0:T(8,128)(2,1)S(1)} %collective-permute-done.1.refs_2_), channel_id=1, source_target_pairs={{0,2},{2,4},{4,6},{6,7},{7,5},{5,3},{3,1},{1,0},{8,10},{10,12},{12... | collective-permute-start | bytes 786440 | tf_op jit(solution)/shard_map/ppermute | solution.py:325
  20.4 11.0 %collective-permute-start.7 = (bf16[32,4096]{1,0:T(8,128)(2,1)S(1)}, bf16[32,4096]{1,0:T(8,128)(2,1)S(1)}, u32[]{:S(2)}, u32[]{:S(2)}) collective-permute-start(bf16[32,4096]{1,0:T(8,128)(2,1)S(1)} %collective-permute-done.3.refs_4_), channel_id=1, source_target_pairs={{0,2},{2,4},{4,6},{6,7},{7,5},{5,3},{3,1},{1,0},{8,10},{10,12},{12... | collective-permute-start | bytes 786440 | tf_op jit(solution)/shard_map/ppermute | solution.py:325
  20.5 10.9 %collective-permute-start.8 = (bf16[32,4096]{1,0:T(8,128)(2,1)S(1)}, bf16[32,4096]{1,0:T(8,128)(2,1)S(1)}, u32[]{:S(2)}, u32[]{:S(2)}) collective-permute-start(bf16[32,4096]{1,0:T(8,128)(2,1)S(1)} %collective-permute-done.4.refs_5_), channel_id=1, source_target_pairs={{0,1},{2,0},{4,2},{6,4},{7,6},{5,7},{3,5},{1,3},{8,9},{10,8},{12,1... | collective-permute-start | bytes 786440 | tf_op jit(solution)/shard_map/ppermute | solution.py:328
  29.0 9.3 %collective-permute-start.9 = (bf16[32,4096]{1,0:T(8,128)(2,1)S(1)}, bf16[32,4096]{1,0:T(8,128)(2,1)S(1)}, u32[]{:S(2)}, u32[]{:S(2)}) collective-permute-start(bf16[32,4096]{1,0:T(8,128)(2,1)S(1)} %collective-permute-done.5.refs_6_), channel_id=1, source_target_pairs={{0,2},{2,4},{4,6},{6,7},{7,5},{5,3},{3,1},{1,0},{8,10},{10,12},{12... | collective-permute-start | bytes 786440 | tf_op jit(solution)/shard_map/ppermute | solution.py:325
  29.2 9.2 %collective-permute-start.10 = (bf16[32,4096]{1,0:T(8,128)(2,1)S(1)}, bf16[32,4096]{1,0:T(8,128)(2,1)S(1)}, u32[]{:S(2)}, u32[]{:S(2)}) collective-permute-start(bf16[32,4096]{1,0:T(8,128)(2,1)S(1)} %collective-permute-done.6.refs_7_), channel_id=1, source_target_pairs={{0,1},{2,0},{4,2},{6,4},{7,6},{5,7},{3,5},{1,3},{8,9},{10,8},{12,1... | collective-permute-start | bytes 786440 | tf_op jit(solution)/shard_map/ppermute | solution.py:328
  31.5 12.5 %collective-permute-start.11 = (bf16[32,4096]{1,0:T(8,128)(2,1)S(1)}, bf16[32,4096]{1,0:T(8,128)(2,1)S(1)}, u32[]{:S(2)}, u32[]{:S(2)}) collective-permute-start(bf16[32,4096]{1,0:T(8,128)(2,1)S(1)} %collective-permute-done.7.refs_0_), channel_id=1, source_target_pairs={{0,2},{2,4},{4,6},{6,7},{7,5},{5,3},{3,1},{1,0},{8,10},{10,12},{12... | collective-permute-start | bytes 786440 | tf_op jit(solution)/shard_map/ppermute | solution.py:325
  31.5 12.5 %collective-permute-start.12 = (bf16[32,4096]{1,0:T(8,128)(2,1)S(1)}, bf16[32,4096]{1,0:T(8,128)(2,1)S(1)}, u32[]{:S(2)}, u32[]{:S(2)}) collective-permute-start(bf16[32,4096]{1,0:T(8,128)(2,1)S(1)} %collective-permute-done.8.refs_1_), channel_id=1, source_target_pairs={{0,1},{2,0},{4,2},{6,4},{7,6},{5,7},{3,5},{1,3},{8,9},{10,8},{12,1... | collective-permute-start | bytes 786440 | tf_op jit(solution)/shard_map/ppermute | solution.py:328
  38.5 9.2 %collective-permute-start.13 = (bf16[32,4096]{1,0:T(8,128)(2,1)S(1)}, bf16[32,4096]{1,0:T(8,128)(2,1)S(1)}, u32[]{:S(2)}, u32[]{:S(2)}) collective-permute-start(bf16[32,4096]{1,0:T(8,128)(2,1)S(1)} %collective-permute-done.9.refs_2_), channel_id=1, source_target_pairs={{0,2},{2,4},{4,6},{6,7},{7,5},{5,3},{3,1},{1,0},{8,10},{10,12},{12... | collective-permute-start | bytes 786440 | tf_op jit(solution)/shard_map/ppermute | solution.py:325
  43.9 6.4 %collective-permute-start.14 = (bf16[32,4096]{1,0:T(8,128)(2,1)S(1)}, bf16[32,4096]{1,0:T(8,128)(2,1)S(1)}, u32[]{:S(2)}, u32[]{:S(2)}) collective-permute-start(bf16[32,4096]{1,0:T(8,128)(2,1)S(1)} %collective-permute-done.12.refs_5_), channel_id=1, source_target_pairs={{0,1},{2,0},{4,2},{6,4},{7,6},{5,7},{3,5},{1,3},{8,9},{10,8},{12,1... | collective-permute-start | bytes 786440 | tf_op jit(solution)/shard_map/ppermute | solution.py:328
  53.3 5.1 %collective-permute-start.15 = (bf16[16,4096]{1,0:T(8,128)(2,1)S(1)}, bf16[16,4096]{1,0:T(8,128)(2,1)S(1)}, u32[]{:S(2)}, u32[]{:S(2)}) collective-permute-start(bf16[16,4096]{1,0:T(8,128)(2,1)S(1)} %get-tuple-element.68), channel_id=1, source_target_pairs={{0,2},{2,4},{4,6},{6,7},{7,5},{5,3},{3,1},{1,0},{8,10},{10,12},{12... | collective-permute-start | bytes 393224 | tf_op jit(solution)/shard_map/ppermute | solution.py:325
  53.6 6.4 %collective-permute-start.19 = (bf16[16,4096]{1,0:T(8,128)(2,1)S(1)}, bf16[16,4096]{1,0:T(8,128)(2,1)S(1)}, u32[]{:S(2)}, u32[]{:S(2)}) collective-permute-start(bf16[16,4096]{1,0:T(8,128)(2,1)S(1)} %get-tuple-element.71), channel_id=1, source_target_pairs={{0,1},{2,0},{4,2},{6,4},{7,6},{5,7},{3,5},{1,3},{8,9},{10,8},{12,1... | collective-permute-start | bytes 393224 | tf_op jit(solution)/shard_map/ppermute | solution.py:328
  55.4 9.1 %collective-permute-start.22 = (bf16[16,4096]{1,0:T(8,128)(2,1)S(1)}, bf16[16,4096]{1,0:T(8,128)(2,1)S(1)}, u32[]{:S(2)}, u32[]{:S(2)}) collective-permute-start(bf16[16,4096]{1,0:T(8,128)(2,1)S(1)} %get-tuple-element.77), channel_id=1, source_target_pairs={{0,2},{2,4},{4,6},{6,7},{7,5},{5,3},{3,1},{1,0},{8,10},{10,12},{12... | collective-permute-start | bytes 393224 | tf_op jit(solution)/shard_map/ppermute | solution.py:325
  55.6 6.9 %collective-permute-start.23 = (bf16[16,4096]{1,0:T(8,128)(2,1)S(1)}, bf16[16,4096]{1,0:T(8,128)(2,1)S(1)}, u32[]{:S(2)}, u32[]{:S(2)}) collective-permute-start(bf16[16,4096]{1,0:T(8,128)(2,1)S(1)} %get-tuple-element.79), channel_id=1, source_target_pairs={{0,1},{2,0},{4,2},{6,4},{7,6},{5,7},{3,5},{1,3},{8,9},{10,8},{12,1... | collective-permute-start | bytes 393224 | tf_op jit(solution)/shard_map/ppermute | solution.py:328
  58.4 6.3 %collective-permute-start.16 = (bf16[16,4096]{1,0:T(8,128)(2,1)S(1)}, bf16[16,4096]{1,0:T(8,128)(2,1)S(1)}, u32[]{:S(2)}, u32[]{:S(2)}) collective-permute-start(bf16[16,4096]{1,0:T(8,128)(2,1)S(1)} %add_convert_fusion.10), channel_id=1, source_target_pairs={{0,2},{2,4},{4,6},{6,7},{7,5},{5,3},{3,1},{1,0},{8,10},{10,12},{12... | collective-permute-start | bytes 393224 | tf_op jit(solution)/shard_map/ppermute | solution.py:325
  60.0 6.6 %collective-permute-start.20 = (bf16[16,4096]{1,0:T(8,128)(2,1)S(1)}, bf16[16,4096]{1,0:T(8,128)(2,1)S(1)}, u32[]{:S(2)}, u32[]{:S(2)}) collective-permute-start(bf16[16,4096]{1,0:T(8,128)(2,1)S(1)} %add_convert_fusion.7), channel_id=1, source_target_pairs={{0,1},{2,0},{4,2},{6,4},{7,6},{5,7},{3,5},{1,3},{8,9},{10,8},{12,1... | collective-permute-start | bytes 393224 | tf_op jit(solution)/shard_map/ppermute | solution.py:328
  62.5 5.0 %collective-permute-start.25 = (bf16[16,4096]{1,0:T(8,128)(2,1)S(1)}, bf16[16,4096]{1,0:T(8,128)(2,1)S(1)}, u32[]{:S(2)}, u32[]{:S(2)}) collective-permute-start(bf16[16,4096]{1,0:T(8,128)(2,1)S(1)} %add_convert_fusion.4), channel_id=1, source_target_pairs={{0,1},{2,0},{4,2},{6,4},{7,6},{5,7},{3,5},{1,3},{8,9},{10,8},{12,1... | collective-permute-start | bytes 393224 | tf_op jit(solution)/shard_map/ppermute | solution.py:328
  64.5 5.2 %collective-permute-start.24 = (bf16[16,4096]{1,0:T(8,128)(2,1)S(1)}, bf16[16,4096]{1,0:T(8,128)(2,1)S(1)}, u32[]{:S(2)}, u32[]{:S(2)}) collective-permute-start(bf16[16,4096]{1,0:T(8,128)(2,1)S(1)} %add_convert_fusion.5), channel_id=1, source_target_pairs={{0,2},{2,4},{4,6},{6,7},{7,5},{5,3},{3,1},{1,0},{8,10},{10,12},{12... | collective-permute-start | bytes 393224 | tf_op jit(solution)/shard_map/ppermute | solution.py:325
  64.8 6.2 %collective-permute-start.17 = (bf16[16,4096]{1,0:T(8,128)(2,1)S(1)}, bf16[16,4096]{1,0:T(8,128)(2,1)S(1)}, u32[]{:S(2)}, u32[]{:S(2)}) collective-permute-start(bf16[16,4096]{1,0:T(8,128)(2,1)S(1)} %add_convert_fusion.9), channel_id=1, source_target_pairs={{0,2},{2,4},{4,6},{6,7},{7,5},{5,3},{3,1},{1,0},{8,10},{10,12},{12... | collective-permute-start | bytes 393224 | tf_op jit(solution)/shard_map/ppermute | solution.py:325
  66.6 11.7 %collective-permute-start.21 = (bf16[16,4096]{1,0:T(8,128)(2,1)S(1)}, bf16[16,4096]{1,0:T(8,128)(2,1)S(1)}, u32[]{:S(2)}, u32[]{:S(2)}) collective-permute-start(bf16[16,4096]{1,0:T(8,128)(2,1)S(1)} %add_convert_fusion.6), channel_id=1, source_target_pairs={{0,1},{2,0},{4,2},{6,4},{7,6},{5,7},{3,5},{1,3},{8,9},{10,8},{12,1... | collective-permute-start | bytes 393224 | tf_op jit(solution)/shard_map/ppermute | solution.py:328
  67.6 5.4 %collective-permute-start.27 = (bf16[16,4096]{1,0:T(8,128)(2,1)S(1)}, bf16[16,4096]{1,0:T(8,128)(2,1)S(1)}, u32[]{:S(2)}, u32[]{:S(2)}) collective-permute-start(bf16[16,4096]{1,0:T(8,128)(2,1)S(1)} %add_convert_fusion.2), channel_id=1, source_target_pairs={{0,1},{2,0},{4,2},{6,4},{7,6},{5,7},{3,5},{1,3},{8,9},{10,8},{12,1... | collective-permute-start | bytes 393224 | tf_op jit(solution)/shard_map/ppermute | solution.py:328
  69.8 5.0 %collective-permute-start.26 = (bf16[16,4096]{1,0:T(8,128)(2,1)S(1)}, bf16[16,4096]{1,0:T(8,128)(2,1)S(1)}, u32[]{:S(2)}, u32[]{:S(2)}) collective-permute-start(bf16[16,4096]{1,0:T(8,128)(2,1)S(1)} %add_convert_fusion.3), channel_id=1, source_target_pairs={{0,2},{2,4},{4,6},{6,7},{7,5},{5,3},{3,1},{1,0},{8,10},{10,12},{12... | collective-permute-start | bytes 393224 | tf_op jit(solution)/shard_map/ppermute | solution.py:325
  70.9 7.3 %collective-permute-start.18 = (bf16[16,4096]{1,0:T(8,128)(2,1)S(1)}, bf16[16,4096]{1,0:T(8,128)(2,1)S(1)}, u32[]{:S(2)}, u32[]{:S(2)}) collective-permute-start(bf16[16,4096]{1,0:T(8,128)(2,1)S(1)} %add_convert_fusion.8), channel_id=1, source_target_pairs={{0,2},{2,4},{4,6},{6,7},{7,5},{5,3},{3,1},{1,0},{8,10},{10,12},{12... | collective-permute-start | bytes 393224 | tf_op jit(solution)/shard_map/ppermute | solution.py:325
  73.1 5.0 %collective-permute-start.29 = (bf16[16,4096]{1,0:T(8,128)(2,1)S(1)}, bf16[16,4096]{1,0:T(8,128)(2,1)S(1)}, u32[]{:S(2)}, u32[]{:S(2)}) collective-permute-start(bf16[16,4096]{1,0:T(8,128)(2,1)S(1)} %add_convert_fusion), channel_id=1, source_target_pairs={{0,1},{2,0},{4,2},{6,4},{7,6},{5,7},{3,5},{1,3},{8,9},{10,8},{12,1... | collective-permute-start | bytes 393224 | tf_op jit(solution)/shard_map/ppermute | solution.py:328
  77.7 1.4 %collective-permute-start.28 = (bf16[16,4096]{1,0:T(8,128)(2,1)S(1)}, bf16[16,4096]{1,0:T(8,128)(2,1)S(1)}, u32[]{:S(2)}, u32[]{:S(2)}) collective-permute-start(bf16[16,4096]{1,0:T(8,128)(2,1)S(1)} %add_convert_fusion.1), channel_id=1, source_target_pairs={{0,8},{8,0},{1,9},{9,1},{2,10},{10,2},{3,11},{11,3},{4,12},{12,4},... | collective-permute-start | bytes 393224 | tf_op jit(solution)/shard_map/ppermute | solution.py:376
  78.1 1.3 %collective-permute-start.30 = (bf16[16,4096]{1,0:T(8,128)(2,1)S(1)}, bf16[16,4096]{1,0:T(8,128)(2,1)S(1)}, u32[]{:S(2)}, u32[]{:S(2)}) collective-permute-start(bf16[16,4096]{1,0:T(8,128)(2,1)S(1)} %collective-permute-done.29), channel_id=1, source_target_pairs={{0,8},{8,0},{1,9},{9,1},{2,10},{10,2},{3,11},{11,3},{4,12},{12,4},... | collective-permute-start | bytes 393224 | tf_op jit(solution)/shard_map/ppermute | solution.py:377

commit v3 on v2

--- a/solution.py
+++ b/solution.py
@@ -12,6 +12,7 @@
 TOK_DEV = 128
 CAP = 16
 BF = jnp.bfloat16
+WORK_COST = pl.CostEstimate(flops=3000000000, bytes_accessed=0, transcendentals=0)
 F32 = jnp.float32
 NT = (((1,), (1,)), ((), ()))
 TN = (((0,), (0,)), ((), ()))
@@ -241,7 +242,7 @@
             piece[:, k] = p[i * CAP : (i + 1) * CAP]
 
 
-def work(blocks, w_gate, w_up, w_down):
+def work(blocks, w_gate, w_up, w_down, flops):
     n = len(blocks)
     hid, width = w_gate.shape
     outs = [in_vmem(CAP, width)] * n + [in_vmem(n * CAP, hid)] * 3 + [in_vmem(n * CAP, width)] * 2
@@ -250,7 +251,7 @@
         in_specs=[IN_VMEM] * (n + 3),
         out_specs=[IN_VMEM] * len(outs),
         out_shape=outs,
-        cost_estimate=LIGHT,
+        cost_estimate=pl.CostEstimate(flops=flops, bytes_accessed=0, transcendentals=0),
         compiler_params=pltpu.CompilerParams(vmem_limit_bytes=4 << 20),
         name="work",
     )(*[held(x) for x in blocks], held(w_gate), held(w_up), held(w_down))
@@ -280,7 +281,7 @@
         out_specs=[pl.BlockSpec(memory_space=pl.ANY)] * 3,
         out_shape=[jax.ShapeDtypeStruct((hid, width), BF)] * 3,
         scratch_shapes=[pltpu.VMEM((3, hid, width), BF), pltpu.SemaphoreType.DMA((3,))],
-        cost_estimate=LIGHT,
+        cost_estimate=WORK_COST,
         compiler_params=pltpu.CompilerParams(vmem_limit_bytes=8 << 20),
         name="weight_grads",
     )(*[held(x) for part in zip(*saved) for x in part])
@@ -327,6 +328,11 @@
     def back(x):
         return lax.ppermute(x, "local", behind)
 
+    def cross(x, hops):
+        count = lax.axis_size("local")
+        pairs = [(i * count + a, (1 - i) * count + b) for i in (0, 1) for a, b in hops]
+        return lax.ppermute(x, ("node", "local"), pairs)
+
     near, other, select = pick(expert_ids.T, gate_probs.T, sample_ids, grad_out, layer_in)
     far = lax.ppermute(other, "node", swap)
 
@@ -334,8 +340,8 @@
     saved = []
     pieces = {}
 
-    def work_on(members):
-        outs, keep = work([rows[member] for member in members], *weights)
+    def work_on(members, flops=0):
+        outs, keep = work([rows[member] for member in members], *weights, flops)
         pieces.update(zip(members, outs))
         saved.append(keep)
         return keep[0]
@@ -349,14 +355,14 @@
         far_go, far_back = go(far_go), back(far_back)
         rows.update({(-s, 0): near_go, (s, 0): near_back, (-s, 1): far_go, (s, 1): far_back})
         if s == half - 2:
-            done = work_on(list(rows)[:-2])
-            near_go, near_back = after(near_go, done), after(near_back, done)
+            done = work_on(list(rows)[:-2], 3000000000)
+            far_go, far_back = after(far_go, done), after(far_back, done)
     near_go, near_back = together(near_go, near_back)
     far_go, far_back = together(far_go, far_back)
     near_go = go(near_go)
     far_back = back(far_back)
     rows.update({(half, 0): near_go, (half, 1): far_back})
-    work_on([member for member in rows if member not in pieces])
+    work_on([member for member in rows if member not in pieces], 0)
 
     def add(x, y):
         return (x.astype(F32) + y.astype(F32)).astype(BF)
@@ -372,10 +378,9 @@
             far_short, near_short = after(far_short, far_long), after(near_short, near_long)
     saved[0] = [after(saved[0][0], far_long, near_long), *saved[0][1:]]
     grad_gate, grad_up, grad_down = weight_grads(saved)
-    far_long, near_long = back(far_long), go(near_long)
-    first = lax.ppermute(after(add(pieces[0, 1], far_short), grad_gate), "node", swap)
-    second = lax.ppermute(far_long, "node", swap)
-    grad_in = place(select, pieces[0, 0], near_long, near_short, first, second)
+    far_long, near_long = cross(far_long, behind), go(near_long)
+    first = lax.ppermute(add(pieces[0, 1], far_short), "node", swap)
+    grad_in = place(select, pieces[0, 0], near_long, near_short, first, far_long)
     return (grad_in, grad_gate, grad_up, grad_down)
 
 

time: 80.9 us -> 80.1 us (level)
  starting transfers between devices: 32.9 us -> 28.6 us
  waiting for transfers between devices: 32.3 us -> 35.8 us
    ppermute x14, waiting for transfers between devices: 16.9 us -> 21.4 us  [go(): return lax.ppermute(x, 'local', ahead)]
    ppermute x14, starting transfers between devices: 6.49 us -> 3.94 us  [go(): return lax.ppermute(x, 'local', ahead)]
    ppermute x14 -> x13, starting transfers between devices: 25.6 us -> 24 us  [back(): return lax.ppermute(x, 'local', behind)]
    ppermute x14 -> x13, waiting for transfers between devices: 14.2 us -> 13.9 us  [back(): return lax.ppermute(x, 'local', behind)]
  transfers between devices with their start and end apart: 31 -> 30, of which waited for: 20 -> 20; matrix products, arithmetic and copies ran while one was open for 0% -> 0% of each run, Pallas kernels for 10% -> 10%
where the time goes in v3:
time: 80.1 us; the launch traced here: 80 us
  waiting for transfers between devices  35.8 us (45%)
  starting transfers between devices  28.6 us (36%)
  Pallas kernels  14.5 us (18%)
    ppermute x13, starting transfers between devices, back(): return lax.ppermute(x, 'local', behind)  24 us
    ppermute x14, waiting for transfers between devices, go(): return lax.ppermute(x, 'local', ahead)  21.4 us
    ppermute x13, waiting for transfers between devices, back(): return lax.ppermute(x, 'local', behind)  13.9 us
    pallas_call x2, Pallas kernels, work(): pl.pallas_call(functools.partial(work_kernel, n), in_specs=[IN_VMEM] * (n...  6.03 us
    ppermute x14, starting transfers between devices, go(): return lax.ppermute(x, 'local', ahead)  3.94 us
    pallas_call x1, Pallas kernels, weight_grads(): pl.pallas_call(functools.partial(weight_grads_kernel, n), in_specs=[IN_VM...  2.84 us
    pallas_call x1, Pallas kernels, load(): pl.pallas_call(functools.partial(load_kernel, n), in_specs=[pl.BlockSpec(...  2.38 us
    pallas_call x1, Pallas kernels, pick(): pl.pallas_call(pick_kernel, in_specs=[pl.BlockSpec(memory_space=pltpu.HBM...  1.91 us
  transfers between devices with their start and end apart: 30, of which 20 were waited for; matrix products, arithmetic and copies ran while one was open for 0% of the time, Pallas kernels for 10%

profile of v3, /device:TPU:0, one launch (start us, length us, event | category | flops | bytes accessed | tf_op | source)
XLA Modules:
  0.0 80.0 jit_solution(15981886930294655821)
XLA Ops:
  0.6 1.9 %pick.1 = (bf16[32,4096]{1,0:T(8,128)(2,1)S(1)}, bf16[32,4096]{1,0:T(8,128)(2,1)S(1)}, bf16[32,128]{1,0:T(8,128)(2,1)S(1)}) custom-call(s32[8,128]{1,0:T(8,128)} %bitcast.2, f32[8,128]{1,0:T(8,128)} %bitcast.3, s32[1,128]{1,0:T(1,128)} %samples_hbm.1, bf16[128,4096]{1,0:T(8,128)(2,1)} %grad_hbm.1, bf16[128,4096]{1,0:T(8,128)(2,1)} %in_hbm.1), custom_call_target="tpu_custom_call" | custom-call | tf_op jit(solution)/shard_map/pick/pallas_call | solution.py:186
  2.6 0.5 collective-permute-start
  3.1 2.6 %collective-permute-start.2 = (bf16[32,4096]{1,0:T(8,128)(2,1)S(1)}, bf16[32,4096]{1,0:T(8,128)(2,1)S(1)}, u32[]{:S(2)}, u32[]{:S(2)}) collective-permute-start(bf16[32,4096]{1,0:T(8,128)(2,1)S(1)} %get-tuple-element.51.refs_0_), channel_id=1, source_target_pairs={{0,1},{2,0},{4,2},{6,4},{7,6},{5,7},{3,5},{1,3},{8,9},{10,8},{12,1... | collective-permute-start | bytes 786440 | tf_op jit(solution)/shard_map/ppermute | solution.py:329
  5.6 0.1 collective-permute-start.1
  5.8 1.9 %collective-permute-start.4 = (bf16[32,4096]{1,0:T(8,128)(2,1)S(1)}, bf16[32,4096]{1,0:T(8,128)(2,1)S(1)}, u32[]{:S(2)}, u32[]{:S(2)}) collective-permute-start(bf16[32,4096]{1,0:T(8,128)(2,1)S(1)} %collective-permute-done.refs_1_), channel_id=1, source_target_pairs={{0,1},{2,0},{4,2},{6,4},{7,6},{5,7},{3,5},{1,3},{8,9},{10,8},{12,1... | collective-permute-start | bytes 786440 | tf_op jit(solution)/shard_map/ppermute | solution.py:329
  7.7 0.1 collective-permute-start.3
  7.8 5.0 %collective-permute-done.2.refs_3_ = bf16[32,4096]{1,0:T(8,128)(2,1)S(1)} collective-permute-done((bf16[32,4096]{1,0:T(8,128)(2,1)S(1)}, bf16[32,4096]{1,0:T(8,128)(2,1)S(1)}, u32[]{:S(2)}, u32[]{:S(2)}) %collective-permute-start.2) | collective-permute-done | bytes 262176 | tf_op jit(solution)/shard_map/ppermute | solution.py:329
  12.9 1.9 %collective-permute-start.6 = (bf16[32,4096]{1,0:T(8,128)(2,1)S(1)}, bf16[32,4096]{1,0:T(8,128)(2,1)S(1)}, u32[]{:S(2)}, u32[]{:S(2)}) collective-permute-start(bf16[32,4096]{1,0:T(8,128)(2,1)S(1)} %collective-permute-done.2.refs_3_), channel_id=1, source_target_pairs={{0,1},{2,0},{4,2},{6,4},{7,6},{5,7},{3,5},{1,3},{8,9},{10,8},{12,1... | collective-permute-start | bytes 786440 | tf_op jit(solution)/shard_map/ppermute | solution.py:329
  14.9 2.4 %load.1 = (bf16[192,4096]{1,0:T(8,128)(2,1)S(1)}, bf16[192,4096]{1,0:T(8,128)(2,1)S(1)}, bf16[192,4096]{1,0:T(8,128)(2,1)S(1)}) custom-call(bf16[192,4096]{1,0:T(8,128)(2,1)} %refs_0_.1, bf16[192,4096]{1,0:T(8,128)(2,1)} %refs_1_.1, bf16[192,4096]{1,0:T(8,128)(2,1)} %refs_2_.1), custom_call_target="tpu_custom_call" | custom-call | tf_op jit(solution)/shard_map/load/pallas_call | solution.py:207
  17.3 1.2 %collective-permute-done.4.refs_5_ = bf16[32,4096]{1,0:T(8,128)(2,1)S(1)} collective-permute-done((bf16[32,4096]{1,0:T(8,128)(2,1)S(1)}, bf16[32,4096]{1,0:T(8,128)(2,1)S(1)}, u32[]{:S(2)}, u32[]{:S(2)}) %collective-permute-start.4) | collective-permute-done | bytes 262176 | tf_op jit(solution)/shard_map/ppermute | solution.py:329
  18.5 1.9 %collective-permute-done.3.refs_4_ = bf16[32,4096]{1,0:T(8,128)(2,1)S(1)} collective-permute-done((bf16[32,4096]{1,0:T(8,128)(2,1)S(1)}, bf16[32,4096]{1,0:T(8,128)(2,1)S(1)}, u32[]{:S(2)}, u32[]{:S(2)}) %collective-permute-start.3) | collective-permute-done | bytes 262176 | tf_op jit(solution)/shard_map/ppermute | solution.py:326
  20.4 0.1 collective-permute-start.7
  20.5 1.9 %collective-permute-start.8 = (bf16[32,4096]{1,0:T(8,128)(2,1)S(1)}, bf16[32,4096]{1,0:T(8,128)(2,1)S(1)}, u32[]{:S(2)}, u32[]{:S(2)}) collective-permute-start(bf16[32,4096]{1,0:T(8,128)(2,1)S(1)} %collective-permute-done.4.refs_5_), channel_id=1, source_target_pairs={{0,1},{2,0},{4,2},{6,4},{7,6},{5,7},{3,5},{1,3},{8,9},{10,8},{12,1... | collective-permute-start | bytes 786440 | tf_op jit(solution)/shard_map/ppermute | solution.py:329
  22.4 1.7 %collective-permute-done.6.refs_7_ = bf16[32,4096]{1,0:T(8,128)(2,1)S(1)} collective-permute-done((bf16[32,4096]{1,0:T(8,128)(2,1)S(1)}, bf16[32,4096]{1,0:T(8,128)(2,1)S(1)}, u32[]{:S(2)}, u32[]{:S(2)}) %collective-permute-start.6) | collective-permute-done | bytes 262176 | tf_op jit(solution)/shard_map/ppermute | solution.py:329
  24.1 1.9 %collective-permute-start.10 = (bf16[32,4096]{1,0:T(8,128)(2,1)S(1)}, bf16[32,4096]{1,0:T(8,128)(2,1)S(1)}, u32[]{:S(2)}, u32[]{:S(2)}) collective-permute-start(bf16[32,4096]{1,0:T(8,128)(2,1)S(1)} %collective-permute-done.6.refs_7_), channel_id=1, source_target_pairs={{0,1},{2,0},{4,2},{6,4},{7,6},{5,7},{3,5},{1,3},{8,9},{10,8},{12,1... | collective-permute-start | bytes 786440 | tf_op jit(solution)/shard_map/ppermute | solution.py:329
  26.1 3.0 %work.2 = (bf16[16,4096]{1,0:T(8,128)(2,1)S(1)}, bf16[16,4096]{1,0:T(8,128)(2,1)S(1)}, bf16[16,4096]{1,0:T(8,128)(2,1)S(1)}, bf16[16,4096]{1,0:T(8,128)(2,1)S(1)...) custom-call(bf16[32,4096]{1,0:T(8,128)(2,1)S(1)} %get-tuple-element., ...), custom_call_target="tpu_custom_call" | custom-call | flops 3000000000 | tf_op jit(solution)/shard_map/work/pallas_call | solution.py:249
  29.2 0.5 collective-permute-done.8.refs_1_
  29.7 1.9 %collective-permute-done.7.refs_0_ = bf16[32,4096]{1,0:T(8,128)(2,1)S(1)} collective-permute-done((bf16[32,4096]{1,0:T(8,128)(2,1)S(1)}, bf16[32,4096]{1,0:T(8,128)(2,1)S(1)}, u32[]{:S(2)}, u32[]{:S(2)}) %collective-permute-start.7) | collective-permute-done | bytes 262176 | tf_op jit(solution)/shard_map/ppermute | solution.py:326
  31.8 1.9 %collective-permute-start.12 = (bf16[32,4096]{1,0:T(8,128)(2,1)S(1)}, bf16[32,4096]{1,0:T(8,128)(2,1)S(1)}, u32[]{:S(2)}, u32[]{:S(2)}) collective-permute-start(bf16[32,4096]{1,0:T(8,128)(2,1)S(1)} %collective-permute-done.8.refs_1_), channel_id=1, source_target_pairs={{0,1},{2,0},{4,2},{6,4},{7,6},{5,7},{3,5},{1,3},{8,9},{10,8},{12,1... | collective-permute-start | bytes 786440 | tf_op jit(solution)/shard_map/ppermute | solution.py:329
  33.7 1.7 %collective-permute-done.10.refs_3_ = bf16[32,4096]{1,0:T(8,128)(2,1)S(1)} collective-permute-done((bf16[32,4096]{1,0:T(8,128)(2,1)S(1)}, bf16[32,4096]{1,0:T(8,128)(2,1)S(1)}, u32[]{:S(2)}, u32[]{:S(2)}) %collective-permute-start.10) | collective-permute-done | bytes 262176 | tf_op jit(solution)/shard_map/ppermute | solution.py:329
  35.3 1.9 %collective-permute-done.9.refs_2_ = bf16[32,4096]{1,0:T(8,128)(2,1)S(1)} collective-permute-done((bf16[32,4096]{1,0:T(8,128)(2,1)S(1)}, bf16[32,4096]{1,0:T(8,128)(2,1)S(1)}, u32[]{:S(2)}, u32[]{:S(2)}) %collective-permute-start.9) | collective-permute-done | bytes 262176 | tf_op jit(solution)/shard_map/ppermute | solution.py:326
  37.4 5.5 %collective-permute-done.11.refs_4_ = bf16[32,4096]{1,0:T(8,128)(2,1)S(1)} collective-permute-done((bf16[32,4096]{1,0:T(8,128)(2,1)S(1)}, bf16[32,4096]{1,0:T(8,128)(2,1)S(1)}, u32[]{:S(2)}, u32[]{:S(2)}) %collective-permute-start.11) | collective-permute-done | bytes 262176 | tf_op jit(solution)/shard_map/ppermute | solution.py:326
  42.9 1.6 %collective-permute-start.14 = (bf16[32,4096]{1,0:T(8,128)(2,1)S(1)}, bf16[32,4096]{1,0:T(8,128)(2,1)S(1)}, u32[]{:S(2)}, u32[]{:S(2)}) collective-permute-start(bf16[32,4096]{1,0:T(8,128)(2,1)S(1)} %collective-permute-done.12.refs_5_), channel_id=1, source_target_pairs={{0,1},{2,0},{4,2},{6,4},{7,6},{5,7},{3,5},{1,3},{8,9},{10,8},{12,1... | collective-permute-start | bytes 786440 | tf_op jit(solution)/shard_map/ppermute | solution.py:329
  44.5 3.3 %collective-permute-done.13.refs_6_ = bf16[32,4096]{1,0:T(8,128)(2,1)S(1)} collective-permute-done((bf16[32,4096]{1,0:T(8,128)(2,1)S(1)}, bf16[32,4096]{1,0:T(8,128)(2,1)S(1)}, u32[]{:S(2)}, u32[]{:S(2)}) %collective-permute-start.13) | collective-permute-done | bytes 262176 | tf_op jit(solution)/shard_map/ppermute | solution.py:326
  47.7 1.9 %collective-permute-done.14.refs_7_ = bf16[32,4096]{1,0:T(8,128)(2,1)S(1)} collective-permute-done((bf16[32,4096]{1,0:T(8,128)(2,1)S(1)}, bf16[32,4096]{1,0:T(8,128)(2,1)S(1)}, u32[]{:S(2)}, u32[]{:S(2)}) %collective-permute-start.14) | collective-permute-done | bytes 262176 | tf_op jit(solution)/shard_map/ppermute | solution.py:329
  49.7 3.0 %work.3 = (bf16[16,4096]{1,0:T(8,128)(2,1)S(1)}, bf16[16,4096]{1,0:T(8,128)(2,1)S(1)}, bf16[16,4096]{1,0:T(8,128)(2,1)S(1)}, bf16[16,4096]{1,0:T(8,128)(2,1)S(1)...) custom-call(bf16[32,4096]{1,0:T(8,128)(2,1)S(1)} %collective-permute, ...), custom_call_target="tpu_custom_call" | custom-call | tf_op jit(solution)/shard_map/work/pallas_call | solution.py:249
  52.7 0.6 collective-permute-start.15
  53.3 1.5 %collective-permute-start.19 = (bf16[16,4096]{1,0:T(8,128)(2,1)S(1)}, bf16[16,4096]{1,0:T(8,128)(2,1)S(1)}, u32[]{:S(2)}, u32[]{:S(2)}) collective-permute-start(bf16[16,4096]{1,0:T(8,128)(2,1)S(1)} %get-tuple-element.70), channel_id=1, source_target_pairs={{0,1},{2,0},{4,2},{6,4},{7,6},{5,7},{3,5},{1,3},{8,9},{10,8},{12,1... | collective-permute-start | bytes 393224 | tf_op jit(solution)/shard_map/ppermute | solution.py:329
  54.8 0.5 collective-permute-start.22
  55.3 1.5 %collective-permute-start.23 = (bf16[16,4096]{1,0:T(8,128)(2,1)S(1)}, bf16[16,4096]{1,0:T(8,128)(2,1)S(1)}, u32[]{:S(2)}, u32[]{:S(2)}) collective-permute-start(bf16[16,4096]{1,0:T(8,128)(2,1)S(1)} %get-tuple-element.78), channel_id=1, source_target_pairs={{0,1},{2,0},{4,2},{6,4},{7,6},{5,7},{3,5},{1,3},{8,9},{10,8},{12,1... | collective-permute-start | bytes 393224 | tf_op jit(solution)/shard_map/ppermute | solution.py:329
  56.8 1.8 %collective-permute-done.15 = bf16[16,4096]{1,0:T(8,128)(2,1)S(1)} collective-permute-done((bf16[16,4096]{1,0:T(8,128)(2,1)S(1)}, bf16[16,4096]{1,0:T(8,128)(2,1)S(1)}, u32[]{:S(2)}, u32[]{:S(2)}) %collective-permute-start.15) | collective-permute-done | bytes 131104 | tf_op jit(solution)/shard_map/ppermute | solution.py:326
  58.8 2.1 %collective-permute-start.20 = (bf16[16,4096]{1,0:T(8,128)(2,1)S(1)}, bf16[16,4096]{1,0:T(8,128)(2,1)S(1)}, u32[]{:S(2)}, u32[]{:S(2)}) collective-permute-start(bf16[16,4096]{1,0:T(8,128)(2,1)S(1)} %add_convert_fusion.7), channel_id=1, source_target_pairs={{0,1},{2,0},{4,2},{6,4},{7,6},{5,7},{3,5},{1,3},{8,9},{10,8},{12,1... | collective-permute-start | bytes 393224 | tf_op jit(solution)/shard_map/ppermute | solution.py:329
  60.9 0.8 collective-permute-done.23
  61.7 2.0 %collective-permute-start.25 = (bf16[16,4096]{1,0:T(8,128)(2,1)S(1)}, bf16[16,4096]{1,0:T(8,128)(2,1)S(1)}, u32[]{:S(2)}, u32[]{:S(2)}) collective-permute-start(bf16[16,4096]{1,0:T(8,128)(2,1)S(1)} %add_convert_fusion.4), channel_id=1, source_target_pairs={{0,1},{2,0},{4,2},{6,4},{7,6},{5,7},{3,5},{1,3},{8,9},{10,8},{12,1... | collective-permute-start | bytes 393224 | tf_op jit(solution)/shard_map/ppermute | solution.py:329
  63.8 0.1 collective-permute-start.24
  63.9 1.0 %collective-permute-done.16 = bf16[16,4096]{1,0:T(8,128)(2,1)S(1)} collective-permute-done((bf16[16,4096]{1,0:T(8,128)(2,1)S(1)}, bf16[16,4096]{1,0:T(8,128)(2,1)S(1)}, u32[]{:S(2)}, u32[]{:S(2)}) %collective-permute-start.16) | collective-permute-done | bytes 131104 | tf_op jit(solution)/shard_map/ppermute | solution.py:326
  64.9 1.1 %collective-permute-start.17 = (bf16[16,4096]{1,0:T(8,128)(2,1)S(1)}, bf16[16,4096]{1,0:T(8,128)(2,1)S(1)}, u32[]{:S(2)}, u32[]{:S(2)}) collective-permute-start(bf16[16,4096]{1,0:T(8,128)(2,1)S(1)} %add_convert_fusion.9), channel_id=1, source_target_pairs={{0,2},{2,4},{4,6},{6,7},{7,5},{5,3},{3,1},{1,0},{8,10},{10,12},{12... | collective-permute-start | bytes 393224 | tf_op jit(solution)/shard_map/ppermute | solution.py:326
  66.0 1.4 %collective-permute-start.21 = (bf16[16,4096]{1,0:T(8,128)(2,1)S(1)}, bf16[16,4096]{1,0:T(8,128)(2,1)S(1)}, u32[]{:S(2)}, u32[]{:S(2)}) collective-permute-start(bf16[16,4096]{1,0:T(8,128)(2,1)S(1)} %add_convert_fusion.6), channel_id=1, source_target_pairs={{0,1},{2,0},{4,2},{6,4},{7,6},{5,7},{3,5},{1,3},{8,9},{10,8},{12,1... | collective-permute-start | bytes 393224 | tf_op jit(solution)/shard_map/ppermute | solution.py:329
  67.4 0.7 collective-permute-done.25
  68.1 1.8 %collective-permute-start.28 = (bf16[16,4096]{1,0:T(8,128)(2,1)S(1)}, bf16[16,4096]{1,0:T(8,128)(2,1)S(1)}, u32[]{:S(2)}, u32[]{:S(2)}) collective-permute-start(bf16[16,4096]{1,0:T(8,128)(2,1)S(1)} %add_convert_fusion.2), channel_id=1, source_target_pairs={{0,1},{2,0},{4,2},{6,4},{7,6},{5,7},{3,5},{1,3},{8,9},{10,8},{12,1... | collective-permute-start | bytes 393224 | tf_op jit(solution)/shard_map/ppermute | solution.py:329
  70.0 0.2 collective-permute-done.24
  70.3 1.9 %collective-permute-done.17 = bf16[16,4096]{1,0:T(8,128)(2,1)S(1)} collective-permute-done((bf16[16,4096]{1,0:T(8,128)(2,1)S(1)}, bf16[16,4096]{1,0:T(8,128)(2,1)S(1)}, u32[]{:S(2)}, u32[]{:S(2)}) %collective-permute-start.17) | collective-permute-done | bytes 131104 | tf_op jit(solution)/shard_map/ppermute | solution.py:326
  72.2 0.6 collective-permute-start.18
  72.8 0.4 collective-permute-done.28
  73.3 2.0 %collective-permute-done.26 = bf16[16,4096]{1,0:T(8,128)(2,1)S(1)} collective-permute-done((bf16[16,4096]{1,0:T(8,128)(2,1)S(1)}, bf16[16,4096]{1,0:T(8,128)(2,1)S(1)}, u32[]{:S(2)}, u32[]{:S(2)}) %collective-permute-start.26) | collective-permute-done | bytes 131104 | tf_op jit(solution)/shard_map/ppermute | solution.py:326
  75.3 2.8 %weight_grads.1 = (bf16[192,4096]{1,0:T(8,128)(2,1)}, bf16[192,4096]{1,0:T(8,128)(2,1)}, bf16[192,4096]{1,0:T(8,128)(2,1)}) custom-call(bf16[128,192]{1,0:T(8,128)(2,1)S(1)} %get-tuple-element.83.refs_0_, bf16[128,192]{1,0:T(8,128)(2,1)S(1)} %get-tuple-element.84.refs_1_, bf16[128,192]{1,0:T(8,128)(2,1)S(1)} %get-tuple-element.85.refs_2_, ...), custom_call_target="tpu_custom_call" | custom-call | flops 3000000000 | tf_op jit(solution)/shard_map/weight_grads/pallas_call | solution.py:278
  78.2 0.4 collective-permute-done.29.second_ref
  78.6 1.3 %place.1 = bf16[128,4096]{1,0:T(8,128)(2,1)} custom-call(bf16[32,128]{1,0:T(8,128)(2,1)S(1)} %get-tuple-element.50.select_ref, bf16[16,4096]{1,0:T(8,128)(2,1)S(1)} %get-tuple-element.56.own_ref, bf16[16,4096]{1,0:T(8,128)(2,1)S(1)} %collective-permute-done.18.ahead_ref, bf16[16,4096]{1,0:T(8,128)(2,1)S(1)} %collective-permute-done.21.behind_ref, ...), custom_call_target="tpu_custom_call" | custom-call | tf_op jit(solution)/shard_map/place/pallas_call | solution.py:309
  (29 shorter events, 1.3 us)
Async XLA Ops:
  2.6 3.2 %collective-permute-start = (bf16[32,4096]{1,0:T(8,128)(2,1)S(1)}, bf16[32,4096]{1,0:T(8,128)(2,1)S(1)}, u32[]{:S(2)}, u32[]{:S(2)}) collective-permute-start(bf16[32,4096]{1,0:T(8,128)(2,1)S(1)} %get-tuple-element.52), channel_id=1, source_target_pairs={{0,8},{8,0},{1,9},{9,1},{2,10},{10,2},{3,11},{11,3},{4,12},{12,4},... | collective-permute-start | bytes 786440 | tf_op jit(solution)/shard_map/ppermute | solution.py:337
  3.1 9.8 %collective-permute-start.2 = (bf16[32,4096]{1,0:T(8,128)(2,1)S(1)}, bf16[32,4096]{1,0:T(8,128)(2,1)S(1)}, u32[]{:S(2)}, u32[]{:S(2)}) collective-permute-start(bf16[32,4096]{1,0:T(8,128)(2,1)S(1)} %get-tuple-element.51.refs_0_), channel_id=1, source_target_pairs={{0,1},{2,0},{4,2},{6,4},{7,6},{5,7},{3,5},{1,3},{8,9},{10,8},{12,1... | collective-permute-start | bytes 786440 | tf_op jit(solution)/shard_map/ppermute | solution.py:329
  5.6 9.1 %collective-permute-start.1 = (bf16[32,4096]{1,0:T(8,128)(2,1)S(1)}, bf16[32,4096]{1,0:T(8,128)(2,1)S(1)}, u32[]{:S(2)}, u32[]{:S(2)}) collective-permute-start(bf16[32,4096]{1,0:T(8,128)(2,1)S(1)} %get-tuple-element.51.refs_0_), channel_id=1, source_target_pairs={{0,2},{2,4},{4,6},{6,7},{7,5},{5,3},{3,1},{1,0},{8,10},{10,12},{12... | collective-permute-start | bytes 786440 | tf_op jit(solution)/shard_map/ppermute | solution.py:326
  5.8 12.7 %collective-permute-start.4 = (bf16[32,4096]{1,0:T(8,128)(2,1)S(1)}, bf16[32,4096]{1,0:T(8,128)(2,1)S(1)}, u32[]{:S(2)}, u32[]{:S(2)}) collective-permute-start(bf16[32,4096]{1,0:T(8,128)(2,1)S(1)} %collective-permute-done.refs_1_), channel_id=1, source_target_pairs={{0,1},{2,0},{4,2},{6,4},{7,6},{5,7},{3,5},{1,3},{8,9},{10,8},{12,1... | collective-permute-start | bytes 786440 | tf_op jit(solution)/shard_map/ppermute | solution.py:329
  7.7 12.7 %collective-permute-start.3 = (bf16[32,4096]{1,0:T(8,128)(2,1)S(1)}, bf16[32,4096]{1,0:T(8,128)(2,1)S(1)}, u32[]{:S(2)}, u32[]{:S(2)}) collective-permute-start(bf16[32,4096]{1,0:T(8,128)(2,1)S(1)} %collective-permute-done.refs_1_), channel_id=1, source_target_pairs={{0,2},{2,4},{4,6},{6,7},{7,5},{5,3},{3,1},{1,0},{8,10},{10,12},{12... | collective-permute-start | bytes 786440 | tf_op jit(solution)/shard_map/ppermute | solution.py:326
  12.9 11.2 %collective-permute-start.6 = (bf16[32,4096]{1,0:T(8,128)(2,1)S(1)}, bf16[32,4096]{1,0:T(8,128)(2,1)S(1)}, u32[]{:S(2)}, u32[]{:S(2)}) collective-permute-start(bf16[32,4096]{1,0:T(8,128)(2,1)S(1)} %collective-permute-done.2.refs_3_), channel_id=1, source_target_pairs={{0,1},{2,0},{4,2},{6,4},{7,6},{5,7},{3,5},{1,3},{8,9},{10,8},{12,1... | collective-permute-start | bytes 786440 | tf_op jit(solution)/shard_map/ppermute | solution.py:329
  14.8 11.2 %collective-permute-start.5 = (bf16[32,4096]{1,0:T(8,128)(2,1)S(1)}, bf16[32,4096]{1,0:T(8,128)(2,1)S(1)}, u32[]{:S(2)}, u32[]{:S(2)}) collective-permute-start(bf16[32,4096]{1,0:T(8,128)(2,1)S(1)} %collective-permute-done.1.refs_2_), channel_id=1, source_target_pairs={{0,2},{2,4},{4,6},{6,7},{7,5},{5,3},{3,1},{1,0},{8,10},{10,12},{12... | collective-permute-start | bytes 786440 | tf_op jit(solution)/shard_map/ppermute | solution.py:326
  20.4 11.2 %collective-permute-start.7 = (bf16[32,4096]{1,0:T(8,128)(2,1)S(1)}, bf16[32,4096]{1,0:T(8,128)(2,1)S(1)}, u32[]{:S(2)}, u32[]{:S(2)}) collective-permute-start(bf16[32,4096]{1,0:T(8,128)(2,1)S(1)} %collective-permute-done.3.refs_4_), channel_id=1, source_target_pairs={{0,2},{2,4},{4,6},{6,7},{7,5},{5,3},{3,1},{1,0},{8,10},{10,12},{12... | collective-permute-start | bytes 786440 | tf_op jit(solution)/shard_map/ppermute | solution.py:326
  20.5 9.2 %collective-permute-start.8 = (bf16[32,4096]{1,0:T(8,128)(2,1)S(1)}, bf16[32,4096]{1,0:T(8,128)(2,1)S(1)}, u32[]{:S(2)}, u32[]{:S(2)}) collective-permute-start(bf16[32,4096]{1,0:T(8,128)(2,1)S(1)} %collective-permute-done.4.refs_5_), channel_id=1, source_target_pairs={{0,1},{2,0},{4,2},{6,4},{7,6},{5,7},{3,5},{1,3},{8,9},{10,8},{12,1... | collective-permute-start | bytes 786440 | tf_op jit(solution)/shard_map/ppermute | solution.py:329
  24.1 11.2 %collective-permute-start.10 = (bf16[32,4096]{1,0:T(8,128)(2,1)S(1)}, bf16[32,4096]{1,0:T(8,128)(2,1)S(1)}, u32[]{:S(2)}, u32[]{:S(2)}) collective-permute-start(bf16[32,4096]{1,0:T(8,128)(2,1)S(1)} %collective-permute-done.6.refs_7_), channel_id=1, source_target_pairs={{0,1},{2,0},{4,2},{6,4},{7,6},{5,7},{3,5},{1,3},{8,9},{10,8},{12,1... | collective-permute-start | bytes 786440 | tf_op jit(solution)/shard_map/ppermute | solution.py:329
  26.0 11.2 %collective-permute-start.9 = (bf16[32,4096]{1,0:T(8,128)(2,1)S(1)}, bf16[32,4096]{1,0:T(8,128)(2,1)S(1)}, u32[]{:S(2)}, u32[]{:S(2)}) collective-permute-start(bf16[32,4096]{1,0:T(8,128)(2,1)S(1)} %collective-permute-done.5.refs_6_), channel_id=1, source_target_pairs={{0,2},{2,4},{4,6},{6,7},{7,5},{5,3},{3,1},{1,0},{8,10},{10,12},{12... | collective-permute-start | bytes 786440 | tf_op jit(solution)/shard_map/ppermute | solution.py:326
  31.7 11.2 %collective-permute-start.11 = (bf16[32,4096]{1,0:T(8,128)(2,1)S(1)}, bf16[32,4096]{1,0:T(8,128)(2,1)S(1)}, u32[]{:S(2)}, u32[]{:S(2)}) collective-permute-start(bf16[32,4096]{1,0:T(8,128)(2,1)S(1)} %collective-permute-done.7.refs_0_), channel_id=1, source_target_pairs={{0,2},{2,4},{4,6},{6,7},{7,5},{5,3},{3,1},{1,0},{8,10},{10,12},{12... | collective-permute-start | bytes 786440 | tf_op jit(solution)/shard_map/ppermute | solution.py:326
  31.8 11.1 %collective-permute-start.12 = (bf16[32,4096]{1,0:T(8,128)(2,1)S(1)}, bf16[32,4096]{1,0:T(8,128)(2,1)S(1)}, u32[]{:S(2)}, u32[]{:S(2)}) collective-permute-start(bf16[32,4096]{1,0:T(8,128)(2,1)S(1)} %collective-permute-done.8.refs_1_), channel_id=1, source_target_pairs={{0,1},{2,0},{4,2},{6,4},{7,6},{5,7},{3,5},{1,3},{8,9},{10,8},{12,1... | collective-permute-start | bytes 786440 | tf_op jit(solution)/shard_map/ppermute | solution.py:329
  37.3 10.5 %collective-permute-start.13 = (bf16[32,4096]{1,0:T(8,128)(2,1)S(1)}, bf16[32,4096]{1,0:T(8,128)(2,1)S(1)}, u32[]{:S(2)}, u32[]{:S(2)}) collective-permute-start(bf16[32,4096]{1,0:T(8,128)(2,1)S(1)} %collective-permute-done.9.refs_2_), channel_id=1, source_target_pairs={{0,2},{2,4},{4,6},{6,7},{7,5},{5,3},{3,1},{1,0},{8,10},{10,12},{12... | collective-permute-start | bytes 786440 | tf_op jit(solution)/shard_map/ppermute | solution.py:326
  42.9 6.8 %collective-permute-start.14 = (bf16[32,4096]{1,0:T(8,128)(2,1)S(1)}, bf16[32,4096]{1,0:T(8,128)(2,1)S(1)}, u32[]{:S(2)}, u32[]{:S(2)}) collective-permute-start(bf16[32,4096]{1,0:T(8,128)(2,1)S(1)} %collective-permute-done.12.refs_5_), channel_id=1, source_target_pairs={{0,1},{2,0},{4,2},{6,4},{7,6},{5,7},{3,5},{1,3},{8,9},{10,8},{12,1... | collective-permute-start | bytes 786440 | tf_op jit(solution)/shard_map/ppermute | solution.py:329
  52.7 5.9 %collective-permute-start.15 = (bf16[16,4096]{1,0:T(8,128)(2,1)S(1)}, bf16[16,4096]{1,0:T(8,128)(2,1)S(1)}, u32[]{:S(2)}, u32[]{:S(2)}) collective-permute-start(bf16[16,4096]{1,0:T(8,128)(2,1)S(1)} %get-tuple-element.67), channel_id=1, source_target_pairs={{0,2},{2,4},{4,6},{6,7},{7,5},{5,3},{3,1},{1,0},{8,10},{10,12},{12... | collective-permute-start | bytes 393224 | tf_op jit(solution)/shard_map/ppermute | solution.py:326
  53.3 5.5 %collective-permute-start.19 = (bf16[16,4096]{1,0:T(8,128)(2,1)S(1)}, bf16[16,4096]{1,0:T(8,128)(2,1)S(1)}, u32[]{:S(2)}, u32[]{:S(2)}) collective-permute-start(bf16[16,4096]{1,0:T(8,128)(2,1)S(1)} %get-tuple-element.70), channel_id=1, source_target_pairs={{0,1},{2,0},{4,2},{6,4},{7,6},{5,7},{3,5},{1,3},{8,9},{10,8},{12,1... | collective-permute-start | bytes 393224 | tf_op jit(solution)/shard_map/ppermute | solution.py:329
  54.8 9.0 %collective-permute-start.22 = (bf16[16,4096]{1,0:T(8,128)(2,1)S(1)}, bf16[16,4096]{1,0:T(8,128)(2,1)S(1)}, u32[]{:S(2)}, u32[]{:S(2)}) collective-permute-start(bf16[16,4096]{1,0:T(8,128)(2,1)S(1)} %get-tuple-element.76), channel_id=1, source_target_pairs={{0,2},{2,4},{4,6},{6,7},{7,5},{5,3},{3,1},{1,0},{8,10},{10,12},{12... | collective-permute-start | bytes 393224 | tf_op jit(solution)/shard_map/ppermute | solution.py:326
  55.3 6.4 %collective-permute-start.23 = (bf16[16,4096]{1,0:T(8,128)(2,1)S(1)}, bf16[16,4096]{1,0:T(8,128)(2,1)S(1)}, u32[]{:S(2)}, u32[]{:S(2)}) collective-permute-start(bf16[16,4096]{1,0:T(8,128)(2,1)S(1)} %get-tuple-element.78), channel_id=1, source_target_pairs={{0,1},{2,0},{4,2},{6,4},{7,6},{5,7},{3,5},{1,3},{8,9},{10,8},{12,1... | collective-permute-start | bytes 393224 | tf_op jit(solution)/shard_map/ppermute | solution.py:329
  58.6 6.2 %collective-permute-start.16 = (bf16[16,4096]{1,0:T(8,128)(2,1)S(1)}, bf16[16,4096]{1,0:T(8,128)(2,1)S(1)}, u32[]{:S(2)}, u32[]{:S(2)}) collective-permute-start(bf16[16,4096]{1,0:T(8,128)(2,1)S(1)} %add_convert_fusion.10), channel_id=1, source_target_pairs={{0,2},{2,4},{4,6},{6,7},{7,5},{5,3},{3,1},{1,0},{8,10},{10,12},{12... | collective-permute-start | bytes 393224 | tf_op jit(solution)/shard_map/ppermute | solution.py:326
  58.8 7.2 %collective-permute-start.20 = (bf16[16,4096]{1,0:T(8,128)(2,1)S(1)}, bf16[16,4096]{1,0:T(8,128)(2,1)S(1)}, u32[]{:S(2)}, u32[]{:S(2)}) collective-permute-start(bf16[16,4096]{1,0:T(8,128)(2,1)S(1)} %add_convert_fusion.7), channel_id=1, source_target_pairs={{0,1},{2,0},{4,2},{6,4},{7,6},{5,7},{3,5},{1,3},{8,9},{10,8},{12,1... | collective-permute-start | bytes 393224 | tf_op jit(solution)/shard_map/ppermute | solution.py:329
  61.7 6.4 %collective-permute-start.25 = (bf16[16,4096]{1,0:T(8,128)(2,1)S(1)}, bf16[16,4096]{1,0:T(8,128)(2,1)S(1)}, u32[]{:S(2)}, u32[]{:S(2)}) collective-permute-start(bf16[16,4096]{1,0:T(8,128)(2,1)S(1)} %add_convert_fusion.4), channel_id=1, source_target_pairs={{0,1},{2,0},{4,2},{6,4},{7,6},{5,7},{3,5},{1,3},{8,9},{10,8},{12,1... | collective-permute-start | bytes 393224 | tf_op jit(solution)/shard_map/ppermute | solution.py:329
  63.8 6.4 %collective-permute-start.24 = (bf16[16,4096]{1,0:T(8,128)(2,1)S(1)}, bf16[16,4096]{1,0:T(8,128)(2,1)S(1)}, u32[]{:S(2)}, u32[]{:S(2)}) collective-permute-start(bf16[16,4096]{1,0:T(8,128)(2,1)S(1)} %add_convert_fusion.5), channel_id=1, source_target_pairs={{0,2},{2,4},{4,6},{6,7},{7,5},{5,3},{3,1},{1,0},{8,10},{10,12},{12... | collective-permute-start | bytes 393224 | tf_op jit(solution)/shard_map/ppermute | solution.py:326
  64.9 7.3 %collective-permute-start.17 = (bf16[16,4096]{1,0:T(8,128)(2,1)S(1)}, bf16[16,4096]{1,0:T(8,128)(2,1)S(1)}, u32[]{:S(2)}, u32[]{:S(2)}) collective-permute-start(bf16[16,4096]{1,0:T(8,128)(2,1)S(1)} %add_convert_fusion.9), channel_id=1, source_target_pairs={{0,2},{2,4},{4,6},{6,7},{7,5},{5,3},{3,1},{1,0},{8,10},{10,12},{12... | collective-permute-start | bytes 393224 | tf_op jit(solution)/shard_map/ppermute | solution.py:326
  66.0 12.2 %collective-permute-start.21 = (bf16[16,4096]{1,0:T(8,128)(2,1)S(1)}, bf16[16,4096]{1,0:T(8,128)(2,1)S(1)}, u32[]{:S(2)}, u32[]{:S(2)}) collective-permute-start(bf16[16,4096]{1,0:T(8,128)(2,1)S(1)} %add_convert_fusion.6), channel_id=1, source_target_pairs={{0,1},{2,0},{4,2},{6,4},{7,6},{5,7},{3,5},{1,3},{8,9},{10,8},{12,1... | collective-permute-start | bytes 393224 | tf_op jit(solution)/shard_map/ppermute | solution.py:329
  68.1 5.0 %collective-permute-start.28 = (bf16[16,4096]{1,0:T(8,128)(2,1)S(1)}, bf16[16,4096]{1,0:T(8,128)(2,1)S(1)}, u32[]{:S(2)}, u32[]{:S(2)}) collective-permute-start(bf16[16,4096]{1,0:T(8,128)(2,1)S(1)} %add_convert_fusion.2), channel_id=1, source_target_pairs={{0,1},{2,0},{4,2},{6,4},{7,6},{5,7},{3,5},{1,3},{8,9},{10,8},{12,1... | collective-permute-start | bytes 393224 | tf_op jit(solution)/shard_map/ppermute | solution.py:329
  70.2 5.0 %collective-permute-start.26 = (bf16[16,4096]{1,0:T(8,128)(2,1)S(1)}, bf16[16,4096]{1,0:T(8,128)(2,1)S(1)}, u32[]{:S(2)}, u32[]{:S(2)}) collective-permute-start(bf16[16,4096]{1,0:T(8,128)(2,1)S(1)} %add_convert_fusion.3), channel_id=1, source_target_pairs={{0,2},{2,4},{4,6},{6,7},{7,5},{5,3},{3,1},{1,0},{8,10},{10,12},{12... | collective-permute-start | bytes 393224 | tf_op jit(solution)/shard_map/ppermute | solution.py:326
  72.2 6.0 %collective-permute-start.18 = (bf16[16,4096]{1,0:T(8,128)(2,1)S(1)}, bf16[16,4096]{1,0:T(8,128)(2,1)S(1)}, u32[]{:S(2)}, u32[]{:S(2)}) collective-permute-start(bf16[16,4096]{1,0:T(8,128)(2,1)S(1)} %add_convert_fusion.8), channel_id=1, source_target_pairs={{0,2},{2,4},{4,6},{6,7},{7,5},{5,3},{3,1},{1,0},{8,10},{10,12},{12... | collective-permute-start | bytes 393224 | tf_op jit(solution)/shard_map/ppermute | solution.py:326
  73.2 5.4 %collective-permute-start.29 = (bf16[16,4096]{1,0:T(8,128)(2,1)S(1)}, bf16[16,4096]{1,0:T(8,128)(2,1)S(1)}, u32[]{:S(2)}, u32[]{:S(2)}) collective-permute-start(bf16[16,4096]{1,0:T(8,128)(2,1)S(1)} %add_convert_fusion), channel_id=1, source_target_pairs={{0,9},{2,8},{4,10},{6,12},{7,14},{5,15},{3,13},{1,11},{8,1},{10,0}... | collective-permute-start | bytes 393224 | tf_op jit(solution)/shard_map/ppermute | solution.py:334
  75.3 3.0 %collective-permute-start.27 = (bf16[16,4096]{1,0:T(8,128)(2,1)S(1)}, bf16[16,4096]{1,0:T(8,128)(2,1)S(1)}, u32[]{:S(2)}, u32[]{:S(2)}) collective-permute-start(bf16[16,4096]{1,0:T(8,128)(2,1)S(1)} %add_convert_fusion.1), channel_id=1, source_target_pairs={{0,8},{8,0},{1,9},{9,1},{2,10},{10,2},{3,11},{11,3},{4,12},{12,4},... | collective-permute-start | bytes 393224 | tf_op jit(solution)/shard_map/ppermute | solution.py:382

commit v4 on v3

--- a/solution.py
+++ b/solution.py
@@ -359,9 +359,9 @@
             far_go, far_back = after(far_go, done), after(far_back, done)
     near_go, near_back = together(near_go, near_back)
     far_go, far_back = together(far_go, far_back)
-    near_go = go(near_go)
-    far_back = back(far_back)
-    rows.update({(half, 0): near_go, (half, 1): far_back})
+    last_near = jnp.concatenate([go(near_go[:CAP]), back(near_back[CAP:])])
+    last_far = jnp.concatenate([go(far_go[:CAP]), back(far_back[CAP:])])
+    rows.update({(half, 0): last_near, (half, 1): last_far})
     work_on([member for member in rows if member not in pieces], 0)
 
     def add(x, y):

time: 80.1 us -> 79.8 us (level)
  waiting for transfers between devices: 35.8 us -> 33.1 us
  starting transfers between devices: 28.6 us -> 30.8 us
    ppermute x14 -> x15, waiting for transfers between devices: 21.4 us -> 17.3 us  [go(): return lax.ppermute(x, 'local', ahead)]
    ppermute x13 -> x14, waiting for transfers between devices: 13.9 us -> 15.8 us  [back(): return lax.ppermute(x, 'local', behind)]
    ppermute x14 -> x15, starting transfers between devices: 3.94 us -> 5.25 us  [go(): return lax.ppermute(x, 'local', ahead)]
    ppermute x13 -> x14, starting transfers between devices: 24 us -> 24.9 us  [back(): return lax.ppermute(x, 'local', behind)]
  transfers between devices with their start and end apart: 30 -> 32, of which waited for: 20 -> 20; matrix products, arithmetic and copies ran while one was open for 0% -> 1% of each run, Pallas kernels for 10% -> 10%
where the time goes in v4:
time: 79.8 us; the launch traced here: 79.6 us
  waiting for transfers between devices  33.1 us (41%)
  starting transfers between devices  30.8 us (39%)
  Pallas kernels  14.5 us (18%)
  between operations  0.82 us (1%)
    ppermute x14, starting transfers between devices, back(): return lax.ppermute(x, 'local', behind)  24.9 us
    ppermute x15, waiting for transfers between devices, go(): return lax.ppermute(x, 'local', ahead)  17.3 us
    ppermute x14, waiting for transfers between devices, back(): return lax.ppermute(x, 'local', behind)  15.8 us
    pallas_call x2, Pallas kernels, work(): pl.pallas_call(functools.partial(work_kernel, n), in_specs=[IN_VMEM] * (n...  6.03 us
    ppermute x15, starting transfers between devices, go(): return lax.ppermute(x, 'local', ahead)  5.25 us
    pallas_call x1, Pallas kernels, weight_grads(): pl.pallas_call(functools.partial(weight_grads_kernel, n), in_specs=[IN_VM...  2.84 us
    pallas_call x1, Pallas kernels, load(): pl.pallas_call(functools.partial(load_kernel, n), in_specs=[pl.BlockSpec(...  2.38 us
    pallas_call x1, Pallas kernels, pick(): pl.pallas_call(pick_kernel, in_specs=[pl.BlockSpec(memory_space=pltpu.HBM...  1.91 us
  transfers between devices with their start and end apart: 32, of which 20 were waited for; matrix products, arithmetic and copies ran while one was open for 1% of the time, Pallas kernels for 10%

profile of v4, /device:TPU:0, one launch (start us, length us, event | category | flops | bytes accessed | tf_op | source)
XLA Modules:
  0.0 79.6 jit_solution(1851573692603806188)
XLA Ops:
  0.6 1.9 %pick.1 = (bf16[32,4096]{1,0:T(8,128)(2,1)S(1)}, bf16[32,4096]{1,0:T(8,128)(2,1)S(1)}, bf16[32,128]{1,0:T(8,128)(2,1)S(1)}) custom-call(s32[8,128]{1,0:T(8,128)} %bitcast.2, f32[8,128]{1,0:T(8,128)} %bitcast.3, s32[1,128]{1,0:T(1,128)} %samples_hbm.1, bf16[128,4096]{1,0:T(8,128)(2,1)} %grad_hbm.1, bf16[128,4096]{1,0:T(8,128)(2,1)} %in_hbm.1), custom_call_target="tpu_custom_call" | custom-call | tf_op jit(solution)/shard_map/pick/pallas_call | solution.py:186
  2.6 0.5 collective-permute-start
  3.1 2.6 %collective-permute-start.2 = (bf16[32,4096]{1,0:T(8,128)(2,1)S(1)}, bf16[32,4096]{1,0:T(8,128)(2,1)S(1)}, u32[]{:S(2)}, u32[]{:S(2)}) collective-permute-start(bf16[32,4096]{1,0:T(8,128)(2,1)S(1)} %get-tuple-element.53.refs_0_), channel_id=1, source_target_pairs={{0,1},{2,0},{4,2},{6,4},{7,6},{5,7},{3,5},{1,3},{8,9},{10,8},{12,1... | collective-permute-start | bytes 786440 | tf_op jit(solution)/shard_map/ppermute | solution.py:329
  5.8 1.9 %collective-permute-start.4 = (bf16[32,4096]{1,0:T(8,128)(2,1)S(1)}, bf16[32,4096]{1,0:T(8,128)(2,1)S(1)}, u32[]{:S(2)}, u32[]{:S(2)}) collective-permute-start(bf16[32,4096]{1,0:T(8,128)(2,1)S(1)} %collective-permute-done.refs_1_), channel_id=1, source_target_pairs={{0,1},{2,0},{4,2},{6,4},{7,6},{5,7},{3,5},{1,3},{8,9},{10,8},{12,1... | collective-permute-start | bytes 786440 | tf_op jit(solution)/shard_map/ppermute | solution.py:329
  7.8 5.0 %collective-permute-done.2.refs_3_ = bf16[32,4096]{1,0:T(8,128)(2,1)S(1)} collective-permute-done((bf16[32,4096]{1,0:T(8,128)(2,1)S(1)}, bf16[32,4096]{1,0:T(8,128)(2,1)S(1)}, u32[]{:S(2)}, u32[]{:S(2)}) %collective-permute-start.2) | collective-permute-done | bytes 262176 | tf_op jit(solution)/shard_map/ppermute | solution.py:329
  12.9 1.9 %collective-permute-start.6 = (bf16[32,4096]{1,0:T(8,128)(2,1)S(1)}, bf16[32,4096]{1,0:T(8,128)(2,1)S(1)}, u32[]{:S(2)}, u32[]{:S(2)}) collective-permute-start(bf16[32,4096]{1,0:T(8,128)(2,1)S(1)} %collective-permute-done.2.refs_3_), channel_id=1, source_target_pairs={{0,1},{2,0},{4,2},{6,4},{7,6},{5,7},{3,5},{1,3},{8,9},{10,8},{12,1... | collective-permute-start | bytes 786440 | tf_op jit(solution)/shard_map/ppermute | solution.py:329
  14.9 2.4 %load.1 = (bf16[192,4096]{1,0:T(8,128)(2,1)S(1)}, bf16[192,4096]{1,0:T(8,128)(2,1)S(1)}, bf16[192,4096]{1,0:T(8,128)(2,1)S(1)}) custom-call(bf16[192,4096]{1,0:T(8,128)(2,1)} %refs_0_.1, bf16[192,4096]{1,0:T(8,128)(2,1)} %refs_1_.1, bf16[192,4096]{1,0:T(8,128)(2,1)} %refs_2_.1), custom_call_target="tpu_custom_call" | custom-call | tf_op jit(solution)/shard_map/load/pallas_call | solution.py:207
  17.3 1.2 %collective-permute-done.4.refs_5_ = bf16[32,4096]{1,0:T(8,128)(2,1)S(1)} collective-permute-done((bf16[32,4096]{1,0:T(8,128)(2,1)S(1)}, bf16[32,4096]{1,0:T(8,128)(2,1)S(1)}, u32[]{:S(2)}, u32[]{:S(2)}) %collective-permute-start.4) | collective-permute-done | bytes 262176 | tf_op jit(solution)/shard_map/ppermute | solution.py:329
  18.5 1.9 %collective-permute-done.3.refs_4_ = bf16[32,4096]{1,0:T(8,128)(2,1)S(1)} collective-permute-done((bf16[32,4096]{1,0:T(8,128)(2,1)S(1)}, bf16[32,4096]{1,0:T(8,128)(2,1)S(1)}, u32[]{:S(2)}, u32[]{:S(2)}) %collective-permute-start.3) | collective-permute-done | bytes 262176 | tf_op jit(solution)/shard_map/ppermute | solution.py:326
  20.5 1.9 %collective-permute-start.8 = (bf16[32,4096]{1,0:T(8,128)(2,1)S(1)}, bf16[32,4096]{1,0:T(8,128)(2,1)S(1)}, u32[]{:S(2)}, u32[]{:S(2)}) collective-permute-start(bf16[32,4096]{1,0:T(8,128)(2,1)S(1)} %collective-permute-done.4.refs_5_), channel_id=1, source_target_pairs={{0,1},{2,0},{4,2},{6,4},{7,6},{5,7},{3,5},{1,3},{8,9},{10,8},{12,1... | collective-permute-start | bytes 786440 | tf_op jit(solution)/shard_map/ppermute | solution.py:329
  22.4 1.7 %collective-permute-done.6.refs_7_ = bf16[32,4096]{1,0:T(8,128)(2,1)S(1)} collective-permute-done((bf16[32,4096]{1,0:T(8,128)(2,1)S(1)}, bf16[32,4096]{1,0:T(8,128)(2,1)S(1)}, u32[]{:S(2)}, u32[]{:S(2)}) %collective-permute-start.6) | collective-permute-done | bytes 262176 | tf_op jit(solution)/shard_map/ppermute | solution.py:329
  24.1 1.9 %collective-permute-start.10 = (bf16[32,4096]{1,0:T(8,128)(2,1)S(1)}, bf16[32,4096]{1,0:T(8,128)(2,1)S(1)}, u32[]{:S(2)}, u32[]{:S(2)}) collective-permute-start(bf16[32,4096]{1,0:T(8,128)(2,1)S(1)} %collective-permute-done.6.refs_7_), channel_id=1, source_target_pairs={{0,1},{2,0},{4,2},{6,4},{7,6},{5,7},{3,5},{1,3},{8,9},{10,8},{12,1... | collective-permute-start | bytes 786440 | tf_op jit(solution)/shard_map/ppermute | solution.py:329
  26.1 3.0 %work.2 = (bf16[16,4096]{1,0:T(8,128)(2,1)S(1)}, bf16[16,4096]{1,0:T(8,128)(2,1)S(1)}, bf16[16,4096]{1,0:T(8,128)(2,1)S(1)}, bf16[16,4096]{1,0:T(8,128)(2,1)S(1)...) custom-call(bf16[32,4096]{1,0:T(8,128)(2,1)S(1)} %get-tuple-element., ...), custom_call_target="tpu_custom_call" | custom-call | flops 3000000000 | tf_op jit(solution)/shard_map/work/pallas_call | solution.py:249
  29.2 0.5 collective-permute-done.8.refs_1_
  29.7 1.9 %collective-permute-done.7.refs_0_ = bf16[32,4096]{1,0:T(8,128)(2,1)S(1)} collective-permute-done((bf16[32,4096]{1,0:T(8,128)(2,1)S(1)}, bf16[32,4096]{1,0:T(8,128)(2,1)S(1)}, u32[]{:S(2)}, u32[]{:S(2)}) %collective-permute-start.7) | collective-permute-done | bytes 262176 | tf_op jit(solution)/shard_map/ppermute | solution.py:326
  31.8 1.9 %collective-permute-start.12 = (bf16[32,4096]{1,0:T(8,128)(2,1)S(1)}, bf16[32,4096]{1,0:T(8,128)(2,1)S(1)}, u32[]{:S(2)}, u32[]{:S(2)}) collective-permute-start(bf16[32,4096]{1,0:T(8,128)(2,1)S(1)} %collective-permute-done.8.refs_1_), channel_id=1, source_target_pairs={{0,1},{2,0},{4,2},{6,4},{7,6},{5,7},{3,5},{1,3},{8,9},{10,8},{12,1... | collective-permute-start | bytes 786440 | tf_op jit(solution)/shard_map/ppermute | solution.py:329
  33.7 1.7 %collective-permute-done.10.refs_3_ = bf16[32,4096]{1,0:T(8,128)(2,1)S(1)} collective-permute-done((bf16[32,4096]{1,0:T(8,128)(2,1)S(1)}, bf16[32,4096]{1,0:T(8,128)(2,1)S(1)}, u32[]{:S(2)}, u32[]{:S(2)}) %collective-permute-start.10) | collective-permute-done | bytes 262176 | tf_op jit(solution)/shard_map/ppermute | solution.py:329
  35.3 1.9 %collective-permute-done.9.refs_2_ = bf16[32,4096]{1,0:T(8,128)(2,1)S(1)} collective-permute-done((bf16[32,4096]{1,0:T(8,128)(2,1)S(1)}, bf16[32,4096]{1,0:T(8,128)(2,1)S(1)}, u32[]{:S(2)}, u32[]{:S(2)}) %collective-permute-start.9) | collective-permute-done | bytes 262176 | tf_op jit(solution)/shard_map/ppermute | solution.py:326
  37.3 1.6 %collective-permute-start.14 = (bf16[16,4096]{1,0:T(8,128)(2,1)S(1)}, bf16[16,4096]{1,0:T(8,128)(2,1)S(1)}, u32[]{:S(2)}, u32[]{:S(2)}) collective-permute-start(bf16[16,4096]{1,0:T(8,128)(2,1)S(1)} %slice.13), channel_id=1, source_target_pairs={{0,1},{2,0},{4,2},{6,4},{7,6},{5,7},{3,5},{1,3},{8,9},{10,8},{12,1... | collective-permute-start | bytes 393224 | tf_op jit(solution)/shard_map/ppermute | solution.py:329
  38.9 0.4 collective-permute-start.13
  39.4 3.5 %collective-permute-done.11.refs_4_ = bf16[32,4096]{1,0:T(8,128)(2,1)S(1)} collective-permute-done((bf16[32,4096]{1,0:T(8,128)(2,1)S(1)}, bf16[32,4096]{1,0:T(8,128)(2,1)S(1)}, u32[]{:S(2)}, u32[]{:S(2)}) %collective-permute-start.11) | collective-permute-done | bytes 262176 | tf_op jit(solution)/shard_map/ppermute | solution.py:326
  42.9 1.6 %collective-permute-start.16 = (bf16[16,4096]{1,0:T(8,128)(2,1)S(1)}, bf16[16,4096]{1,0:T(8,128)(2,1)S(1)}, u32[]{:S(2)}, u32[]{:S(2)}) collective-permute-start(bf16[16,4096]{1,0:T(8,128)(2,1)S(1)} %slice.15), channel_id=1, source_target_pairs={{0,1},{2,0},{4,2},{6,4},{7,6},{5,7},{3,5},{1,3},{8,9},{10,8},{12,1... | collective-permute-start | bytes 393224 | tf_op jit(solution)/shard_map/ppermute | solution.py:329
  45.0 2.9 %collective-permute-done.16 = bf16[16,4096]{1,0:T(8,128)(2,1)S(1)} collective-permute-done((bf16[16,4096]{1,0:T(8,128)(2,1)S(1)}, bf16[16,4096]{1,0:T(8,128)(2,1)S(1)}, u32[]{:S(2)}, u32[]{:S(2)}) %collective-permute-start.16) | collective-permute-done | bytes 131104 | tf_op jit(solution)/shard_map/ppermute | solution.py:329
  47.9 1.6 %collective-permute-done.15 = bf16[16,4096]{1,0:T(8,128)(2,1)S(1)} collective-permute-done((bf16[16,4096]{1,0:T(8,128)(2,1)S(1)}, bf16[16,4096]{1,0:T(8,128)(2,1)S(1)}, u32[]{:S(2)}, u32[]{:S(2)}) %collective-permute-start.15) | collective-permute-done | bytes 131104 | tf_op jit(solution)/shard_map/ppermute | solution.py:326
  49.5 3.0 %work.3 = (bf16[16,4096]{1,0:T(8,128)(2,1)S(1)}, bf16[16,4096]{1,0:T(8,128)(2,1)S(1)}, bf16[16,4096]{1,0:T(8,128)(2,1)S(1)}, bf16[16,4096]{1,0:T(8,128)(2,1)S(1)...) custom-call(bf16[32,4096]{1,0:T(8,128)(2,1)S(1)} %collective-permute, ...), custom_call_target="tpu_custom_call" | custom-call | tf_op jit(solution)/shard_map/work/pallas_call | solution.py:249
  52.6 0.5 collective-permute-start.17
  53.1 1.6 %collective-permute-start.21 = (bf16[16,4096]{1,0:T(8,128)(2,1)S(1)}, bf16[16,4096]{1,0:T(8,128)(2,1)S(1)}, u32[]{:S(2)}, u32[]{:S(2)}) collective-permute-start(bf16[16,4096]{1,0:T(8,128)(2,1)S(1)} %get-tuple-element.74), channel_id=1, source_target_pairs={{0,1},{2,0},{4,2},{6,4},{7,6},{5,7},{3,5},{1,3},{8,9},{10,8},{12,1... | collective-permute-start | bytes 393224 | tf_op jit(solution)/shard_map/ppermute | solution.py:329
  54.7 0.5 collective-permute-start.24
  55.1 1.6 %collective-permute-start.25 = (bf16[16,4096]{1,0:T(8,128)(2,1)S(1)}, bf16[16,4096]{1,0:T(8,128)(2,1)S(1)}, u32[]{:S(2)}, u32[]{:S(2)}) collective-permute-start(bf16[16,4096]{1,0:T(8,128)(2,1)S(1)} %get-tuple-element.82), channel_id=1, source_target_pairs={{0,1},{2,0},{4,2},{6,4},{7,6},{5,7},{3,5},{1,3},{8,9},{10,8},{12,1... | collective-permute-start | bytes 393224 | tf_op jit(solution)/shard_map/ppermute | solution.py:329
  56.7 2.0 %collective-permute-done.17 = bf16[16,4096]{1,0:T(8,128)(2,1)S(1)} collective-permute-done((bf16[16,4096]{1,0:T(8,128)(2,1)S(1)}, bf16[16,4096]{1,0:T(8,128)(2,1)S(1)}, u32[]{:S(2)}, u32[]{:S(2)}) %collective-permute-start.17) | collective-permute-done | bytes 131104 | tf_op jit(solution)/shard_map/ppermute | solution.py:326
  58.8 0.5 collective-permute-start.18
  59.3 1.6 %collective-permute-start.22 = (bf16[16,4096]{1,0:T(8,128)(2,1)S(1)}, bf16[16,4096]{1,0:T(8,128)(2,1)S(1)}, u32[]{:S(2)}, u32[]{:S(2)}) collective-permute-start(bf16[16,4096]{1,0:T(8,128)(2,1)S(1)} %add_convert_fusion.7), channel_id=1, source_target_pairs={{0,1},{2,0},{4,2},{6,4},{7,6},{5,7},{3,5},{1,3},{8,9},{10,8},{12,1... | collective-permute-start | bytes 393224 | tf_op jit(solution)/shard_map/ppermute | solution.py:329
  60.9 1.2 %collective-permute-done.25 = bf16[16,4096]{1,0:T(8,128)(2,1)S(1)} collective-permute-done((bf16[16,4096]{1,0:T(8,128)(2,1)S(1)}, bf16[16,4096]{1,0:T(8,128)(2,1)S(1)}, u32[]{:S(2)}, u32[]{:S(2)}) %collective-permute-start.25) | collective-permute-done | bytes 131104 | tf_op jit(solution)/shard_map/ppermute | solution.py:329
  62.1 1.6 %collective-permute-start.27 = (bf16[16,4096]{1,0:T(8,128)(2,1)S(1)}, bf16[16,4096]{1,0:T(8,128)(2,1)S(1)}, u32[]{:S(2)}, u32[]{:S(2)}) collective-permute-start(bf16[16,4096]{1,0:T(8,128)(2,1)S(1)} %add_convert_fusion.4), channel_id=1, source_target_pairs={{0,1},{2,0},{4,2},{6,4},{7,6},{5,7},{3,5},{1,3},{8,9},{10,8},{12,1... | collective-permute-start | bytes 393224 | tf_op jit(solution)/shard_map/ppermute | solution.py:329
  63.8 0.5 collective-permute-start.26
  64.3 0.6 collective-permute-done.18
  64.9 0.5 collective-permute-start.19
  65.6 1.6 %collective-permute-start.23 = (bf16[16,4096]{1,0:T(8,128)(2,1)S(1)}, bf16[16,4096]{1,0:T(8,128)(2,1)S(1)}, u32[]{:S(2)}, u32[]{:S(2)}) collective-permute-start(bf16[16,4096]{1,0:T(8,128)(2,1)S(1)} %add_convert_fusion.6), channel_id=1, source_target_pairs={{0,1},{2,0},{4,2},{6,4},{7,6},{5,7},{3,5},{1,3},{8,9},{10,8},{12,1... | collective-permute-start | bytes 393224 | tf_op jit(solution)/shard_map/ppermute | solution.py:329
  67.2 0.9 %collective-permute-done.27 = bf16[16,4096]{1,0:T(8,128)(2,1)S(1)} collective-permute-done((bf16[16,4096]{1,0:T(8,128)(2,1)S(1)}, bf16[16,4096]{1,0:T(8,128)(2,1)S(1)}, u32[]{:S(2)}, u32[]{:S(2)}) %collective-permute-start.27) | collective-permute-done | bytes 131104 | tf_op jit(solution)/shard_map/ppermute | solution.py:329
  68.1 1.6 %collective-permute-start.30 = (bf16[16,4096]{1,0:T(8,128)(2,1)S(1)}, bf16[16,4096]{1,0:T(8,128)(2,1)S(1)}, u32[]{:S(2)}, u32[]{:S(2)}) collective-permute-start(bf16[16,4096]{1,0:T(8,128)(2,1)S(1)} %add_convert_fusion.2), channel_id=1, source_target_pairs={{0,1},{2,0},{4,2},{6,4},{7,6},{5,7},{3,5},{1,3},{8,9},{10,8},{12,1... | collective-permute-start | bytes 393224 | tf_op jit(solution)/shard_map/ppermute | solution.py:329
  69.7 0.5 collective-permute-done.26
  70.3 0.5 collective-permute-start.28
  70.8 1.1 %collective-permute-done.19 = bf16[16,4096]{1,0:T(8,128)(2,1)S(1)} collective-permute-done((bf16[16,4096]{1,0:T(8,128)(2,1)S(1)}, bf16[16,4096]{1,0:T(8,128)(2,1)S(1)}, u32[]{:S(2)}, u32[]{:S(2)}) %collective-permute-start.19) | collective-permute-done | bytes 131104 | tf_op jit(solution)/shard_map/ppermute | solution.py:326
  71.9 0.5 collective-permute-start.20
  72.5 0.7 collective-permute-done.30
  73.2 2.1 %collective-permute-done.28 = bf16[16,4096]{1,0:T(8,128)(2,1)S(1)} collective-permute-done((bf16[16,4096]{1,0:T(8,128)(2,1)S(1)}, bf16[16,4096]{1,0:T(8,128)(2,1)S(1)}, u32[]{:S(2)}, u32[]{:S(2)}) %collective-permute-start.28) | collective-permute-done | bytes 131104 | tf_op jit(solution)/shard_map/ppermute | solution.py:326
  75.4 2.8 %weight_grads.1 = (bf16[192,4096]{1,0:T(8,128)(2,1)}, bf16[192,4096]{1,0:T(8,128)(2,1)}, bf16[192,4096]{1,0:T(8,128)(2,1)}) custom-call(bf16[128,192]{1,0:T(8,128)(2,1)S(1)} %get-tuple-element.87.refs_0_, bf16[128,192]{1,0:T(8,128)(2,1)S(1)} %get-tuple-element.88.refs_1_, bf16[128,192]{1,0:T(8,128)(2,1)S(1)} %get-tuple-element.89.refs_2_, ...), custom_call_target="tpu_custom_call" | custom-call | flops 3000000000 | tf_op jit(solution)/shard_map/weight_grads/pallas_call | solution.py:278
  78.3 1.3 %place.1 = bf16[128,4096]{1,0:T(8,128)(2,1)} custom-call(bf16[32,128]{1,0:T(8,128)(2,1)S(1)} %get-tuple-element.52.select_ref, bf16[16,4096]{1,0:T(8,128)(2,1)S(1)} %get-tuple-element.58.own_ref, bf16[16,4096]{1,0:T(8,128)(2,1)S(1)} %collective-permute-done.20.ahead_ref, bf16[16,4096]{1,0:T(8,128)(2,1)S(1)} %collective-permute-done.23.behind_ref, ...), custom_call_target="tpu_custom_call" | custom-call | tf_op jit(solution)/shard_map/place/pallas_call | solution.py:309
  (39 shorter events, 2.0 us)
Async XLA Ops:
  2.6 3.2 %collective-permute-start = (bf16[32,4096]{1,0:T(8,128)(2,1)S(1)}, bf16[32,4096]{1,0:T(8,128)(2,1)S(1)}, u32[]{:S(2)}, u32[]{:S(2)}) collective-permute-start(bf16[32,4096]{1,0:T(8,128)(2,1)S(1)} %get-tuple-element.54), channel_id=1, source_target_pairs={{0,8},{8,0},{1,9},{9,1},{2,10},{10,2},{3,11},{11,3},{4,12},{12,4},... | collective-permute-start | bytes 786440 | tf_op jit(solution)/shard_map/ppermute | solution.py:337
  3.1 9.8 %collective-permute-start.2 = (bf16[32,4096]{1,0:T(8,128)(2,1)S(1)}, bf16[32,4096]{1,0:T(8,128)(2,1)S(1)}, u32[]{:S(2)}, u32[]{:S(2)}) collective-permute-start(bf16[32,4096]{1,0:T(8,128)(2,1)S(1)} %get-tuple-element.53.refs_0_), channel_id=1, source_target_pairs={{0,1},{2,0},{4,2},{6,4},{7,6},{5,7},{3,5},{1,3},{8,9},{10,8},{12,1... | collective-permute-start | bytes 786440 | tf_op jit(solution)/shard_map/ppermute | solution.py:329
  5.6 9.1 %collective-permute-start.1 = (bf16[32,4096]{1,0:T(8,128)(2,1)S(1)}, bf16[32,4096]{1,0:T(8,128)(2,1)S(1)}, u32[]{:S(2)}, u32[]{:S(2)}) collective-permute-start(bf16[32,4096]{1,0:T(8,128)(2,1)S(1)} %get-tuple-element.53.refs_0_), channel_id=1, source_target_pairs={{0,2},{2,4},{4,6},{6,7},{7,5},{5,3},{3,1},{1,0},{8,10},{10,12},{12... | collective-permute-start | bytes 786440 | tf_op jit(solution)/shard_map/ppermute | solution.py:326
  5.8 12.7 %collective-permute-start.4 = (bf16[32,4096]{1,0:T(8,128)(2,1)S(1)}, bf16[32,4096]{1,0:T(8,128)(2,1)S(1)}, u32[]{:S(2)}, u32[]{:S(2)}) collective-permute-start(bf16[32,4096]{1,0:T(8,128)(2,1)S(1)} %collective-permute-done.refs_1_), channel_id=1, source_target_pairs={{0,1},{2,0},{4,2},{6,4},{7,6},{5,7},{3,5},{1,3},{8,9},{10,8},{12,1... | collective-permute-start | bytes 786440 | tf_op jit(solution)/shard_map/ppermute | solution.py:329
  7.7 12.7 %collective-permute-start.3 = (bf16[32,4096]{1,0:T(8,128)(2,1)S(1)}, bf16[32,4096]{1,0:T(8,128)(2,1)S(1)}, u32[]{:S(2)}, u32[]{:S(2)}) collective-permute-start(bf16[32,4096]{1,0:T(8,128)(2,1)S(1)} %collective-permute-done.refs_1_), channel_id=1, source_target_pairs={{0,2},{2,4},{4,6},{6,7},{7,5},{5,3},{3,1},{1,0},{8,10},{10,12},{12... | collective-permute-start | bytes 786440 | tf_op jit(solution)/shard_map/ppermute | solution.py:326
  12.9 11.2 %collective-permute-start.6 = (bf16[32,4096]{1,0:T(8,128)(2,1)S(1)}, bf16[32,4096]{1,0:T(8,128)(2,1)S(1)}, u32[]{:S(2)}, u32[]{:S(2)}) collective-permute-start(bf16[32,4096]{1,0:T(8,128)(2,1)S(1)} %collective-permute-done.2.refs_3_), channel_id=1, source_target_pairs={{0,1},{2,0},{4,2},{6,4},{7,6},{5,7},{3,5},{1,3},{8,9},{10,8},{12,1... | collective-permute-start | bytes 786440 | tf_op jit(solution)/shard_map/ppermute | solution.py:329
  14.8 11.2 %collective-permute-start.5 = (bf16[32,4096]{1,0:T(8,128)(2,1)S(1)}, bf16[32,4096]{1,0:T(8,128)(2,1)S(1)}, u32[]{:S(2)}, u32[]{:S(2)}) collective-permute-start(bf16[32,4096]{1,0:T(8,128)(2,1)S(1)} %collective-permute-done.1.refs_2_), channel_id=1, source_target_pairs={{0,2},{2,4},{4,6},{6,7},{7,5},{5,3},{3,1},{1,0},{8,10},{10,12},{12... | collective-permute-start | bytes 786440 | tf_op jit(solution)/shard_map/ppermute | solution.py:326
  20.4 11.2 %collective-permute-start.7 = (bf16[32,4096]{1,0:T(8,128)(2,1)S(1)}, bf16[32,4096]{1,0:T(8,128)(2,1)S(1)}, u32[]{:S(2)}, u32[]{:S(2)}) collective-permute-start(bf16[32,4096]{1,0:T(8,128)(2,1)S(1)} %collective-permute-done.3.refs_4_), channel_id=1, source_target_pairs={{0,2},{2,4},{4,6},{6,7},{7,5},{5,3},{3,1},{1,0},{8,10},{10,12},{12... | collective-permute-start | bytes 786440 | tf_op jit(solution)/shard_map/ppermute | solution.py:326
  20.5 9.2 %collective-permute-start.8 = (bf16[32,4096]{1,0:T(8,128)(2,1)S(1)}, bf16[32,4096]{1,0:T(8,128)(2,1)S(1)}, u32[]{:S(2)}, u32[]{:S(2)}) collective-permute-start(bf16[32,4096]{1,0:T(8,128)(2,1)S(1)} %collective-permute-done.4.refs_5_), channel_id=1, source_target_pairs={{0,1},{2,0},{4,2},{6,4},{7,6},{5,7},{3,5},{1,3},{8,9},{10,8},{12,1... | collective-permute-start | bytes 786440 | tf_op jit(solution)/shard_map/ppermute | solution.py:329
  24.1 11.2 %collective-permute-start.10 = (bf16[32,4096]{1,0:T(8,128)(2,1)S(1)}, bf16[32,4096]{1,0:T(8,128)(2,1)S(1)}, u32[]{:S(2)}, u32[]{:S(2)}) collective-permute-start(bf16[32,4096]{1,0:T(8,128)(2,1)S(1)} %collective-permute-done.6.refs_7_), channel_id=1, source_target_pairs={{0,1},{2,0},{4,2},{6,4},{7,6},{5,7},{3,5},{1,3},{8,9},{10,8},{12,1... | collective-permute-start | bytes 786440 | tf_op jit(solution)/shard_map/ppermute | solution.py:329
  26.0 11.2 %collective-permute-start.9 = (bf16[32,4096]{1,0:T(8,128)(2,1)S(1)}, bf16[32,4096]{1,0:T(8,128)(2,1)S(1)}, u32[]{:S(2)}, u32[]{:S(2)}) collective-permute-start(bf16[32,4096]{1,0:T(8,128)(2,1)S(1)} %collective-permute-done.5.refs_6_), channel_id=1, source_target_pairs={{0,2},{2,4},{4,6},{6,7},{7,5},{5,3},{3,1},{1,0},{8,10},{10,12},{12... | collective-permute-start | bytes 786440 | tf_op jit(solution)/shard_map/ppermute | solution.py:326
  31.7 11.2 %collective-permute-start.11 = (bf16[32,4096]{1,0:T(8,128)(2,1)S(1)}, bf16[32,4096]{1,0:T(8,128)(2,1)S(1)}, u32[]{:S(2)}, u32[]{:S(2)}) collective-permute-start(bf16[32,4096]{1,0:T(8,128)(2,1)S(1)} %collective-permute-done.7.refs_0_), channel_id=1, source_target_pairs={{0,2},{2,4},{4,6},{6,7},{7,5},{5,3},{3,1},{1,0},{8,10},{10,12},{12... | collective-permute-start | bytes 786440 | tf_op jit(solution)/shard_map/ppermute | solution.py:326
  31.8 11.1 %collective-permute-start.12 = (bf16[32,4096]{1,0:T(8,128)(2,1)S(1)}, bf16[32,4096]{1,0:T(8,128)(2,1)S(1)}, u32[]{:S(2)}, u32[]{:S(2)}) collective-permute-start(bf16[32,4096]{1,0:T(8,128)(2,1)S(1)} %collective-permute-done.8.refs_1_), channel_id=1, source_target_pairs={{0,1},{2,0},{4,2},{6,4},{7,6},{5,7},{3,5},{1,3},{8,9},{10,8},{12,1... | collective-permute-start | bytes 786440 | tf_op jit(solution)/shard_map/ppermute | solution.py:329
  37.3 7.7 %collective-permute-start.14 = (bf16[16,4096]{1,0:T(8,128)(2,1)S(1)}, bf16[16,4096]{1,0:T(8,128)(2,1)S(1)}, u32[]{:S(2)}, u32[]{:S(2)}) collective-permute-start(bf16[16,4096]{1,0:T(8,128)(2,1)S(1)} %slice.13), channel_id=1, source_target_pairs={{0,1},{2,0},{4,2},{6,4},{7,6},{5,7},{3,5},{1,3},{8,9},{10,8},{12,1... | collective-permute-start | bytes 393224 | tf_op jit(solution)/shard_map/ppermute | solution.py:329
  38.9 6.1 %collective-permute-start.13 = (bf16[16,4096]{1,0:T(8,128)(2,1)S(1)}, bf16[16,4096]{1,0:T(8,128)(2,1)S(1)}, u32[]{:S(2)}, u32[]{:S(2)}) collective-permute-start(bf16[16,4096]{1,0:T(8,128)(2,1)S(1)} %slice.12), channel_id=1, source_target_pairs={{0,2},{2,4},{4,6},{6,7},{7,5},{5,3},{3,1},{1,0},{8,10},{10,12},{12... | collective-permute-start | bytes 393224 | tf_op jit(solution)/shard_map/ppermute | solution.py:326
  42.9 5.0 %collective-permute-start.16 = (bf16[16,4096]{1,0:T(8,128)(2,1)S(1)}, bf16[16,4096]{1,0:T(8,128)(2,1)S(1)}, u32[]{:S(2)}, u32[]{:S(2)}) collective-permute-start(bf16[16,4096]{1,0:T(8,128)(2,1)S(1)} %slice.15), channel_id=1, source_target_pairs={{0,1},{2,0},{4,2},{6,4},{7,6},{5,7},{3,5},{1,3},{8,9},{10,8},{12,1... | collective-permute-start | bytes 393224 | tf_op jit(solution)/shard_map/ppermute | solution.py:329
  44.6 5.0 %collective-permute-start.15 = (bf16[16,4096]{1,0:T(8,128)(2,1)S(1)}, bf16[16,4096]{1,0:T(8,128)(2,1)S(1)}, u32[]{:S(2)}, u32[]{:S(2)}) collective-permute-start(bf16[16,4096]{1,0:T(8,128)(2,1)S(1)} %slice.14), channel_id=1, source_target_pairs={{0,2},{2,4},{4,6},{6,7},{7,5},{5,3},{3,1},{1,0},{8,10},{10,12},{12... | collective-permute-start | bytes 393224 | tf_op jit(solution)/shard_map/ppermute | solution.py:326
  52.6 6.2 %collective-permute-start.17 = (bf16[16,4096]{1,0:T(8,128)(2,1)S(1)}, bf16[16,4096]{1,0:T(8,128)(2,1)S(1)}, u32[]{:S(2)}, u32[]{:S(2)}) collective-permute-start(bf16[16,4096]{1,0:T(8,128)(2,1)S(1)} %get-tuple-element.71), channel_id=1, source_target_pairs={{0,2},{2,4},{4,6},{6,7},{7,5},{5,3},{3,1},{1,0},{8,10},{10,12},{12... | collective-permute-start | bytes 393224 | tf_op jit(solution)/shard_map/ppermute | solution.py:326
  53.1 6.2 %collective-permute-start.21 = (bf16[16,4096]{1,0:T(8,128)(2,1)S(1)}, bf16[16,4096]{1,0:T(8,128)(2,1)S(1)}, u32[]{:S(2)}, u32[]{:S(2)}) collective-permute-start(bf16[16,4096]{1,0:T(8,128)(2,1)S(1)} %get-tuple-element.74), channel_id=1, source_target_pairs={{0,1},{2,0},{4,2},{6,4},{7,6},{5,7},{3,5},{1,3},{8,9},{10,8},{12,1... | collective-permute-start | bytes 393224 | tf_op jit(solution)/shard_map/ppermute | solution.py:329
  54.7 9.1 %collective-permute-start.24 = (bf16[16,4096]{1,0:T(8,128)(2,1)S(1)}, bf16[16,4096]{1,0:T(8,128)(2,1)S(1)}, u32[]{:S(2)}, u32[]{:S(2)}) collective-permute-start(bf16[16,4096]{1,0:T(8,128)(2,1)S(1)} %get-tuple-element.80), channel_id=1, source_target_pairs={{0,2},{2,4},{4,6},{6,7},{7,5},{5,3},{3,1},{1,0},{8,10},{10,12},{12... | collective-permute-start | bytes 393224 | tf_op jit(solution)/shard_map/ppermute | solution.py:326
  55.1 7.0 %collective-permute-start.25 = (bf16[16,4096]{1,0:T(8,128)(2,1)S(1)}, bf16[16,4096]{1,0:T(8,128)(2,1)S(1)}, u32[]{:S(2)}, u32[]{:S(2)}) collective-permute-start(bf16[16,4096]{1,0:T(8,128)(2,1)S(1)} %get-tuple-element.82), channel_id=1, source_target_pairs={{0,1},{2,0},{4,2},{6,4},{7,6},{5,7},{3,5},{1,3},{8,9},{10,8},{12,1... | collective-permute-start | bytes 393224 | tf_op jit(solution)/shard_map/ppermute | solution.py:329
  58.8 6.1 %collective-permute-start.18 = (bf16[16,4096]{1,0:T(8,128)(2,1)S(1)}, bf16[16,4096]{1,0:T(8,128)(2,1)S(1)}, u32[]{:S(2)}, u32[]{:S(2)}) collective-permute-start(bf16[16,4096]{1,0:T(8,128)(2,1)S(1)} %add_convert_fusion.10), channel_id=1, source_target_pairs={{0,2},{2,4},{4,6},{6,7},{7,5},{5,3},{3,1},{1,0},{8,10},{10,12},{12... | collective-permute-start | bytes 393224 | tf_op jit(solution)/shard_map/ppermute | solution.py:326
  59.3 6.2 %collective-permute-start.22 = (bf16[16,4096]{1,0:T(8,128)(2,1)S(1)}, bf16[16,4096]{1,0:T(8,128)(2,1)S(1)}, u32[]{:S(2)}, u32[]{:S(2)}) collective-permute-start(bf16[16,4096]{1,0:T(8,128)(2,1)S(1)} %add_convert_fusion.7), channel_id=1, source_target_pairs={{0,1},{2,0},{4,2},{6,4},{7,6},{5,7},{3,5},{1,3},{8,9},{10,8},{12,1... | collective-permute-start | bytes 393224 | tf_op jit(solution)/shard_map/ppermute | solution.py:329
  62.1 5.9 %collective-permute-start.27 = (bf16[16,4096]{1,0:T(8,128)(2,1)S(1)}, bf16[16,4096]{1,0:T(8,128)(2,1)S(1)}, u32[]{:S(2)}, u32[]{:S(2)}) collective-permute-start(bf16[16,4096]{1,0:T(8,128)(2,1)S(1)} %add_convert_fusion.4), channel_id=1, source_target_pairs={{0,1},{2,0},{4,2},{6,4},{7,6},{5,7},{3,5},{1,3},{8,9},{10,8},{12,1... | collective-permute-start | bytes 393224 | tf_op jit(solution)/shard_map/ppermute | solution.py:329
  63.8 6.4 %collective-permute-start.26 = (bf16[16,4096]{1,0:T(8,128)(2,1)S(1)}, bf16[16,4096]{1,0:T(8,128)(2,1)S(1)}, u32[]{:S(2)}, u32[]{:S(2)}) collective-permute-start(bf16[16,4096]{1,0:T(8,128)(2,1)S(1)} %add_convert_fusion.5), channel_id=1, source_target_pairs={{0,2},{2,4},{4,6},{6,7},{7,5},{5,3},{3,1},{1,0},{8,10},{10,12},{12... | collective-permute-start | bytes 393224 | tf_op jit(solution)/shard_map/ppermute | solution.py:326
  64.9 7.0 %collective-permute-start.19 = (bf16[16,4096]{1,0:T(8,128)(2,1)S(1)}, bf16[16,4096]{1,0:T(8,128)(2,1)S(1)}, u32[]{:S(2)}, u32[]{:S(2)}) collective-permute-start(bf16[16,4096]{1,0:T(8,128)(2,1)S(1)} %add_convert_fusion.9), channel_id=1, source_target_pairs={{0,2},{2,4},{4,6},{6,7},{7,5},{5,3},{3,1},{1,0},{8,10},{10,12},{12... | collective-permute-start | bytes 393224 | tf_op jit(solution)/shard_map/ppermute | solution.py:326
  65.6 12.7 %collective-permute-start.23 = (bf16[16,4096]{1,0:T(8,128)(2,1)S(1)}, bf16[16,4096]{1,0:T(8,128)(2,1)S(1)}, u32[]{:S(2)}, u32[]{:S(2)}) collective-permute-start(bf16[16,4096]{1,0:T(8,128)(2,1)S(1)} %add_convert_fusion.6), channel_id=1, source_target_pairs={{0,1},{2,0},{4,2},{6,4},{7,6},{5,7},{3,5},{1,3},{8,9},{10,8},{12,1... | collective-permute-start | bytes 393224 | tf_op jit(solution)/shard_map/ppermute | solution.py:329
  68.1 5.0 %collective-permute-start.30 = (bf16[16,4096]{1,0:T(8,128)(2,1)S(1)}, bf16[16,4096]{1,0:T(8,128)(2,1)S(1)}, u32[]{:S(2)}, u32[]{:S(2)}) collective-permute-start(bf16[16,4096]{1,0:T(8,128)(2,1)S(1)} %add_convert_fusion.2), channel_id=1, source_target_pairs={{0,1},{2,0},{4,2},{6,4},{7,6},{5,7},{3,5},{1,3},{8,9},{10,8},{12,1... | collective-permute-start | bytes 393224 | tf_op jit(solution)/shard_map/ppermute | solution.py:329
  70.3 5.0 %collective-permute-start.28 = (bf16[16,4096]{1,0:T(8,128)(2,1)S(1)}, bf16[16,4096]{1,0:T(8,128)(2,1)S(1)}, u32[]{:S(2)}, u32[]{:S(2)}) collective-permute-start(bf16[16,4096]{1,0:T(8,128)(2,1)S(1)} %add_convert_fusion.3), channel_id=1, source_target_pairs={{0,2},{2,4},{4,6},{6,7},{7,5},{5,3},{3,1},{1,0},{8,10},{10,12},{12... | collective-permute-start | bytes 393224 | tf_op jit(solution)/shard_map/ppermute | solution.py:326
  71.9 6.3 %collective-permute-start.20 = (bf16[16,4096]{1,0:T(8,128)(2,1)S(1)}, bf16[16,4096]{1,0:T(8,128)(2,1)S(1)}, u32[]{:S(2)}, u32[]{:S(2)}) collective-permute-start(bf16[16,4096]{1,0:T(8,128)(2,1)S(1)} %add_convert_fusion.8), channel_id=1, source_target_pairs={{0,2},{2,4},{4,6},{6,7},{7,5},{5,3},{3,1},{1,0},{8,10},{10,12},{12... | collective-permute-start | bytes 393224 | tf_op jit(solution)/shard_map/ppermute | solution.py:326
  73.2 5.1 %collective-permute-start.31 = (bf16[16,4096]{1,0:T(8,128)(2,1)S(1)}, bf16[16,4096]{1,0:T(8,128)(2,1)S(1)}, u32[]{:S(2)}, u32[]{:S(2)}) collective-permute-start(bf16[16,4096]{1,0:T(8,128)(2,1)S(1)} %add_convert_fusion), channel_id=1, source_target_pairs={{0,9},{2,8},{4,10},{6,12},{7,14},{5,15},{3,13},{1,11},{8,1},{10,0}... | collective-permute-start | bytes 393224 | tf_op jit(solution)/shard_map/ppermute | solution.py:334
  75.3 3.0 %collective-permute-start.29 = (bf16[16,4096]{1,0:T(8,128)(2,1)S(1)}, bf16[16,4096]{1,0:T(8,128)(2,1)S(1)}, u32[]{:S(2)}, u32[]{:S(2)}) collective-permute-start(bf16[16,4096]{1,0:T(8,128)(2,1)S(1)} %add_convert_fusion.1), channel_id=1, source_target_pairs={{0,8},{8,0},{1,9},{9,1},{2,10},{10,2},{3,11},{11,3},{4,12},{12,4},... | collective-permute-start | bytes 393224 | tf_op jit(solution)/shard_map/ppermute | solution.py:382

commit v5 on v4

--- a/solution.py
+++ b/solution.py
@@ -295,7 +295,7 @@
         rows_ref[:CAP, k] = here.astype(BF)
         rows_ref[CAP:, k] = there.astype(BF)
     copies = []
-    for j, r in enumerate(tiles_of(out_ref.shape[0], buffer.shape[0] // 2)):
+    for j, r in enumerate(tiles_of(out_ref.shape[0], buffer.shape[0] // 4)):
         for k in tiles_of(out_ref.shape[1], 1024):
             buffer[r, k] = dot(spread[r.start : r.start + r.size], rows_ref[:, k]).astype(BF)
         copies.append(pltpu.make_async_copy(buffer.at[r], out_ref.at[r], sem.at[j]))
@@ -311,7 +311,7 @@
         in_specs=[IN_VMEM] * 6,
         out_specs=pl.BlockSpec(memory_space=pl.ANY),
         out_shape=jax.ShapeDtypeStruct((count, width), BF),
-        scratch_shapes=[pltpu.VMEM((2 * CAP, width), BF), pltpu.VMEM((count, width), BF), pltpu.SemaphoreType.DMA((2,))],
+        scratch_shapes=[pltpu.VMEM((2 * CAP, width), BF), pltpu.VMEM((count, width), BF), pltpu.SemaphoreType.DMA((4,))],
         compiler_params=pltpu.CompilerParams(vmem_limit_bytes=8 << 20),
         name="place",
     )(*[held(x) for x in (select, own, ahead, behind, first, second)])
@@ -375,7 +375,6 @@
         far_long, near_long = add(pieces[-s, 1], far_long), add(pieces[s, 0], near_long)
         if s > 1:
             far_short, near_short = add(pieces[s - 1, 1], far_short), add(pieces[1 - s, 0], near_short)
-            far_short, near_short = after(far_short, far_long), after(near_short, near_long)
     saved[0] = [after(saved[0][0], far_long, near_long), *saved[0][1:]]
     grad_gate, grad_up, grad_down = weight_grads(saved)
     far_long, near_long = cross(far_long, behind), go(near_long)

time: 79.8 us -> 79.8 us (level)
  waiting for transfers between devices: 33.1 us -> 31.4 us
  starting transfers between devices: 30.8 us -> 32.4 us
    ppermute x1, starting transfers between devices: 0.07 us -> 1.71 us  [per_device_ring(): first = lax.ppermute(add(pieces[0, 1], far_short), 'node', swap)]
    ppermute x15, waiting for transfers between devices: 17.3 us -> 15.9 us  [go(): return lax.ppermute(x, 'local', ahead)]
  transfers between devices with their start and end apart: 32 -> 32, of which waited for: 20 -> 17; matrix products, arithmetic and copies ran while one was open for 1% -> 1% of each run, Pallas kernels for 10% -> 10%
where the time goes in v5:
time: 79.8 us; the launch traced here: 79.6 us
  starting transfers between devices  32.4 us (41%)
  waiting for transfers between devices  31.4 us (39%)
  Pallas kernels  14.4 us (18%)
  between operations  0.82 us (1%)
    ppermute x14, starting transfers between devices, back(): return lax.ppermute(x, 'local', behind)  24.8 us
    ppermute x15, waiting for transfers between devices, go(): return lax.ppermute(x, 'local', ahead)  15.9 us
    ppermute x14, waiting for transfers between devices, back(): return lax.ppermute(x, 'local', behind)  15.5 us
    pallas_call x2, Pallas kernels, work(): pl.pallas_call(functools.partial(work_kernel, n), in_specs=[IN_VMEM] * (n...  6.03 us
    ppermute x15, starting transfers between devices, go(): return lax.ppermute(x, 'local', ahead)  5.35 us
    pallas_call x1, Pallas kernels, weight_grads(): pl.pallas_call(functools.partial(weight_grads_kernel, n), in_specs=[IN_VM...  2.84 us
    pallas_call x1, Pallas kernels, load(): pl.pallas_call(functools.partial(load_kernel, n), in_specs=[pl.BlockSpec(...  2.38 us
    pallas_call x1, Pallas kernels, pick(): pl.pallas_call(pick_kernel, in_specs=[pl.BlockSpec(memory_space=pltpu.HBM...  1.91 us
  transfers between devices with their start and end apart: 32, of which 17 were waited for; matrix products, arithmetic and copies ran while one was open for 1% of the time, Pallas kernels for 10%

profile of v5, /device:TPU:0, one launch (start us, length us, event | category | flops | bytes accessed | tf_op | source)
XLA Modules:
  0.0 79.6 jit_solution(17900675956077881152)
XLA Ops:
  0.6 1.9 %pick.1 = (bf16[32,4096]{1,0:T(8,128)(2,1)S(1)}, bf16[32,4096]{1,0:T(8,128)(2,1)S(1)}, bf16[32,128]{1,0:T(8,128)(2,1)S(1)}) custom-call(s32[8,128]{1,0:T(8,128)} %bitcast.2, f32[8,128]{1,0:T(8,128)} %bitcast.3, s32[1,128]{1,0:T(1,128)} %samples_hbm.1, bf16[128,4096]{1,0:T(8,128)(2,1)} %grad_hbm.1, bf16[128,4096]{1,0:T(8,128)(2,1)} %in_hbm.1), custom_call_target="tpu_custom_call" | custom-call | tf_op jit(solution)/shard_map/pick/pallas_call | solution.py:186
  2.6 0.5 collective-permute-start
  3.1 2.6 %collective-permute-start.2 = (bf16[32,4096]{1,0:T(8,128)(2,1)S(1)}, bf16[32,4096]{1,0:T(8,128)(2,1)S(1)}, u32[]{:S(2)}, u32[]{:S(2)}) collective-permute-start(bf16[32,4096]{1,0:T(8,128)(2,1)S(1)} %get-tuple-element.49.refs_0_), channel_id=1, source_target_pairs={{0,1},{2,0},{4,2},{6,4},{7,6},{5,7},{3,5},{1,3},{8,9},{10,8},{12,1... | collective-permute-start | bytes 786440 | tf_op jit(solution)/shard_map/ppermute | solution.py:329
  5.8 1.9 %collective-permute-start.4 = (bf16[32,4096]{1,0:T(8,128)(2,1)S(1)}, bf16[32,4096]{1,0:T(8,128)(2,1)S(1)}, u32[]{:S(2)}, u32[]{:S(2)}) collective-permute-start(bf16[32,4096]{1,0:T(8,128)(2,1)S(1)} %collective-permute-done.refs_1_), channel_id=1, source_target_pairs={{0,1},{2,0},{4,2},{6,4},{7,6},{5,7},{3,5},{1,3},{8,9},{10,8},{12,1... | collective-permute-start | bytes 786440 | tf_op jit(solution)/shard_map/ppermute | solution.py:329
  7.8 5.0 %collective-permute-done.2.refs_3_ = bf16[32,4096]{1,0:T(8,128)(2,1)S(1)} collective-permute-done((bf16[32,4096]{1,0:T(8,128)(2,1)S(1)}, bf16[32,4096]{1,0:T(8,128)(2,1)S(1)}, u32[]{:S(2)}, u32[]{:S(2)}) %collective-permute-start.2) | collective-permute-done | bytes 262176 | tf_op jit(solution)/shard_map/ppermute | solution.py:329
  12.9 1.9 %collective-permute-start.6 = (bf16[32,4096]{1,0:T(8,128)(2,1)S(1)}, bf16[32,4096]{1,0:T(8,128)(2,1)S(1)}, u32[]{:S(2)}, u32[]{:S(2)}) collective-permute-start(bf16[32,4096]{1,0:T(8,128)(2,1)S(1)} %collective-permute-done.2.refs_3_), channel_id=1, source_target_pairs={{0,1},{2,0},{4,2},{6,4},{7,6},{5,7},{3,5},{1,3},{8,9},{10,8},{12,1... | collective-permute-start | bytes 786440 | tf_op jit(solution)/shard_map/ppermute | solution.py:329
  14.9 2.4 %load.1 = (bf16[192,4096]{1,0:T(8,128)(2,1)S(1)}, bf16[192,4096]{1,0:T(8,128)(2,1)S(1)}, bf16[192,4096]{1,0:T(8,128)(2,1)S(1)}) custom-call(bf16[192,4096]{1,0:T(8,128)(2,1)} %refs_0_.1, bf16[192,4096]{1,0:T(8,128)(2,1)} %refs_1_.1, bf16[192,4096]{1,0:T(8,128)(2,1)} %refs_2_.1), custom_call_target="tpu_custom_call" | custom-call | tf_op jit(solution)/shard_map/load/pallas_call | solution.py:207
  17.3 1.2 %collective-permute-done.4.refs_5_ = bf16[32,4096]{1,0:T(8,128)(2,1)S(1)} collective-permute-done((bf16[32,4096]{1,0:T(8,128)(2,1)S(1)}, bf16[32,4096]{1,0:T(8,128)(2,1)S(1)}, u32[]{:S(2)}, u32[]{:S(2)}) %collective-permute-start.4) | collective-permute-done | bytes 262176 | tf_op jit(solution)/shard_map/ppermute | solution.py:329
  18.5 1.9 %collective-permute-done.3.refs_4_ = bf16[32,4096]{1,0:T(8,128)(2,1)S(1)} collective-permute-done((bf16[32,4096]{1,0:T(8,128)(2,1)S(1)}, bf16[32,4096]{1,0:T(8,128)(2,1)S(1)}, u32[]{:S(2)}, u32[]{:S(2)}) %collective-permute-start.3) | collective-permute-done | bytes 262176 | tf_op jit(solution)/shard_map/ppermute | solution.py:326
  20.5 1.9 %collective-permute-start.8 = (bf16[32,4096]{1,0:T(8,128)(2,1)S(1)}, bf16[32,4096]{1,0:T(8,128)(2,1)S(1)}, u32[]{:S(2)}, u32[]{:S(2)}) collective-permute-start(bf16[32,4096]{1,0:T(8,128)(2,1)S(1)} %collective-permute-done.4.refs_5_), channel_id=1, source_target_pairs={{0,1},{2,0},{4,2},{6,4},{7,6},{5,7},{3,5},{1,3},{8,9},{10,8},{12,1... | collective-permute-start | bytes 786440 | tf_op jit(solution)/shard_map/ppermute | solution.py:329
  22.4 1.7 %collective-permute-done.6.refs_7_ = bf16[32,4096]{1,0:T(8,128)(2,1)S(1)} collective-permute-done((bf16[32,4096]{1,0:T(8,128)(2,1)S(1)}, bf16[32,4096]{1,0:T(8,128)(2,1)S(1)}, u32[]{:S(2)}, u32[]{:S(2)}) %collective-permute-start.6) | collective-permute-done | bytes 262176 | tf_op jit(solution)/shard_map/ppermute | solution.py:329
  24.1 1.9 %collective-permute-start.10 = (bf16[32,4096]{1,0:T(8,128)(2,1)S(1)}, bf16[32,4096]{1,0:T(8,128)(2,1)S(1)}, u32[]{:S(2)}, u32[]{:S(2)}) collective-permute-start(bf16[32,4096]{1,0:T(8,128)(2,1)S(1)} %collective-permute-done.6.refs_7_), channel_id=1, source_target_pairs={{0,1},{2,0},{4,2},{6,4},{7,6},{5,7},{3,5},{1,3},{8,9},{10,8},{12,1... | collective-permute-start | bytes 786440 | tf_op jit(solution)/shard_map/ppermute | solution.py:329
  26.1 3.0 %work.2 = (bf16[16,4096]{1,0:T(8,128)(2,1)S(1)}, bf16[16,4096]{1,0:T(8,128)(2,1)S(1)}, bf16[16,4096]{1,0:T(8,128)(2,1)S(1)}, bf16[16,4096]{1,0:T(8,128)(2,1)S(1)...) custom-call(bf16[32,4096]{1,0:T(8,128)(2,1)S(1)} %get-tuple-element., ...), custom_call_target="tpu_custom_call" | custom-call | flops 3000000000 | tf_op jit(solution)/shard_map/work/pallas_call | solution.py:249
  29.2 0.5 collective-permute-done.8.refs_1_
  29.7 1.9 %collective-permute-done.7.refs_0_ = bf16[32,4096]{1,0:T(8,128)(2,1)S(1)} collective-permute-done((bf16[32,4096]{1,0:T(8,128)(2,1)S(1)}, bf16[32,4096]{1,0:T(8,128)(2,1)S(1)}, u32[]{:S(2)}, u32[]{:S(2)}) %collective-permute-start.7) | collective-permute-done | bytes 262176 | tf_op jit(solution)/shard_map/ppermute | solution.py:326
  31.8 1.9 %collective-permute-start.12 = (bf16[32,4096]{1,0:T(8,128)(2,1)S(1)}, bf16[32,4096]{1,0:T(8,128)(2,1)S(1)}, u32[]{:S(2)}, u32[]{:S(2)}) collective-permute-start(bf16[32,4096]{1,0:T(8,128)(2,1)S(1)} %collective-permute-done.8.refs_1_), channel_id=1, source_target_pairs={{0,1},{2,0},{4,2},{6,4},{7,6},{5,7},{3,5},{1,3},{8,9},{10,8},{12,1... | collective-permute-start | bytes 786440 | tf_op jit(solution)/shard_map/ppermute | solution.py:329
  33.7 1.7 %collective-permute-done.10.refs_3_ = bf16[32,4096]{1,0:T(8,128)(2,1)S(1)} collective-permute-done((bf16[32,4096]{1,0:T(8,128)(2,1)S(1)}, bf16[32,4096]{1,0:T(8,128)(2,1)S(1)}, u32[]{:S(2)}, u32[]{:S(2)}) %collective-permute-start.10) | collective-permute-done | bytes 262176 | tf_op jit(solution)/shard_map/ppermute | solution.py:329
  35.3 1.9 %collective-permute-done.9.refs_2_ = bf16[32,4096]{1,0:T(8,128)(2,1)S(1)} collective-permute-done((bf16[32,4096]{1,0:T(8,128)(2,1)S(1)}, bf16[32,4096]{1,0:T(8,128)(2,1)S(1)}, u32[]{:S(2)}, u32[]{:S(2)}) %collective-permute-start.9) | collective-permute-done | bytes 262176 | tf_op jit(solution)/shard_map/ppermute | solution.py:326
  37.3 1.6 %collective-permute-start.14 = (bf16[16,4096]{1,0:T(8,128)(2,1)S(1)}, bf16[16,4096]{1,0:T(8,128)(2,1)S(1)}, u32[]{:S(2)}, u32[]{:S(2)}) collective-permute-start(bf16[16,4096]{1,0:T(8,128)(2,1)S(1)} %slice.13), channel_id=1, source_target_pairs={{0,1},{2,0},{4,2},{6,4},{7,6},{5,7},{3,5},{1,3},{8,9},{10,8},{12,1... | collective-permute-start | bytes 393224 | tf_op jit(solution)/shard_map/ppermute | solution.py:329
  38.9 0.4 collective-permute-start.13
  39.4 3.5 %collective-permute-done.11.refs_4_ = bf16[32,4096]{1,0:T(8,128)(2,1)S(1)} collective-permute-done((bf16[32,4096]{1,0:T(8,128)(2,1)S(1)}, bf16[32,4096]{1,0:T(8,128)(2,1)S(1)}, u32[]{:S(2)}, u32[]{:S(2)}) %collective-permute-start.11) | collective-permute-done | bytes 262176 | tf_op jit(solution)/shard_map/ppermute | solution.py:326
  42.9 1.6 %collective-permute-start.16 = (bf16[16,4096]{1,0:T(8,128)(2,1)S(1)}, bf16[16,4096]{1,0:T(8,128)(2,1)S(1)}, u32[]{:S(2)}, u32[]{:S(2)}) collective-permute-start(bf16[16,4096]{1,0:T(8,128)(2,1)S(1)} %slice.15), channel_id=1, source_target_pairs={{0,1},{2,0},{4,2},{6,4},{7,6},{5,7},{3,5},{1,3},{8,9},{10,8},{12,1... | collective-permute-start | bytes 393224 | tf_op jit(solution)/shard_map/ppermute | solution.py:329
  44.6 0.4 collective-permute-start.15
  45.0 2.9 %collective-permute-done.16 = bf16[16,4096]{1,0:T(8,128)(2,1)S(1)} collective-permute-done((bf16[16,4096]{1,0:T(8,128)(2,1)S(1)}, bf16[16,4096]{1,0:T(8,128)(2,1)S(1)}, u32[]{:S(2)}, u32[]{:S(2)}) %collective-permute-start.16) | collective-permute-done | bytes 131104 | tf_op jit(solution)/shard_map/ppermute | solution.py:329
  47.9 1.6 %collective-permute-done.15 = bf16[16,4096]{1,0:T(8,128)(2,1)S(1)} collective-permute-done((bf16[16,4096]{1,0:T(8,128)(2,1)S(1)}, bf16[16,4096]{1,0:T(8,128)(2,1)S(1)}, u32[]{:S(2)}, u32[]{:S(2)}) %collective-permute-start.15) | collective-permute-done | bytes 131104 | tf_op jit(solution)/shard_map/ppermute | solution.py:326
  49.5 3.0 %work.3 = (bf16[16,4096]{1,0:T(8,128)(2,1)S(1)}, bf16[16,4096]{1,0:T(8,128)(2,1)S(1)}, bf16[16,4096]{1,0:T(8,128)(2,1)S(1)}, bf16[16,4096]{1,0:T(8,128)(2,1)S(1)...) custom-call(bf16[32,4096]{1,0:T(8,128)(2,1)S(1)} %collective-permute, ...), custom_call_target="tpu_custom_call" | custom-call | tf_op jit(solution)/shard_map/work/pallas_call | solution.py:249
  52.6 0.5 collective-permute-start.17
  53.1 1.6 %collective-permute-start.21 = (bf16[16,4096]{1,0:T(8,128)(2,1)S(1)}, bf16[16,4096]{1,0:T(8,128)(2,1)S(1)}, u32[]{:S(2)}, u32[]{:S(2)}) collective-permute-start(bf16[16,4096]{1,0:T(8,128)(2,1)S(1)} %get-tuple-element.70), channel_id=1, source_target_pairs={{0,1},{2,0},{4,2},{6,4},{7,6},{5,7},{3,5},{1,3},{8,9},{10,8},{12,1... | collective-permute-start | bytes 393224 | tf_op jit(solution)/shard_map/ppermute | solution.py:329
  54.7 0.5 collective-permute-start.24
  55.1 1.6 %collective-permute-start.28 = (bf16[16,4096]{1,0:T(8,128)(2,1)S(1)}, bf16[16,4096]{1,0:T(8,128)(2,1)S(1)}, u32[]{:S(2)}, u32[]{:S(2)}) collective-permute-start(bf16[16,4096]{1,0:T(8,128)(2,1)S(1)} %get-tuple-element.78), channel_id=1, source_target_pairs={{0,1},{2,0},{4,2},{6,4},{7,6},{5,7},{3,5},{1,3},{8,9},{10,8},{12,1... | collective-permute-start | bytes 393224 | tf_op jit(solution)/shard_map/ppermute | solution.py:329
  56.7 2.0 %collective-permute-done.17 = bf16[16,4096]{1,0:T(8,128)(2,1)S(1)} collective-permute-done((bf16[16,4096]{1,0:T(8,128)(2,1)S(1)}, bf16[16,4096]{1,0:T(8,128)(2,1)S(1)}, u32[]{:S(2)}, u32[]{:S(2)}) %collective-permute-start.17) | collective-permute-done | bytes 131104 | tf_op jit(solution)/shard_map/ppermute | solution.py:326
  58.8 0.5 collective-permute-start.18
  59.3 1.6 %collective-permute-start.22 = (bf16[16,4096]{1,0:T(8,128)(2,1)S(1)}, bf16[16,4096]{1,0:T(8,128)(2,1)S(1)}, u32[]{:S(2)}, u32[]{:S(2)}) collective-permute-start(bf16[16,4096]{1,0:T(8,128)(2,1)S(1)} %add_convert_fusion.7), channel_id=1, source_target_pairs={{0,1},{2,0},{4,2},{6,4},{7,6},{5,7},{3,5},{1,3},{8,9},{10,8},{12,1... | collective-permute-start | bytes 393224 | tf_op jit(solution)/shard_map/ppermute | solution.py:329
  60.9 0.6 collective-permute-done.24
  61.6 0.5 collective-permute-start.25
  62.1 1.6 %collective-permute-start.29 = (bf16[16,4096]{1,0:T(8,128)(2,1)S(1)}, bf16[16,4096]{1,0:T(8,128)(2,1)S(1)}, u32[]{:S(2)}, u32[]{:S(2)}) collective-permute-start(bf16[16,4096]{1,0:T(8,128)(2,1)S(1)} %add_convert_fusion.2), channel_id=1, source_target_pairs={{0,1},{2,0},{4,2},{6,4},{7,6},{5,7},{3,5},{1,3},{8,9},{10,8},{12,1... | collective-permute-start | bytes 393224 | tf_op jit(solution)/shard_map/ppermute | solution.py:329
  63.8 1.3 %collective-permute-done.18 = bf16[16,4096]{1,0:T(8,128)(2,1)S(1)} collective-permute-done((bf16[16,4096]{1,0:T(8,128)(2,1)S(1)}, bf16[16,4096]{1,0:T(8,128)(2,1)S(1)}, u32[]{:S(2)}, u32[]{:S(2)}) %collective-permute-start.18) | collective-permute-done | bytes 131104 | tf_op jit(solution)/shard_map/ppermute | solution.py:326
  65.1 0.6 collective-permute-start.19
  65.8 1.5 %collective-permute-start.23 = (bf16[16,4096]{1,0:T(8,128)(2,1)S(1)}, bf16[16,4096]{1,0:T(8,128)(2,1)S(1)}, u32[]{:S(2)}, u32[]{:S(2)}) collective-permute-start(bf16[16,4096]{1,0:T(8,128)(2,1)S(1)} %add_convert_fusion.6), channel_id=1, source_target_pairs={{0,1},{2,0},{4,2},{6,4},{7,6},{5,7},{3,5},{1,3},{8,9},{10,8},{12,1... | collective-permute-start | bytes 393224 | tf_op jit(solution)/shard_map/ppermute | solution.py:329
  67.3 0.6 collective-permute-done.25
  68.0 0.5 collective-permute-start.26
  68.5 1.6 %collective-permute-start.30 = (bf16[16,4096]{1,0:T(8,128)(2,1)S(1)}, bf16[16,4096]{1,0:T(8,128)(2,1)S(1)}, u32[]{:S(2)}, u32[]{:S(2)}) collective-permute-start(bf16[16,4096]{1,0:T(8,128)(2,1)S(1)} %add_convert_fusion.1), channel_id=1, source_target_pairs={{0,1},{2,0},{4,2},{6,4},{7,6},{5,7},{3,5},{1,3},{8,9},{10,8},{12,1... | collective-permute-start | bytes 393224 | tf_op jit(solution)/shard_map/ppermute | solution.py:329
  70.2 0.3 collective-permute-done.19
  70.5 0.5 collective-permute-start.20
  71.1 2.5 %collective-permute-done.30 = bf16[16,4096]{1,0:T(8,128)(2,1)S(1)} collective-permute-done((bf16[16,4096]{1,0:T(8,128)(2,1)S(1)}, bf16[16,4096]{1,0:T(8,128)(2,1)S(1)}, u32[]{:S(2)}, u32[]{:S(2)}) %collective-permute-start.30) | collective-permute-done | bytes 131104 | tf_op jit(solution)/shard_map/ppermute | solution.py:329
  73.7 1.7 %collective-permute-start.27 = (bf16[16,4096]{1,0:T(8,128)(2,1)S(1)}, bf16[16,4096]{1,0:T(8,128)(2,1)S(1)}, u32[]{:S(2)}, u32[]{:S(2)}) collective-permute-start(bf16[16,4096]{1,0:T(8,128)(2,1)S(1)} %add_convert_fusion.3), channel_id=1, source_target_pairs={{0,8},{8,0},{1,9},{9,1},{2,10},{10,2},{3,11},{11,3},{4,12},{12,4},... | collective-permute-start | bytes 393224 | tf_op jit(solution)/shard_map/ppermute | solution.py:381
  75.4 2.8 %weight_grads.1 = (bf16[192,4096]{1,0:T(8,128)(2,1)}, bf16[192,4096]{1,0:T(8,128)(2,1)}, bf16[192,4096]{1,0:T(8,128)(2,1)}) custom-call(bf16[128,192]{1,0:T(8,128)(2,1)S(1)} %get-tuple-element.79.refs_0_, bf16[128,192]{1,0:T(8,128)(2,1)S(1)} %get-tuple-element.80.refs_1_, bf16[128,192]{1,0:T(8,128)(2,1)S(1)} %get-tuple-element.81.refs_2_, ...), custom_call_target="tpu_custom_call" | custom-call | flops 3000000000 | tf_op jit(solution)/shard_map/weight_grads/pallas_call | solution.py:278
  78.3 1.3 %place.1 = bf16[128,4096]{1,0:T(8,128)(2,1)} custom-call(bf16[32,128]{1,0:T(8,128)(2,1)S(1)} %get-tuple-element.48.select_ref, bf16[16,4096]{1,0:T(8,128)(2,1)S(1)} %get-tuple-element.54.own_ref, bf16[16,4096]{1,0:T(8,128)(2,1)S(1)} %collective-permute-done.20.ahead_ref, bf16[16,4096]{1,0:T(8,128)(2,1)S(1)} %collective-permute-done.23.behind_ref, ...), custom_call_target="tpu_custom_call" | custom-call | tf_op jit(solution)/shard_map/place/pallas_call | solution.py:309
  (39 shorter events, 1.4 us)
Async XLA Ops:
  2.6 3.2 %collective-permute-start = (bf16[32,4096]{1,0:T(8,128)(2,1)S(1)}, bf16[32,4096]{1,0:T(8,128)(2,1)S(1)}, u32[]{:S(2)}, u32[]{:S(2)}) collective-permute-start(bf16[32,4096]{1,0:T(8,128)(2,1)S(1)} %get-tuple-element.50), channel_id=1, source_target_pairs={{0,8},{8,0},{1,9},{9,1},{2,10},{10,2},{3,11},{11,3},{4,12},{12,4},... | collective-permute-start | bytes 786440 | tf_op jit(solution)/shard_map/ppermute | solution.py:337
  3.1 9.8 %collective-permute-start.2 = (bf16[32,4096]{1,0:T(8,128)(2,1)S(1)}, bf16[32,4096]{1,0:T(8,128)(2,1)S(1)}, u32[]{:S(2)}, u32[]{:S(2)}) collective-permute-start(bf16[32,4096]{1,0:T(8,128)(2,1)S(1)} %get-tuple-element.49.refs_0_), channel_id=1, source_target_pairs={{0,1},{2,0},{4,2},{6,4},{7,6},{5,7},{3,5},{1,3},{8,9},{10,8},{12,1... | collective-permute-start | bytes 786440 | tf_op jit(solution)/shard_map/ppermute | solution.py:329
  5.6 9.1 %collective-permute-start.1 = (bf16[32,4096]{1,0:T(8,128)(2,1)S(1)}, bf16[32,4096]{1,0:T(8,128)(2,1)S(1)}, u32[]{:S(2)}, u32[]{:S(2)}) collective-permute-start(bf16[32,4096]{1,0:T(8,128)(2,1)S(1)} %get-tuple-element.49.refs_0_), channel_id=1, source_target_pairs={{0,2},{2,4},{4,6},{6,7},{7,5},{5,3},{3,1},{1,0},{8,10},{10,12},{12... | collective-permute-start | bytes 786440 | tf_op jit(solution)/shard_map/ppermute | solution.py:326
  5.8 12.7 %collective-permute-start.4 = (bf16[32,4096]{1,0:T(8,128)(2,1)S(1)}, bf16[32,4096]{1,0:T(8,128)(2,1)S(1)}, u32[]{:S(2)}, u32[]{:S(2)}) collective-permute-start(bf16[32,4096]{1,0:T(8,128)(2,1)S(1)} %collective-permute-done.refs_1_), channel_id=1, source_target_pairs={{0,1},{2,0},{4,2},{6,4},{7,6},{5,7},{3,5},{1,3},{8,9},{10,8},{12,1... | collective-permute-start | bytes 786440 | tf_op jit(solution)/shard_map/ppermute | solution.py:329
  7.7 12.7 %collective-permute-start.3 = (bf16[32,4096]{1,0:T(8,128)(2,1)S(1)}, bf16[32,4096]{1,0:T(8,128)(2,1)S(1)}, u32[]{:S(2)}, u32[]{:S(2)}) collective-permute-start(bf16[32,4096]{1,0:T(8,128)(2,1)S(1)} %collective-permute-done.refs_1_), channel_id=1, source_target_pairs={{0,2},{2,4},{4,6},{6,7},{7,5},{5,3},{3,1},{1,0},{8,10},{10,12},{12... | collective-permute-start | bytes 786440 | tf_op jit(solution)/shard_map/ppermute | solution.py:326
  12.9 11.2 %collective-permute-start.6 = (bf16[32,4096]{1,0:T(8,128)(2,1)S(1)}, bf16[32,4096]{1,0:T(8,128)(2,1)S(1)}, u32[]{:S(2)}, u32[]{:S(2)}) collective-permute-start(bf16[32,4096]{1,0:T(8,128)(2,1)S(1)} %collective-permute-done.2.refs_3_), channel_id=1, source_target_pairs={{0,1},{2,0},{4,2},{6,4},{7,6},{5,7},{3,5},{1,3},{8,9},{10,8},{12,1... | collective-permute-start | bytes 786440 | tf_op jit(solution)/shard_map/ppermute | solution.py:329
  14.8 11.2 %collective-permute-start.5 = (bf16[32,4096]{1,0:T(8,128)(2,1)S(1)}, bf16[32,4096]{1,0:T(8,128)(2,1)S(1)}, u32[]{:S(2)}, u32[]{:S(2)}) collective-permute-start(bf16[32,4096]{1,0:T(8,128)(2,1)S(1)} %collective-permute-done.1.refs_2_), channel_id=1, source_target_pairs={{0,2},{2,4},{4,6},{6,7},{7,5},{5,3},{3,1},{1,0},{8,10},{10,12},{12... | collective-permute-start | bytes 786440 | tf_op jit(solution)/shard_map/ppermute | solution.py:326
  20.4 11.2 %collective-permute-start.7 = (bf16[32,4096]{1,0:T(8,128)(2,1)S(1)}, bf16[32,4096]{1,0:T(8,128)(2,1)S(1)}, u32[]{:S(2)}, u32[]{:S(2)}) collective-permute-start(bf16[32,4096]{1,0:T(8,128)(2,1)S(1)} %collective-permute-done.3.refs_4_), channel_id=1, source_target_pairs={{0,2},{2,4},{4,6},{6,7},{7,5},{5,3},{3,1},{1,0},{8,10},{10,12},{12... | collective-permute-start | bytes 786440 | tf_op jit(solution)/shard_map/ppermute | solution.py:326
  20.5 9.2 %collective-permute-start.8 = (bf16[32,4096]{1,0:T(8,128)(2,1)S(1)}, bf16[32,4096]{1,0:T(8,128)(2,1)S(1)}, u32[]{:S(2)}, u32[]{:S(2)}) collective-permute-start(bf16[32,4096]{1,0:T(8,128)(2,1)S(1)} %collective-permute-done.4.refs_5_), channel_id=1, source_target_pairs={{0,1},{2,0},{4,2},{6,4},{7,6},{5,7},{3,5},{1,3},{8,9},{10,8},{12,1... | collective-permute-start | bytes 786440 | tf_op jit(solution)/shard_map/ppermute | solution.py:329
  24.1 11.2 %collective-permute-start.10 = (bf16[32,4096]{1,0:T(8,128)(2,1)S(1)}, bf16[32,4096]{1,0:T(8,128)(2,1)S(1)}, u32[]{:S(2)}, u32[]{:S(2)}) collective-permute-start(bf16[32,4096]{1,0:T(8,128)(2,1)S(1)} %collective-permute-done.6.refs_7_), channel_id=1, source_target_pairs={{0,1},{2,0},{4,2},{6,4},{7,6},{5,7},{3,5},{1,3},{8,9},{10,8},{12,1... | collective-permute-start | bytes 786440 | tf_op jit(solution)/shard_map/ppermute | solution.py:329
  26.0 11.2 %collective-permute-start.9 = (bf16[32,4096]{1,0:T(8,128)(2,1)S(1)}, bf16[32,4096]{1,0:T(8,128)(2,1)S(1)}, u32[]{:S(2)}, u32[]{:S(2)}) collective-permute-start(bf16[32,4096]{1,0:T(8,128)(2,1)S(1)} %collective-permute-done.5.refs_6_), channel_id=1, source_target_pairs={{0,2},{2,4},{4,6},{6,7},{7,5},{5,3},{3,1},{1,0},{8,10},{10,12},{12... | collective-permute-start | bytes 786440 | tf_op jit(solution)/shard_map/ppermute | solution.py:326
  31.7 11.2 %collective-permute-start.11 = (bf16[32,4096]{1,0:T(8,128)(2,1)S(1)}, bf16[32,4096]{1,0:T(8,128)(2,1)S(1)}, u32[]{:S(2)}, u32[]{:S(2)}) collective-permute-start(bf16[32,4096]{1,0:T(8,128)(2,1)S(1)} %collective-permute-done.7.refs_0_), channel_id=1, source_target_pairs={{0,2},{2,4},{4,6},{6,7},{7,5},{5,3},{3,1},{1,0},{8,10},{10,12},{12... | collective-permute-start | bytes 786440 | tf_op jit(solution)/shard_map/ppermute | solution.py:326
  31.8 11.1 %collective-permute-start.12 = (bf16[32,4096]{1,0:T(8,128)(2,1)S(1)}, bf16[32,4096]{1,0:T(8,128)(2,1)S(1)}, u32[]{:S(2)}, u32[]{:S(2)}) collective-permute-start(bf16[32,4096]{1,0:T(8,128)(2,1)S(1)} %collective-permute-done.8.refs_1_), channel_id=1, source_target_pairs={{0,1},{2,0},{4,2},{6,4},{7,6},{5,7},{3,5},{1,3},{8,9},{10,8},{12,1... | collective-permute-start | bytes 786440 | tf_op jit(solution)/shard_map/ppermute | solution.py:329
  37.3 7.7 %collective-permute-start.14 = (bf16[16,4096]{1,0:T(8,128)(2,1)S(1)}, bf16[16,4096]{1,0:T(8,128)(2,1)S(1)}, u32[]{:S(2)}, u32[]{:S(2)}) collective-permute-start(bf16[16,4096]{1,0:T(8,128)(2,1)S(1)} %slice.13), channel_id=1, source_target_pairs={{0,1},{2,0},{4,2},{6,4},{7,6},{5,7},{3,5},{1,3},{8,9},{10,8},{12,1... | collective-permute-start | bytes 393224 | tf_op jit(solution)/shard_map/ppermute | solution.py:329
  38.9 6.1 %collective-permute-start.13 = (bf16[16,4096]{1,0:T(8,128)(2,1)S(1)}, bf16[16,4096]{1,0:T(8,128)(2,1)S(1)}, u32[]{:S(2)}, u32[]{:S(2)}) collective-permute-start(bf16[16,4096]{1,0:T(8,128)(2,1)S(1)} %slice.12), channel_id=1, source_target_pairs={{0,2},{2,4},{4,6},{6,7},{7,5},{5,3},{3,1},{1,0},{8,10},{10,12},{12... | collective-permute-start | bytes 393224 | tf_op jit(solution)/shard_map/ppermute | solution.py:326
  42.9 5.0 %collective-permute-start.16 = (bf16[16,4096]{1,0:T(8,128)(2,1)S(1)}, bf16[16,4096]{1,0:T(8,128)(2,1)S(1)}, u32[]{:S(2)}, u32[]{:S(2)}) collective-permute-start(bf16[16,4096]{1,0:T(8,128)(2,1)S(1)} %slice.15), channel_id=1, source_target_pairs={{0,1},{2,0},{4,2},{6,4},{7,6},{5,7},{3,5},{1,3},{8,9},{10,8},{12,1... | collective-permute-start | bytes 393224 | tf_op jit(solution)/shard_map/ppermute | solution.py:329
  44.6 5.0 %collective-permute-start.15 = (bf16[16,4096]{1,0:T(8,128)(2,1)S(1)}, bf16[16,4096]{1,0:T(8,128)(2,1)S(1)}, u32[]{:S(2)}, u32[]{:S(2)}) collective-permute-start(bf16[16,4096]{1,0:T(8,128)(2,1)S(1)} %slice.14), channel_id=1, source_target_pairs={{0,2},{2,4},{4,6},{6,7},{7,5},{5,3},{3,1},{1,0},{8,10},{10,12},{12... | collective-permute-start | bytes 393224 | tf_op jit(solution)/shard_map/ppermute | solution.py:326
  52.6 6.2 %collective-permute-start.17 = (bf16[16,4096]{1,0:T(8,128)(2,1)S(1)}, bf16[16,4096]{1,0:T(8,128)(2,1)S(1)}, u32[]{:S(2)}, u32[]{:S(2)}) collective-permute-start(bf16[16,4096]{1,0:T(8,128)(2,1)S(1)} %get-tuple-element.67), channel_id=1, source_target_pairs={{0,2},{2,4},{4,6},{6,7},{7,5},{5,3},{3,1},{1,0},{8,10},{10,12},{12... | collective-permute-start | bytes 393224 | tf_op jit(solution)/shard_map/ppermute | solution.py:326
  53.1 6.2 %collective-permute-start.21 = (bf16[16,4096]{1,0:T(8,128)(2,1)S(1)}, bf16[16,4096]{1,0:T(8,128)(2,1)S(1)}, u32[]{:S(2)}, u32[]{:S(2)}) collective-permute-start(bf16[16,4096]{1,0:T(8,128)(2,1)S(1)} %get-tuple-element.70), channel_id=1, source_target_pairs={{0,1},{2,0},{4,2},{6,4},{7,6},{5,7},{3,5},{1,3},{8,9},{10,8},{12,1... | collective-permute-start | bytes 393224 | tf_op jit(solution)/shard_map/ppermute | solution.py:329
  54.7 6.9 %collective-permute-start.24 = (bf16[16,4096]{1,0:T(8,128)(2,1)S(1)}, bf16[16,4096]{1,0:T(8,128)(2,1)S(1)}, u32[]{:S(2)}, u32[]{:S(2)}) collective-permute-start(bf16[16,4096]{1,0:T(8,128)(2,1)S(1)} %get-tuple-element.74), channel_id=1, source_target_pairs={{0,2},{2,4},{4,6},{6,7},{7,5},{5,3},{3,1},{1,0},{8,10},{10,12},{12... | collective-permute-start | bytes 393224 | tf_op jit(solution)/shard_map/ppermute | solution.py:326
  55.1 7.0 %collective-permute-start.28 = (bf16[16,4096]{1,0:T(8,128)(2,1)S(1)}, bf16[16,4096]{1,0:T(8,128)(2,1)S(1)}, u32[]{:S(2)}, u32[]{:S(2)}) collective-permute-start(bf16[16,4096]{1,0:T(8,128)(2,1)S(1)} %get-tuple-element.78), channel_id=1, source_target_pairs={{0,1},{2,0},{4,2},{6,4},{7,6},{5,7},{3,5},{1,3},{8,9},{10,8},{12,1... | collective-permute-start | bytes 393224 | tf_op jit(solution)/shard_map/ppermute | solution.py:329
  58.8 6.3 %collective-permute-start.18 = (bf16[16,4096]{1,0:T(8,128)(2,1)S(1)}, bf16[16,4096]{1,0:T(8,128)(2,1)S(1)}, u32[]{:S(2)}, u32[]{:S(2)}) collective-permute-start(bf16[16,4096]{1,0:T(8,128)(2,1)S(1)} %add_convert_fusion.10), channel_id=1, source_target_pairs={{0,2},{2,4},{4,6},{6,7},{7,5},{5,3},{3,1},{1,0},{8,10},{10,12},{12... | collective-permute-start | bytes 393224 | tf_op jit(solution)/shard_map/ppermute | solution.py:326
  59.3 6.4 %collective-permute-start.22 = (bf16[16,4096]{1,0:T(8,128)(2,1)S(1)}, bf16[16,4096]{1,0:T(8,128)(2,1)S(1)}, u32[]{:S(2)}, u32[]{:S(2)}) collective-permute-start(bf16[16,4096]{1,0:T(8,128)(2,1)S(1)} %add_convert_fusion.7), channel_id=1, source_target_pairs={{0,1},{2,0},{4,2},{6,4},{7,6},{5,7},{3,5},{1,3},{8,9},{10,8},{12,1... | collective-permute-start | bytes 393224 | tf_op jit(solution)/shard_map/ppermute | solution.py:329
  61.6 6.4 %collective-permute-start.25 = (bf16[16,4096]{1,0:T(8,128)(2,1)S(1)}, bf16[16,4096]{1,0:T(8,128)(2,1)S(1)}, u32[]{:S(2)}, u32[]{:S(2)}) collective-permute-start(bf16[16,4096]{1,0:T(8,128)(2,1)S(1)} %add_convert_fusion.5), channel_id=1, source_target_pairs={{0,2},{2,4},{4,6},{6,7},{7,5},{5,3},{3,1},{1,0},{8,10},{10,12},{12... | collective-permute-start | bytes 393224 | tf_op jit(solution)/shard_map/ppermute | solution.py:326
  62.1 6.4 %collective-permute-start.29 = (bf16[16,4096]{1,0:T(8,128)(2,1)S(1)}, bf16[16,4096]{1,0:T(8,128)(2,1)S(1)}, u32[]{:S(2)}, u32[]{:S(2)}) collective-permute-start(bf16[16,4096]{1,0:T(8,128)(2,1)S(1)} %add_convert_fusion.2), channel_id=1, source_target_pairs={{0,1},{2,0},{4,2},{6,4},{7,6},{5,7},{3,5},{1,3},{8,9},{10,8},{12,1... | collective-permute-start | bytes 393224 | tf_op jit(solution)/shard_map/ppermute | solution.py:329
  65.1 5.4 %collective-permute-start.19 = (bf16[16,4096]{1,0:T(8,128)(2,1)S(1)}, bf16[16,4096]{1,0:T(8,128)(2,1)S(1)}, u32[]{:S(2)}, u32[]{:S(2)}) collective-permute-start(bf16[16,4096]{1,0:T(8,128)(2,1)S(1)} %add_convert_fusion.9), channel_id=1, source_target_pairs={{0,2},{2,4},{4,6},{6,7},{7,5},{5,3},{3,1},{1,0},{8,10},{10,12},{12... | collective-permute-start | bytes 393224 | tf_op jit(solution)/shard_map/ppermute | solution.py:326
  65.8 12.5 %collective-permute-start.23 = (bf16[16,4096]{1,0:T(8,128)(2,1)S(1)}, bf16[16,4096]{1,0:T(8,128)(2,1)S(1)}, u32[]{:S(2)}, u32[]{:S(2)}) collective-permute-start(bf16[16,4096]{1,0:T(8,128)(2,1)S(1)} %add_convert_fusion.6), channel_id=1, source_target_pairs={{0,1},{2,0},{4,2},{6,4},{7,6},{5,7},{3,5},{1,3},{8,9},{10,8},{12,1... | collective-permute-start | bytes 393224 | tf_op jit(solution)/shard_map/ppermute | solution.py:329
  68.0 5.7 %collective-permute-start.26 = (bf16[16,4096]{1,0:T(8,128)(2,1)S(1)}, bf16[16,4096]{1,0:T(8,128)(2,1)S(1)}, u32[]{:S(2)}, u32[]{:S(2)}) collective-permute-start(bf16[16,4096]{1,0:T(8,128)(2,1)S(1)} %add_convert_fusion.4), channel_id=1, source_target_pairs={{0,2},{2,4},{4,6},{6,7},{7,5},{5,3},{3,1},{1,0},{8,10},{10,12},{12... | collective-permute-start | bytes 393224 | tf_op jit(solution)/shard_map/ppermute | solution.py:326
  68.5 5.0 %collective-permute-start.30 = (bf16[16,4096]{1,0:T(8,128)(2,1)S(1)}, bf16[16,4096]{1,0:T(8,128)(2,1)S(1)}, u32[]{:S(2)}, u32[]{:S(2)}) collective-permute-start(bf16[16,4096]{1,0:T(8,128)(2,1)S(1)} %add_convert_fusion.1), channel_id=1, source_target_pairs={{0,1},{2,0},{4,2},{6,4},{7,6},{5,7},{3,5},{1,3},{8,9},{10,8},{12,1... | collective-permute-start | bytes 393224 | tf_op jit(solution)/shard_map/ppermute | solution.py:329
  70.5 7.8 %collective-permute-start.20 = (bf16[16,4096]{1,0:T(8,128)(2,1)S(1)}, bf16[16,4096]{1,0:T(8,128)(2,1)S(1)}, u32[]{:S(2)}, u32[]{:S(2)}) collective-permute-start(bf16[16,4096]{1,0:T(8,128)(2,1)S(1)} %add_convert_fusion.8), channel_id=1, source_target_pairs={{0,2},{2,4},{4,6},{6,7},{7,5},{5,3},{3,1},{1,0},{8,10},{10,12},{12... | collective-permute-start | bytes 393224 | tf_op jit(solution)/shard_map/ppermute | solution.py:326
  73.6 4.7 %collective-permute-start.31 = (bf16[16,4096]{1,0:T(8,128)(2,1)S(1)}, bf16[16,4096]{1,0:T(8,128)(2,1)S(1)}, u32[]{:S(2)}, u32[]{:S(2)}) collective-permute-start(bf16[16,4096]{1,0:T(8,128)(2,1)S(1)} %add_convert_fusion), channel_id=1, source_target_pairs={{0,9},{2,8},{4,10},{6,12},{7,14},{5,15},{3,13},{1,11},{8,1},{10,0}... | collective-permute-start | bytes 393224 | tf_op jit(solution)/shard_map/ppermute | solution.py:334
  73.7 4.6 %collective-permute-start.27 = (bf16[16,4096]{1,0:T(8,128)(2,1)S(1)}, bf16[16,4096]{1,0:T(8,128)(2,1)S(1)}, u32[]{:S(2)}, u32[]{:S(2)}) collective-permute-start(bf16[16,4096]{1,0:T(8,128)(2,1)S(1)} %add_convert_fusion.3), channel_id=1, source_target_pairs={{0,8},{8,0},{1,9},{9,1},{2,10},{10,2},{3,11},{11,3},{4,12},{12,4},... | collective-permute-start | bytes 393224 | tf_op jit(solution)/shard_map/ppermute | solution.py:381

commit v6 on v5

--- a/solution.py
+++ b/solution.py
@@ -350,8 +350,6 @@
     near_go, near_back, far_go, far_back = near, near, far, far
     for s in range(1, half):
         near_go, near_back = go(near_go), back(near_back)
-        if s == 2:
-            far_go, far_back = after(far_go, weights[0]), after(far_back, weights[0])
         far_go, far_back = go(far_go), back(far_back)
         rows.update({(-s, 0): near_go, (s, 0): near_back, (-s, 1): far_go, (s, 1): far_back})
         if s == half - 2:

time: 79.8 us -> 79.8 us (level)
    ppermute x14, waiting for transfers between devices: 15.5 us -> 17.4 us  [back(): return lax.ppermute(x, 'local', behind)]
    ppermute x15, waiting for transfers between devices: 15.9 us -> 14 us  [go(): return lax.ppermute(x, 'local', ahead)]
  transfers between devices with their start and end apart: 32 -> 32, of which waited for: 17 -> 16; matrix products, arithmetic and copies ran while one was open for 1% -> 1% of each run, Pallas kernels for 10% -> 10%
where the time goes in v6:
time: 79.8 us; the launch traced here: 79.6 us
  starting transfers between devices  32.4 us (41%)
  waiting for transfers between devices  31.5 us (39%)
  Pallas kernels  14.4 us (18%)
  between operations  0.82 us (1%)
    ppermute x14, starting transfers between devices, back(): return lax.ppermute(x, 'local', behind)  24.8 us
    ppermute x14, waiting for transfers between devices, back(): return lax.ppermute(x, 'local', behind)  17.4 us
    ppermute x15, waiting for transfers between devices, go(): return lax.ppermute(x, 'local', ahead)  14 us
    pallas_call x2, Pallas kernels, work(): pl.pallas_call(functools.partial(work_kernel, n), in_specs=[IN_VMEM] * (n...  6.03 us
    ppermute x15, starting transfers between devices, go(): return lax.ppermute(x, 'local', ahead)  5.35 us
    pallas_call x1, Pallas kernels, weight_grads(): pl.pallas_call(functools.partial(weight_grads_kernel, n), in_specs=[IN_VM...  2.84 us
    pallas_call x1, Pallas kernels, load(): pl.pallas_call(functools.partial(load_kernel, n), in_specs=[pl.BlockSpec(...  2.38 us
    pallas_call x1, Pallas kernels, pick(): pl.pallas_call(pick_kernel, in_specs=[pl.BlockSpec(memory_space=pltpu.HBM...  1.91 us
  transfers between devices with their start and end apart: 32, of which 16 were waited for; matrix products, arithmetic and copies ran while one was open for 1% of the time, Pallas kernels for 10%

profile of v6, /device:TPU:0, one launch (start us, length us, event | category | flops | bytes accessed | tf_op | source)
XLA Modules:
  0.0 79.6 jit_solution(13899588494535923567)
XLA Ops:
  0.6 1.9 %pick.1 = (bf16[32,4096]{1,0:T(8,128)(2,1)S(1)}, bf16[32,4096]{1,0:T(8,128)(2,1)S(1)}, bf16[32,128]{1,0:T(8,128)(2,1)S(1)}) custom-call(s32[8,128]{1,0:T(8,128)} %bitcast.2, f32[8,128]{1,0:T(8,128)} %bitcast.3, s32[1,128]{1,0:T(1,128)} %samples_hbm.1, bf16[128,4096]{1,0:T(8,128)(2,1)} %grad_hbm.1, bf16[128,4096]{1,0:T(8,128)(2,1)} %in_hbm.1), custom_call_target="tpu_custom_call" | custom-call | tf_op jit(solution)/shard_map/pick/pallas_call | solution.py:186
  2.6 0.5 collective-permute-start
  3.1 2.6 %collective-permute-start.2 = (bf16[32,4096]{1,0:T(8,128)(2,1)S(1)}, bf16[32,4096]{1,0:T(8,128)(2,1)S(1)}, u32[]{:S(2)}, u32[]{:S(2)}) collective-permute-start(bf16[32,4096]{1,0:T(8,128)(2,1)S(1)} %get-tuple-element.47.refs_0_), channel_id=1, source_target_pairs={{0,1},{2,0},{4,2},{6,4},{7,6},{5,7},{3,5},{1,3},{8,9},{10,8},{12,1... | collective-permute-start | bytes 786440 | tf_op jit(solution)/shard_map/ppermute | solution.py:329
  5.6 0.1 collective-permute-start.1
  5.8 1.9 %collective-permute-start.4 = (bf16[32,4096]{1,0:T(8,128)(2,1)S(1)}, bf16[32,4096]{1,0:T(8,128)(2,1)S(1)}, u32[]{:S(2)}, u32[]{:S(2)}) collective-permute-start(bf16[32,4096]{1,0:T(8,128)(2,1)S(1)} %collective-permute-done.refs_1_), channel_id=1, source_target_pairs={{0,1},{2,0},{4,2},{6,4},{7,6},{5,7},{3,5},{1,3},{8,9},{10,8},{12,1... | collective-permute-start | bytes 786440 | tf_op jit(solution)/shard_map/ppermute | solution.py:329
  7.8 5.0 %collective-permute-done.2.refs_3_ = bf16[32,4096]{1,0:T(8,128)(2,1)S(1)} collective-permute-done((bf16[32,4096]{1,0:T(8,128)(2,1)S(1)}, bf16[32,4096]{1,0:T(8,128)(2,1)S(1)}, u32[]{:S(2)}, u32[]{:S(2)}) %collective-permute-start.2) | collective-permute-done | bytes 262176 | tf_op jit(solution)/shard_map/ppermute | solution.py:329
  12.9 1.9 %collective-permute-start.6 = (bf16[32,4096]{1,0:T(8,128)(2,1)S(1)}, bf16[32,4096]{1,0:T(8,128)(2,1)S(1)}, u32[]{:S(2)}, u32[]{:S(2)}) collective-permute-start(bf16[32,4096]{1,0:T(8,128)(2,1)S(1)} %collective-permute-done.2.refs_3_), channel_id=1, source_target_pairs={{0,1},{2,0},{4,2},{6,4},{7,6},{5,7},{3,5},{1,3},{8,9},{10,8},{12,1... | collective-permute-start | bytes 786440 | tf_op jit(solution)/shard_map/ppermute | solution.py:329
  14.9 2.4 %load.1 = (bf16[192,4096]{1,0:T(8,128)(2,1)S(1)}, bf16[192,4096]{1,0:T(8,128)(2,1)S(1)}, bf16[192,4096]{1,0:T(8,128)(2,1)S(1)}) custom-call(bf16[192,4096]{1,0:T(8,128)(2,1)} %refs_0_.1, bf16[192,4096]{1,0:T(8,128)(2,1)} %refs_1_.1, bf16[192,4096]{1,0:T(8,128)(2,1)} %refs_2_.1), custom_call_target="tpu_custom_call" | custom-call | tf_op jit(solution)/shard_map/load/pallas_call | solution.py:207
  17.3 1.2 %collective-permute-done.4.refs_5_ = bf16[32,4096]{1,0:T(8,128)(2,1)S(1)} collective-permute-done((bf16[32,4096]{1,0:T(8,128)(2,1)S(1)}, bf16[32,4096]{1,0:T(8,128)(2,1)S(1)}, u32[]{:S(2)}, u32[]{:S(2)}) %collective-permute-start.4) | collective-permute-done | bytes 262176 | tf_op jit(solution)/shard_map/ppermute | solution.py:329
  18.5 1.9 %collective-permute-start.8 = (bf16[32,4096]{1,0:T(8,128)(2,1)S(1)}, bf16[32,4096]{1,0:T(8,128)(2,1)S(1)}, u32[]{:S(2)}, u32[]{:S(2)}) collective-permute-start(bf16[32,4096]{1,0:T(8,128)(2,1)S(1)} %collective-permute-done.4.refs_5_), channel_id=1, source_target_pairs={{0,1},{2,0},{4,2},{6,4},{7,6},{5,7},{3,5},{1,3},{8,9},{10,8},{12,1... | collective-permute-start | bytes 786440 | tf_op jit(solution)/shard_map/ppermute | solution.py:329
  20.5 3.6 %collective-permute-done.6.refs_7_ = bf16[32,4096]{1,0:T(8,128)(2,1)S(1)} collective-permute-done((bf16[32,4096]{1,0:T(8,128)(2,1)S(1)}, bf16[32,4096]{1,0:T(8,128)(2,1)S(1)}, u32[]{:S(2)}, u32[]{:S(2)}) %collective-permute-start.6) | collective-permute-done | bytes 262176 | tf_op jit(solution)/shard_map/ppermute | solution.py:329
  24.1 1.9 %collective-permute-start.10 = (bf16[32,4096]{1,0:T(8,128)(2,1)S(1)}, bf16[32,4096]{1,0:T(8,128)(2,1)S(1)}, u32[]{:S(2)}, u32[]{:S(2)}) collective-permute-start(bf16[32,4096]{1,0:T(8,128)(2,1)S(1)} %collective-permute-done.6.refs_7_), channel_id=1, source_target_pairs={{0,1},{2,0},{4,2},{6,4},{7,6},{5,7},{3,5},{1,3},{8,9},{10,8},{12,1... | collective-permute-start | bytes 786440 | tf_op jit(solution)/shard_map/ppermute | solution.py:329
  26.1 3.0 %work.2 = (bf16[16,4096]{1,0:T(8,128)(2,1)S(1)}, bf16[16,4096]{1,0:T(8,128)(2,1)S(1)}, bf16[16,4096]{1,0:T(8,128)(2,1)S(1)}, bf16[16,4096]{1,0:T(8,128)(2,1)S(1)...) custom-call(bf16[32,4096]{1,0:T(8,128)(2,1)S(1)} %get-tuple-element., ...), custom_call_target="tpu_custom_call" | custom-call | flops 3000000000 | tf_op jit(solution)/shard_map/work/pallas_call | solution.py:249
  29.2 0.5 collective-permute-done.8.refs_1_
  29.7 1.9 %collective-permute-done.7.refs_0_ = bf16[32,4096]{1,0:T(8,128)(2,1)S(1)} collective-permute-done((bf16[32,4096]{1,0:T(8,128)(2,1)S(1)}, bf16[32,4096]{1,0:T(8,128)(2,1)S(1)}, u32[]{:S(2)}, u32[]{:S(2)}) %collective-permute-start.7) | collective-permute-done | bytes 262176 | tf_op jit(solution)/shard_map/ppermute | solution.py:326
  31.8 1.9 %collective-permute-start.12 = (bf16[32,4096]{1,0:T(8,128)(2,1)S(1)}, bf16[32,4096]{1,0:T(8,128)(2,1)S(1)}, u32[]{:S(2)}, u32[]{:S(2)}) collective-permute-start(bf16[32,4096]{1,0:T(8,128)(2,1)S(1)} %collective-permute-done.8.refs_1_), channel_id=1, source_target_pairs={{0,1},{2,0},{4,2},{6,4},{7,6},{5,7},{3,5},{1,3},{8,9},{10,8},{12,1... | collective-permute-start | bytes 786440 | tf_op jit(solution)/shard_map/ppermute | solution.py:329
  33.7 1.7 %collective-permute-done.10.refs_3_ = bf16[32,4096]{1,0:T(8,128)(2,1)S(1)} collective-permute-done((bf16[32,4096]{1,0:T(8,128)(2,1)S(1)}, bf16[32,4096]{1,0:T(8,128)(2,1)S(1)}, u32[]{:S(2)}, u32[]{:S(2)}) %collective-permute-start.10) | collective-permute-done | bytes 262176 | tf_op jit(solution)/shard_map/ppermute | solution.py:329
  35.3 1.9 %collective-permute-done.9.refs_2_ = bf16[32,4096]{1,0:T(8,128)(2,1)S(1)} collective-permute-done((bf16[32,4096]{1,0:T(8,128)(2,1)S(1)}, bf16[32,4096]{1,0:T(8,128)(2,1)S(1)}, u32[]{:S(2)}, u32[]{:S(2)}) %collective-permute-start.9) | collective-permute-done | bytes 262176 | tf_op jit(solution)/shard_map/ppermute | solution.py:326
  37.3 1.6 %collective-permute-start.14 = (bf16[16,4096]{1,0:T(8,128)(2,1)S(1)}, bf16[16,4096]{1,0:T(8,128)(2,1)S(1)}, u32[]{:S(2)}, u32[]{:S(2)}) collective-permute-start(bf16[16,4096]{1,0:T(8,128)(2,1)S(1)} %slice.13), channel_id=1, source_target_pairs={{0,1},{2,0},{4,2},{6,4},{7,6},{5,7},{3,5},{1,3},{8,9},{10,8},{12,1... | collective-permute-start | bytes 393224 | tf_op jit(solution)/shard_map/ppermute | solution.py:329
  38.9 0.4 collective-permute-start.13
  39.4 3.5 %collective-permute-done.11.refs_4_ = bf16[32,4096]{1,0:T(8,128)(2,1)S(1)} collective-permute-done((bf16[32,4096]{1,0:T(8,128)(2,1)S(1)}, bf16[32,4096]{1,0:T(8,128)(2,1)S(1)}, u32[]{:S(2)}, u32[]{:S(2)}) %collective-permute-start.11) | collective-permute-done | bytes 262176 | tf_op jit(solution)/shard_map/ppermute | solution.py:326
  42.9 1.6 %collective-permute-start.16 = (bf16[16,4096]{1,0:T(8,128)(2,1)S(1)}, bf16[16,4096]{1,0:T(8,128)(2,1)S(1)}, u32[]{:S(2)}, u32[]{:S(2)}) collective-permute-start(bf16[16,4096]{1,0:T(8,128)(2,1)S(1)} %slice.15), channel_id=1, source_target_pairs={{0,1},{2,0},{4,2},{6,4},{7,6},{5,7},{3,5},{1,3},{8,9},{10,8},{12,1... | collective-permute-start | bytes 393224 | tf_op jit(solution)/shard_map/ppermute | solution.py:329
  44.6 0.4 collective-permute-start.15
  45.0 2.9 %collective-permute-done.16 = bf16[16,4096]{1,0:T(8,128)(2,1)S(1)} collective-permute-done((bf16[16,4096]{1,0:T(8,128)(2,1)S(1)}, bf16[16,4096]{1,0:T(8,128)(2,1)S(1)}, u32[]{:S(2)}, u32[]{:S(2)}) %collective-permute-start.16) | collective-permute-done | bytes 131104 | tf_op jit(solution)/shard_map/ppermute | solution.py:329
  47.9 1.6 %collective-permute-done.15 = bf16[16,4096]{1,0:T(8,128)(2,1)S(1)} collective-permute-done((bf16[16,4096]{1,0:T(8,128)(2,1)S(1)}, bf16[16,4096]{1,0:T(8,128)(2,1)S(1)}, u32[]{:S(2)}, u32[]{:S(2)}) %collective-permute-start.15) | collective-permute-done | bytes 131104 | tf_op jit(solution)/shard_map/ppermute | solution.py:326
  49.5 3.0 %work.3 = (bf16[16,4096]{1,0:T(8,128)(2,1)S(1)}, bf16[16,4096]{1,0:T(8,128)(2,1)S(1)}, bf16[16,4096]{1,0:T(8,128)(2,1)S(1)}, bf16[16,4096]{1,0:T(8,128)(2,1)S(1)...) custom-call(bf16[32,4096]{1,0:T(8,128)(2,1)S(1)} %collective-permute, ...), custom_call_target="tpu_custom_call" | custom-call | tf_op jit(solution)/shard_map/work/pallas_call | solution.py:249
  52.6 0.5 collective-permute-start.17
  53.1 1.6 %collective-permute-start.21 = (bf16[16,4096]{1,0:T(8,128)(2,1)S(1)}, bf16[16,4096]{1,0:T(8,128)(2,1)S(1)}, u32[]{:S(2)}, u32[]{:S(2)}) collective-permute-start(bf16[16,4096]{1,0:T(8,128)(2,1)S(1)} %get-tuple-element.66), channel_id=1, source_target_pairs={{0,1},{2,0},{4,2},{6,4},{7,6},{5,7},{3,5},{1,3},{8,9},{10,8},{12,1... | collective-permute-start | bytes 393224 | tf_op jit(solution)/shard_map/ppermute | solution.py:329
  54.7 0.5 collective-permute-start.24
  55.1 1.6 %collective-permute-start.28 = (bf16[16,4096]{1,0:T(8,128)(2,1)S(1)}, bf16[16,4096]{1,0:T(8,128)(2,1)S(1)}, u32[]{:S(2)}, u32[]{:S(2)}) collective-permute-start(bf16[16,4096]{1,0:T(8,128)(2,1)S(1)} %get-tuple-element.74), channel_id=1, source_target_pairs={{0,1},{2,0},{4,2},{6,4},{7,6},{5,7},{3,5},{1,3},{8,9},{10,8},{12,1... | collective-permute-start | bytes 393224 | tf_op jit(solution)/shard_map/ppermute | solution.py:329
  56.7 2.0 %collective-permute-done.17 = bf16[16,4096]{1,0:T(8,128)(2,1)S(1)} collective-permute-done((bf16[16,4096]{1,0:T(8,128)(2,1)S(1)}, bf16[16,4096]{1,0:T(8,128)(2,1)S(1)}, u32[]{:S(2)}, u32[]{:S(2)}) %collective-permute-start.17) | collective-permute-done | bytes 131104 | tf_op jit(solution)/shard_map/ppermute | solution.py:326
  58.8 0.5 collective-permute-start.18
  59.3 1.6 %collective-permute-start.22 = (bf16[16,4096]{1,0:T(8,128)(2,1)S(1)}, bf16[16,4096]{1,0:T(8,128)(2,1)S(1)}, u32[]{:S(2)}, u32[]{:S(2)}) collective-permute-start(bf16[16,4096]{1,0:T(8,128)(2,1)S(1)} %add_convert_fusion.7), channel_id=1, source_target_pairs={{0,1},{2,0},{4,2},{6,4},{7,6},{5,7},{3,5},{1,3},{8,9},{10,8},{12,1... | collective-permute-start | bytes 393224 | tf_op jit(solution)/shard_map/ppermute | solution.py:329
  60.9 0.6 collective-permute-done.24
  61.6 0.5 collective-permute-start.25
  62.1 1.6 %collective-permute-start.29 = (bf16[16,4096]{1,0:T(8,128)(2,1)S(1)}, bf16[16,4096]{1,0:T(8,128)(2,1)S(1)}, u32[]{:S(2)}, u32[]{:S(2)}) collective-permute-start(bf16[16,4096]{1,0:T(8,128)(2,1)S(1)} %add_convert_fusion.2), channel_id=1, source_target_pairs={{0,1},{2,0},{4,2},{6,4},{7,6},{5,7},{3,5},{1,3},{8,9},{10,8},{12,1... | collective-permute-start | bytes 393224 | tf_op jit(solution)/shard_map/ppermute | solution.py:329
  63.8 1.3 %collective-permute-done.18 = bf16[16,4096]{1,0:T(8,128)(2,1)S(1)} collective-permute-done((bf16[16,4096]{1,0:T(8,128)(2,1)S(1)}, bf16[16,4096]{1,0:T(8,128)(2,1)S(1)}, u32[]{:S(2)}, u32[]{:S(2)}) %collective-permute-start.18) | collective-permute-done | bytes 131104 | tf_op jit(solution)/shard_map/ppermute | solution.py:326
  65.1 0.6 collective-permute-start.19
  65.8 1.5 %collective-permute-start.23 = (bf16[16,4096]{1,0:T(8,128)(2,1)S(1)}, bf16[16,4096]{1,0:T(8,128)(2,1)S(1)}, u32[]{:S(2)}, u32[]{:S(2)}) collective-permute-start(bf16[16,4096]{1,0:T(8,128)(2,1)S(1)} %add_convert_fusion.6), channel_id=1, source_target_pairs={{0,1},{2,0},{4,2},{6,4},{7,6},{5,7},{3,5},{1,3},{8,9},{10,8},{12,1... | collective-permute-start | bytes 393224 | tf_op jit(solution)/shard_map/ppermute | solution.py:329
  67.3 0.6 collective-permute-done.25
  68.0 0.5 collective-permute-start.26
  68.5 1.6 %collective-permute-start.30 = (bf16[16,4096]{1,0:T(8,128)(2,1)S(1)}, bf16[16,4096]{1,0:T(8,128)(2,1)S(1)}, u32[]{:S(2)}, u32[]{:S(2)}) collective-permute-start(bf16[16,4096]{1,0:T(8,128)(2,1)S(1)} %add_convert_fusion.1), channel_id=1, source_target_pairs={{0,1},{2,0},{4,2},{6,4},{7,6},{5,7},{3,5},{1,3},{8,9},{10,8},{12,1... | collective-permute-start | bytes 393224 | tf_op jit(solution)/shard_map/ppermute | solution.py:329
  70.2 0.3 collective-permute-done.19
  70.5 0.5 collective-permute-start.20
  71.1 2.5 %collective-permute-done.30 = bf16[16,4096]{1,0:T(8,128)(2,1)S(1)} collective-permute-done((bf16[16,4096]{1,0:T(8,128)(2,1)S(1)}, bf16[16,4096]{1,0:T(8,128)(2,1)S(1)}, u32[]{:S(2)}, u32[]{:S(2)}) %collective-permute-start.30) | collective-permute-done | bytes 131104 | tf_op jit(solution)/shard_map/ppermute | solution.py:329
  73.7 1.7 %collective-permute-start.27 = (bf16[16,4096]{1,0:T(8,128)(2,1)S(1)}, bf16[16,4096]{1,0:T(8,128)(2,1)S(1)}, u32[]{:S(2)}, u32[]{:S(2)}) collective-permute-start(bf16[16,4096]{1,0:T(8,128)(2,1)S(1)} %add_convert_fusion.3), channel_id=1, source_target_pairs={{0,8},{8,0},{1,9},{9,1},{2,10},{10,2},{3,11},{11,3},{4,12},{12,4},... | collective-permute-start | bytes 393224 | tf_op jit(solution)/shard_map/ppermute | solution.py:379
  75.4 2.8 %weight_grads.1 = (bf16[192,4096]{1,0:T(8,128)(2,1)}, bf16[192,4096]{1,0:T(8,128)(2,1)}, bf16[192,4096]{1,0:T(8,128)(2,1)}) custom-call(bf16[128,192]{1,0:T(8,128)(2,1)S(1)} %get-tuple-element.75.refs_0_, bf16[128,192]{1,0:T(8,128)(2,1)S(1)} %get-tuple-element.76.refs_1_, bf16[128,192]{1,0:T(8,128)(2,1)S(1)} %get-tuple-element.77.refs_2_, ...), custom_call_target="tpu_custom_call" | custom-call | flops 3000000000 | tf_op jit(solution)/shard_map/weight_grads/pallas_call | solution.py:278
  78.3 1.3 %place.1 = bf16[128,4096]{1,0:T(8,128)(2,1)} custom-call(bf16[32,128]{1,0:T(8,128)(2,1)S(1)} %get-tuple-element.46.select_ref, bf16[16,4096]{1,0:T(8,128)(2,1)S(1)} %get-tuple-element.52.own_ref, bf16[16,4096]{1,0:T(8,128)(2,1)S(1)} %collective-permute-done.20.ahead_ref, bf16[16,4096]{1,0:T(8,128)(2,1)S(1)} %collective-permute-done.23.behind_ref, ...), custom_call_target="tpu_custom_call" | custom-call | tf_op jit(solution)/shard_map/place/pallas_call | solution.py:309
  (39 shorter events, 1.3 us)
Async XLA Ops:
  2.6 3.2 %collective-permute-start = (bf16[32,4096]{1,0:T(8,128)(2,1)S(1)}, bf16[32,4096]{1,0:T(8,128)(2,1)S(1)}, u32[]{:S(2)}, u32[]{:S(2)}) collective-permute-start(bf16[32,4096]{1,0:T(8,128)(2,1)S(1)} %get-tuple-element.48), channel_id=1, source_target_pairs={{0,8},{8,0},{1,9},{9,1},{2,10},{10,2},{3,11},{11,3},{4,12},{12,4},... | collective-permute-start | bytes 786440 | tf_op jit(solution)/shard_map/ppermute | solution.py:337
  3.1 9.8 %collective-permute-start.2 = (bf16[32,4096]{1,0:T(8,128)(2,1)S(1)}, bf16[32,4096]{1,0:T(8,128)(2,1)S(1)}, u32[]{:S(2)}, u32[]{:S(2)}) collective-permute-start(bf16[32,4096]{1,0:T(8,128)(2,1)S(1)} %get-tuple-element.47.refs_0_), channel_id=1, source_target_pairs={{0,1},{2,0},{4,2},{6,4},{7,6},{5,7},{3,5},{1,3},{8,9},{10,8},{12,1... | collective-permute-start | bytes 786440 | tf_op jit(solution)/shard_map/ppermute | solution.py:329
  5.6 9.1 %collective-permute-start.1 = (bf16[32,4096]{1,0:T(8,128)(2,1)S(1)}, bf16[32,4096]{1,0:T(8,128)(2,1)S(1)}, u32[]{:S(2)}, u32[]{:S(2)}) collective-permute-start(bf16[32,4096]{1,0:T(8,128)(2,1)S(1)} %get-tuple-element.47.refs_0_), channel_id=1, source_target_pairs={{0,2},{2,4},{4,6},{6,7},{7,5},{5,3},{3,1},{1,0},{8,10},{10,12},{12... | collective-permute-start | bytes 786440 | tf_op jit(solution)/shard_map/ppermute | solution.py:326
  5.8 12.7 %collective-permute-start.4 = (bf16[32,4096]{1,0:T(8,128)(2,1)S(1)}, bf16[32,4096]{1,0:T(8,128)(2,1)S(1)}, u32[]{:S(2)}, u32[]{:S(2)}) collective-permute-start(bf16[32,4096]{1,0:T(8,128)(2,1)S(1)} %collective-permute-done.refs_1_), channel_id=1, source_target_pairs={{0,1},{2,0},{4,2},{6,4},{7,6},{5,7},{3,5},{1,3},{8,9},{10,8},{12,1... | collective-permute-start | bytes 786440 | tf_op jit(solution)/shard_map/ppermute | solution.py:329
  7.7 12.7 %collective-permute-start.3 = (bf16[32,4096]{1,0:T(8,128)(2,1)S(1)}, bf16[32,4096]{1,0:T(8,128)(2,1)S(1)}, u32[]{:S(2)}, u32[]{:S(2)}) collective-permute-start(bf16[32,4096]{1,0:T(8,128)(2,1)S(1)} %collective-permute-done.refs_1_), channel_id=1, source_target_pairs={{0,2},{2,4},{4,6},{6,7},{7,5},{5,3},{3,1},{1,0},{8,10},{10,12},{12... | collective-permute-start | bytes 786440 | tf_op jit(solution)/shard_map/ppermute | solution.py:326
  12.9 11.2 %collective-permute-start.6 = (bf16[32,4096]{1,0:T(8,128)(2,1)S(1)}, bf16[32,4096]{1,0:T(8,128)(2,1)S(1)}, u32[]{:S(2)}, u32[]{:S(2)}) collective-permute-start(bf16[32,4096]{1,0:T(8,128)(2,1)S(1)} %collective-permute-done.2.refs_3_), channel_id=1, source_target_pairs={{0,1},{2,0},{4,2},{6,4},{7,6},{5,7},{3,5},{1,3},{8,9},{10,8},{12,1... | collective-permute-start | bytes 786440 | tf_op jit(solution)/shard_map/ppermute | solution.py:329
  14.8 11.2 %collective-permute-start.5 = (bf16[32,4096]{1,0:T(8,128)(2,1)S(1)}, bf16[32,4096]{1,0:T(8,128)(2,1)S(1)}, u32[]{:S(2)}, u32[]{:S(2)}) collective-permute-start(bf16[32,4096]{1,0:T(8,128)(2,1)S(1)} %collective-permute-done.1.refs_2_), channel_id=1, source_target_pairs={{0,2},{2,4},{4,6},{6,7},{7,5},{5,3},{3,1},{1,0},{8,10},{10,12},{12... | collective-permute-start | bytes 786440 | tf_op jit(solution)/shard_map/ppermute | solution.py:326
  18.5 11.2 %collective-permute-start.8 = (bf16[32,4096]{1,0:T(8,128)(2,1)S(1)}, bf16[32,4096]{1,0:T(8,128)(2,1)S(1)}, u32[]{:S(2)}, u32[]{:S(2)}) collective-permute-start(bf16[32,4096]{1,0:T(8,128)(2,1)S(1)} %collective-permute-done.4.refs_5_), channel_id=1, source_target_pairs={{0,1},{2,0},{4,2},{6,4},{7,6},{5,7},{3,5},{1,3},{8,9},{10,8},{12,1... | collective-permute-start | bytes 786440 | tf_op jit(solution)/shard_map/ppermute | solution.py:329
  20.4 11.2 %collective-permute-start.7 = (bf16[32,4096]{1,0:T(8,128)(2,1)S(1)}, bf16[32,4096]{1,0:T(8,128)(2,1)S(1)}, u32[]{:S(2)}, u32[]{:S(2)}) collective-permute-start(bf16[32,4096]{1,0:T(8,128)(2,1)S(1)} %collective-permute-done.3.refs_4_), channel_id=1, source_target_pairs={{0,2},{2,4},{4,6},{6,7},{7,5},{5,3},{3,1},{1,0},{8,10},{10,12},{12... | collective-permute-start | bytes 786440 | tf_op jit(solution)/shard_map/ppermute | solution.py:326
  24.1 11.2 %collective-permute-start.10 = (bf16[32,4096]{1,0:T(8,128)(2,1)S(1)}, bf16[32,4096]{1,0:T(8,128)(2,1)S(1)}, u32[]{:S(2)}, u32[]{:S(2)}) collective-permute-start(bf16[32,4096]{1,0:T(8,128)(2,1)S(1)} %collective-permute-done.6.refs_7_), channel_id=1, source_target_pairs={{0,1},{2,0},{4,2},{6,4},{7,6},{5,7},{3,5},{1,3},{8,9},{10,8},{12,1... | collective-permute-start | bytes 786440 | tf_op jit(solution)/shard_map/ppermute | solution.py:329
  26.0 11.2 %collective-permute-start.9 = (bf16[32,4096]{1,0:T(8,128)(2,1)S(1)}, bf16[32,4096]{1,0:T(8,128)(2,1)S(1)}, u32[]{:S(2)}, u32[]{:S(2)}) collective-permute-start(bf16[32,4096]{1,0:T(8,128)(2,1)S(1)} %collective-permute-done.5.refs_6_), channel_id=1, source_target_pairs={{0,2},{2,4},{4,6},{6,7},{7,5},{5,3},{3,1},{1,0},{8,10},{10,12},{12... | collective-permute-start | bytes 786440 | tf_op jit(solution)/shard_map/ppermute | solution.py:326
  31.7 11.2 %collective-permute-start.11 = (bf16[32,4096]{1,0:T(8,128)(2,1)S(1)}, bf16[32,4096]{1,0:T(8,128)(2,1)S(1)}, u32[]{:S(2)}, u32[]{:S(2)}) collective-permute-start(bf16[32,4096]{1,0:T(8,128)(2,1)S(1)} %collective-permute-done.7.refs_0_), channel_id=1, source_target_pairs={{0,2},{2,4},{4,6},{6,7},{7,5},{5,3},{3,1},{1,0},{8,10},{10,12},{12... | collective-permute-start | bytes 786440 | tf_op jit(solution)/shard_map/ppermute | solution.py:326
  31.8 11.1 %collective-permute-start.12 = (bf16[32,4096]{1,0:T(8,128)(2,1)S(1)}, bf16[32,4096]{1,0:T(8,128)(2,1)S(1)}, u32[]{:S(2)}, u32[]{:S(2)}) collective-permute-start(bf16[32,4096]{1,0:T(8,128)(2,1)S(1)} %collective-permute-done.8.refs_1_), channel_id=1, source_target_pairs={{0,1},{2,0},{4,2},{6,4},{7,6},{5,7},{3,5},{1,3},{8,9},{10,8},{12,1... | collective-permute-start | bytes 786440 | tf_op jit(solution)/shard_map/ppermute | solution.py:329
  37.3 7.7 %collective-permute-start.14 = (bf16[16,4096]{1,0:T(8,128)(2,1)S(1)}, bf16[16,4096]{1,0:T(8,128)(2,1)S(1)}, u32[]{:S(2)}, u32[]{:S(2)}) collective-permute-start(bf16[16,4096]{1,0:T(8,128)(2,1)S(1)} %slice.13), channel_id=1, source_target_pairs={{0,1},{2,0},{4,2},{6,4},{7,6},{5,7},{3,5},{1,3},{8,9},{10,8},{12,1... | collective-permute-start | bytes 393224 | tf_op jit(solution)/shard_map/ppermute | solution.py:329
  38.9 6.1 %collective-permute-start.13 = (bf16[16,4096]{1,0:T(8,128)(2,1)S(1)}, bf16[16,4096]{1,0:T(8,128)(2,1)S(1)}, u32[]{:S(2)}, u32[]{:S(2)}) collective-permute-start(bf16[16,4096]{1,0:T(8,128)(2,1)S(1)} %slice.12), channel_id=1, source_target_pairs={{0,2},{2,4},{4,6},{6,7},{7,5},{5,3},{3,1},{1,0},{8,10},{10,12},{12... | collective-permute-start | bytes 393224 | tf_op jit(solution)/shard_map/ppermute | solution.py:326
  42.9 5.0 %collective-permute-start.16 = (bf16[16,4096]{1,0:T(8,128)(2,1)S(1)}, bf16[16,4096]{1,0:T(8,128)(2,1)S(1)}, u32[]{:S(2)}, u32[]{:S(2)}) collective-permute-start(bf16[16,4096]{1,0:T(8,128)(2,1)S(1)} %slice.15), channel_id=1, source_target_pairs={{0,1},{2,0},{4,2},{6,4},{7,6},{5,7},{3,5},{1,3},{8,9},{10,8},{12,1... | collective-permute-start | bytes 393224 | tf_op jit(solution)/shard_map/ppermute | solution.py:329
  44.6 5.0 %collective-permute-start.15 = (bf16[16,4096]{1,0:T(8,128)(2,1)S(1)}, bf16[16,4096]{1,0:T(8,128)(2,1)S(1)}, u32[]{:S(2)}, u32[]{:S(2)}) collective-permute-start(bf16[16,4096]{1,0:T(8,128)(2,1)S(1)} %slice.14), channel_id=1, source_target_pairs={{0,2},{2,4},{4,6},{6,7},{7,5},{5,3},{3,1},{1,0},{8,10},{10,12},{12... | collective-permute-start | bytes 393224 | tf_op jit(solution)/shard_map/ppermute | solution.py:326
  52.6 6.2 %collective-permute-start.17 = (bf16[16,4096]{1,0:T(8,128)(2,1)S(1)}, bf16[16,4096]{1,0:T(8,128)(2,1)S(1)}, u32[]{:S(2)}, u32[]{:S(2)}) collective-permute-start(bf16[16,4096]{1,0:T(8,128)(2,1)S(1)} %get-tuple-element.63), channel_id=1, source_target_pairs={{0,2},{2,4},{4,6},{6,7},{7,5},{5,3},{3,1},{1,0},{8,10},{10,12},{12... | collective-permute-start | bytes 393224 | tf_op jit(solution)/shard_map/ppermute | solution.py:326
  53.1 6.2 %collective-permute-start.21 = (bf16[16,4096]{1,0:T(8,128)(2,1)S(1)}, bf16[16,4096]{1,0:T(8,128)(2,1)S(1)}, u32[]{:S(2)}, u32[]{:S(2)}) collective-permute-start(bf16[16,4096]{1,0:T(8,128)(2,1)S(1)} %get-tuple-element.66), channel_id=1, source_target_pairs={{0,1},{2,0},{4,2},{6,4},{7,6},{5,7},{3,5},{1,3},{8,9},{10,8},{12,1... | collective-permute-start | bytes 393224 | tf_op jit(solution)/shard_map/ppermute | solution.py:329
  54.7 6.9 %collective-permute-start.24 = (bf16[16,4096]{1,0:T(8,128)(2,1)S(1)}, bf16[16,4096]{1,0:T(8,128)(2,1)S(1)}, u32[]{:S(2)}, u32[]{:S(2)}) collective-permute-start(bf16[16,4096]{1,0:T(8,128)(2,1)S(1)} %get-tuple-element.70), channel_id=1, source_target_pairs={{0,2},{2,4},{4,6},{6,7},{7,5},{5,3},{3,1},{1,0},{8,10},{10,12},{12... | collective-permute-start | bytes 393224 | tf_op jit(solution)/shard_map/ppermute | solution.py:326
  55.1 7.0 %collective-permute-start.28 = (bf16[16,4096]{1,0:T(8,128)(2,1)S(1)}, bf16[16,4096]{1,0:T(8,128)(2,1)S(1)}, u32[]{:S(2)}, u32[]{:S(2)}) collective-permute-start(bf16[16,4096]{1,0:T(8,128)(2,1)S(1)} %get-tuple-element.74), channel_id=1, source_target_pairs={{0,1},{2,0},{4,2},{6,4},{7,6},{5,7},{3,5},{1,3},{8,9},{10,8},{12,1... | collective-permute-start | bytes 393224 | tf_op jit(solution)/shard_map/ppermute | solution.py:329
  58.8 6.3 %collective-permute-start.18 = (bf16[16,4096]{1,0:T(8,128)(2,1)S(1)}, bf16[16,4096]{1,0:T(8,128)(2,1)S(1)}, u32[]{:S(2)}, u32[]{:S(2)}) collective-permute-start(bf16[16,4096]{1,0:T(8,128)(2,1)S(1)} %add_convert_fusion.10), channel_id=1, source_target_pairs={{0,2},{2,4},{4,6},{6,7},{7,5},{5,3},{3,1},{1,0},{8,10},{10,12},{12... | collective-permute-start | bytes 393224 | tf_op jit(solution)/shard_map/ppermute | solution.py:326
  59.3 6.4 %collective-permute-start.22 = (bf16[16,4096]{1,0:T(8,128)(2,1)S(1)}, bf16[16,4096]{1,0:T(8,128)(2,1)S(1)}, u32[]{:S(2)}, u32[]{:S(2)}) collective-permute-start(bf16[16,4096]{1,0:T(8,128)(2,1)S(1)} %add_convert_fusion.7), channel_id=1, source_target_pairs={{0,1},{2,0},{4,2},{6,4},{7,6},{5,7},{3,5},{1,3},{8,9},{10,8},{12,1... | collective-permute-start | bytes 393224 | tf_op jit(solution)/shard_map/ppermute | solution.py:329
  61.6 6.4 %collective-permute-start.25 = (bf16[16,4096]{1,0:T(8,128)(2,1)S(1)}, bf16[16,4096]{1,0:T(8,128)(2,1)S(1)}, u32[]{:S(2)}, u32[]{:S(2)}) collective-permute-start(bf16[16,4096]{1,0:T(8,128)(2,1)S(1)} %add_convert_fusion.5), channel_id=1, source_target_pairs={{0,2},{2,4},{4,6},{6,7},{7,5},{5,3},{3,1},{1,0},{8,10},{10,12},{12... | collective-permute-start | bytes 393224 | tf_op jit(solution)/shard_map/ppermute | solution.py:326
  62.1 6.4 %collective-permute-start.29 = (bf16[16,4096]{1,0:T(8,128)(2,1)S(1)}, bf16[16,4096]{1,0:T(8,128)(2,1)S(1)}, u32[]{:S(2)}, u32[]{:S(2)}) collective-permute-start(bf16[16,4096]{1,0:T(8,128)(2,1)S(1)} %add_convert_fusion.2), channel_id=1, source_target_pairs={{0,1},{2,0},{4,2},{6,4},{7,6},{5,7},{3,5},{1,3},{8,9},{10,8},{12,1... | collective-permute-start | bytes 393224 | tf_op jit(solution)/shard_map/ppermute | solution.py:329
  65.1 5.4 %collective-permute-start.19 = (bf16[16,4096]{1,0:T(8,128)(2,1)S(1)}, bf16[16,4096]{1,0:T(8,128)(2,1)S(1)}, u32[]{:S(2)}, u32[]{:S(2)}) collective-permute-start(bf16[16,4096]{1,0:T(8,128)(2,1)S(1)} %add_convert_fusion.9), channel_id=1, source_target_pairs={{0,2},{2,4},{4,6},{6,7},{7,5},{5,3},{3,1},{1,0},{8,10},{10,12},{12... | collective-permute-start | bytes 393224 | tf_op jit(solution)/shard_map/ppermute | solution.py:326
  65.8 12.5 %collective-permute-start.23 = (bf16[16,4096]{1,0:T(8,128)(2,1)S(1)}, bf16[16,4096]{1,0:T(8,128)(2,1)S(1)}, u32[]{:S(2)}, u32[]{:S(2)}) collective-permute-start(bf16[16,4096]{1,0:T(8,128)(2,1)S(1)} %add_convert_fusion.6), channel_id=1, source_target_pairs={{0,1},{2,0},{4,2},{6,4},{7,6},{5,7},{3,5},{1,3},{8,9},{10,8},{12,1... | collective-permute-start | bytes 393224 | tf_op jit(solution)/shard_map/ppermute | solution.py:329
  68.0 5.7 %collective-permute-start.26 = (bf16[16,4096]{1,0:T(8,128)(2,1)S(1)}, bf16[16,4096]{1,0:T(8,128)(2,1)S(1)}, u32[]{:S(2)}, u32[]{:S(2)}) collective-permute-start(bf16[16,4096]{1,0:T(8,128)(2,1)S(1)} %add_convert_fusion.4), channel_id=1, source_target_pairs={{0,2},{2,4},{4,6},{6,7},{7,5},{5,3},{3,1},{1,0},{8,10},{10,12},{12... | collective-permute-start | bytes 393224 | tf_op jit(solution)/shard_map/ppermute | solution.py:326
  68.5 5.0 %collective-permute-start.30 = (bf16[16,4096]{1,0:T(8,128)(2,1)S(1)}, bf16[16,4096]{1,0:T(8,128)(2,1)S(1)}, u32[]{:S(2)}, u32[]{:S(2)}) collective-permute-start(bf16[16,4096]{1,0:T(8,128)(2,1)S(1)} %add_convert_fusion.1), channel_id=1, source_target_pairs={{0,1},{2,0},{4,2},{6,4},{7,6},{5,7},{3,5},{1,3},{8,9},{10,8},{12,1... | collective-permute-start | bytes 393224 | tf_op jit(solution)/shard_map/ppermute | solution.py:329
  70.5 7.8 %collective-permute-start.20 = (bf16[16,4096]{1,0:T(8,128)(2,1)S(1)}, bf16[16,4096]{1,0:T(8,128)(2,1)S(1)}, u32[]{:S(2)}, u32[]{:S(2)}) collective-permute-start(bf16[16,4096]{1,0:T(8,128)(2,1)S(1)} %add_convert_fusion.8), channel_id=1, source_target_pairs={{0,2},{2,4},{4,6},{6,7},{7,5},{5,3},{3,1},{1,0},{8,10},{10,12},{12... | collective-permute-start | bytes 393224 | tf_op jit(solution)/shard_map/ppermute | solution.py:326
  73.6 4.7 %collective-permute-start.31 = (bf16[16,4096]{1,0:T(8,128)(2,1)S(1)}, bf16[16,4096]{1,0:T(8,128)(2,1)S(1)}, u32[]{:S(2)}, u32[]{:S(2)}) collective-permute-start(bf16[16,4096]{1,0:T(8,128)(2,1)S(1)} %add_convert_fusion), channel_id=1, source_target_pairs={{0,9},{2,8},{4,10},{6,12},{7,14},{5,15},{3,13},{1,11},{8,1},{10,0}... | collective-permute-start | bytes 393224 | tf_op jit(solution)/shard_map/ppermute | solution.py:334
  73.7 4.6 %collective-permute-start.27 = (bf16[16,4096]{1,0:T(8,128)(2,1)S(1)}, bf16[16,4096]{1,0:T(8,128)(2,1)S(1)}, u32[]{:S(2)}, u32[]{:S(2)}) collective-permute-start(bf16[16,4096]{1,0:T(8,128)(2,1)S(1)} %add_convert_fusion.3), channel_id=1, source_target_pairs={{0,8},{8,0},{1,9},{9,1},{2,10},{10,2},{3,11},{11,3},{4,12},{12,4},... | collective-permute-start | bytes 393224 | tf_op jit(solution)/shard_map/ppermute | solution.py:379
